TPU v7x, 128 devices: a whole 4x4x4 slice. The times are simulated.
128 devices in a mesh: frag: 64 (over z, y, x), inner: 2 (over core).
Axes of the slice: x: 4, y: 4, z: 4, core: 2. Of those that a mesh axis runs over, the one named last changes fastest.
Arguments:
- density: bfloat16 [4096, 256, 256], P('frag', 'inner'), may hold values from -6 to 6
- core_hamiltonian: bfloat16 [4096, 256, 256], P('frag', 'inner'), may hold values from -6 to 6
- coulomb_kernel: bfloat16 [4096, 256, 256], P('frag', 'inner'), may hold values from -0.375 to 0.375
- esp_kernel: bfloat16 [4096, 256, 256], P('frag', 'inner'), may hold values from -0.375 to 0.375
- contacts: int32 [4096, 16], replicated, may hold values from -1 to 4095, as said below
- coupling: float32 [4096, 16], P('frag'), may hold values from 0.1 to 1
- partner: int32 [4096], P('frag'), may hold values from 0 to 4095, as said below
Outputs:
- fock: bfloat16 [4096, 256, 256], P(('frag', 'inner'))
- new_density: bfloat16 [4096, 256, 256], P(('frag', 'inner'))
- partner_energy: float32 [4096], P('frag')
Inputs may be any that keep to these rules, and one draw needn't show every extreme that they name: `contacts`: -1 marks an empty slot. No fragment names itself. Taking groups of 64 fragments in order, a named fragment lies in a group at most 2 groups away from the naming one. At most 4 contact slots of one group name fragments of any one other group (several slots may name the same fragment), and every group has exactly 4 slots naming fragments of some one other group. Taking groups of 64 fragments in order, the partner of a fragment in group 2m lies in group 2m + 1 and the reverse; the partner of a fragment's partner is the fragment itself.
All inputs are finite; a program needn't handle non-finite values.
Results may differ from a plain program's by a relative error of at most 0.009.
The roundings to bfloat16 on the way count: a program that leaves them out, or rounds other values in their place, can miss the bound.
Values may be sent and summed in bfloat16 or wider, within the bound.
No kernel may reach another device: no remote copies, remote signals or barrier semaphores. Data moves between devices by JAX's collectives and lax.ppermute only.
A program may use at most 192 MiB of HBM per device.

v0:
```python
import jax
import jax.numpy as jnp
from jax import lax
from jax.sharding import PartitionSpec as P

NN = 16
CAPG = 4
RG = 2
NPUR = 6


def partner_2(block, axis, stride):
    count = lax.axis_size(axis)
    route = []
    for low in range(count):
        high = low | 1 << stride
        if high != low and high < count:
            route += [(low, high), (high, low)]
    return lax.ppermute(block, axis, route)


def passed_along(array, axis, by):
    length = lax.axis_size(axis)
    pairs = [(i, i + by) for i in range(length) if 0 <= i + by < length]
    return lax.ppermute(array, axis, pairs)


def offset_list(max_reach):
    return [direction * distance for distance in range(1, max_reach + 1) for direction in (1, -1)]


def purified(fock_whole, basis_size):
    wide = fock_whole.astype(jnp.float32)
    symmetric = 0.5 * (wide + jnp.swapaxes(wide, 1, 2))
    identity = jnp.eye(basis_size, dtype=jnp.float32)
    centre = jnp.trace(symmetric, axis1=1, axis2=2) / basis_size
    centred = symmetric - centre[:, None, None] * identity
    spread = jnp.sqrt(jnp.sum(centred * centred, axis=(1, 2)) + 1e-06)
    estimate = (0.5 * identity - centred / (2.0 * spread[:, None, None])).astype(jnp.bfloat16)
    for iteration in range(NPUR):
        square = jnp.einsum(
            "fab,fbc->fac", estimate, estimate, preferred_element_type=jnp.float32
        ).astype(jnp.bfloat16)
        cube_term = jnp.einsum("fab,fbc->fac", square, estimate, preferred_element_type=jnp.float32)
        estimate = (3.0 * square.astype(jnp.float32) - 2.0 * cube_term).astype(jnp.bfloat16)
    return estimate


def body(density, core_hamiltonian, coulomb_kernel, esp_kernel, contacts, coupling, partner):
    group_size, row_count, basis_size = density.shape
    groups = lax.axis_size("frag")
    own_group = lax.axis_index("frag")
    pair_count = group_size * NN
    flat_size = row_count * basis_size
    swapped = partner_2(density, "frag", 0)
    gathered = lax.all_gather(density, "inner", axis=1, tiled=True)
    image_sum = jnp.einsum("frc,fcn->frn", esp_kernel, gathered, preferred_element_type=jnp.float32)
    coulomb = jnp.einsum(
        "frc,fcn->frn", coulomb_kernel, gathered, preferred_element_type=jnp.float32
    )
    esp_image = image_sum.astype(jnp.bfloat16)
    partner_local = partner % group_size
    partner_rows = swapped[partner_local]
    partial_value = (
        jnp.sum(partner_rows.astype(jnp.float32) * esp_image.astype(jnp.float32), axis=(1, 2))
        / basis_size
    )
    partner_energy = lax.psum(partial_value, "inner")
    own_lists = lax.dynamic_slice_in_dim(contacts, own_group * group_size, group_size, 0).reshape(
        -1
    )
    own_weights = coupling.reshape(-1)
    own_target = jnp.where(own_lists >= 0, own_lists // group_size, -1)
    group_ids = jnp.arange(groups)
    slot_ids = jnp.arange(CAPG)
    leaving = (own_target[:, None] == group_ids[None, :]) & (own_target[:, None] != own_group)
    leave_rank = jnp.cumsum(leaving.astype(jnp.int32), axis=0) - 1
    chosen = leaving[:, :, None] & (leave_rank[:, :, None] == slot_ids[None, None, :])
    source_frag = (jnp.arange(pair_count) // NN)[:, None, None]
    source_slot = jnp.sum(jnp.where(chosen, source_frag, 0), axis=0)
    weight_slot = jnp.sum(jnp.where(chosen, own_weights[:, None, None], 0.0), axis=0)
    outgoing = (esp_image[source_slot].astype(jnp.float32) * weight_slot[:, :, None, None]).astype(
        jnp.bfloat16
    )
    all_lists = contacts.reshape(groups, pair_count)
    all_target = jnp.where(all_lists >= 0, all_lists // group_size, -1)
    arriving = (all_target == own_group) & (group_ids[:, None] != own_group)
    arrive_rank = jnp.cumsum(arriving.astype(jnp.int32), axis=1) - 1
    slot_hit = arriving[:, :, None] & (arrive_rank[:, :, None] == slot_ids[None, None, :])
    dest_hit = (all_lists % group_size)[:, :, None] == jnp.arange(group_size)[None, None, :]
    arrival_table = jnp.einsum(
        "gpc,gpi->igc",
        slot_hit.astype(jnp.bfloat16),
        dest_hit.astype(jnp.bfloat16),
        preferred_element_type=jnp.float32,
    ).astype(jnp.bfloat16)
    local_hit = own_lists[None, :] == own_group * group_size + jnp.arange(group_size)[:, None]
    local_weights = jnp.sum(
        jnp.where(local_hit, own_weights[None, :], 0.0).reshape(group_size, group_size, NN), axis=2
    )
    potential = jnp.einsum(
        "ij,jrn->irn", local_weights, esp_image.astype(jnp.float32), precision=lax.Precision.HIGHEST
    )
    for shift_by in offset_list(RG):
        target_index = jnp.clip(own_group + shift_by, 0, groups - 1)
        sending = lax.dynamic_index_in_dim(outgoing, target_index, 0, keepdims=False)
        arrived = passed_along(sending, "frag", shift_by)
        source_index = jnp.clip(own_group - shift_by, 0, groups - 1)
        table_part = lax.dynamic_index_in_dim(arrival_table, source_index, 1, keepdims=False)
        remote_sum = jnp.dot(
            table_part, arrived.reshape(CAPG, flat_size), preferred_element_type=jnp.float32
        )
        potential = potential + remote_sum.reshape(group_size, row_count, basis_size)
    fock_rows = (core_hamiltonian.astype(jnp.float32) + coulomb + potential).astype(jnp.bfloat16)
    fock_whole = lax.all_to_all(fock_rows, "inner", split_axis=0, concat_axis=1, tiled=True)
    new_density = purified(fock_whole, basis_size)
    return (fock_whole, new_density, partner_energy)


def solution(mesh):
    placed = (
        P("frag", "inner", None),
        P("frag", "inner", None),
        P("frag", "inner", None),
        P("frag", "inner", None),
        P(),
        P("frag", None),
        P("frag"),
    )
    return jax.shard_map(
        body,
        mesh=mesh,
        in_specs=placed,
        out_specs=(P(("frag", "inner"), None, None), P(("frag", "inner"), None, None), P("frag")),
        check_vma=False,
    )
```

profile of v0, /device:TPU:97, one launch (start us, length us, event | category | flops | bytes accessed | tf_op | source)
XLA Modules:
  0.0 286.5 jit_solution(10010834449098432740)
XLA Ops:
  10.1 1.6 reshape.343
  12.5 18.2 %reduce-window.16 = s32[64,8,128]{2,1,0:T(8,128)S(1)} reduce-window(s32[64,8,128]{2,1,0:T(8,128)S(1)} %fusion.29, s32[]{:T(128)} %constant.128.clone.1), window={size=1x1x128 pad=0_0x0_0x127_0}, to_apply=%region_3.4 | reduce-window | flops 8323072 | bytes 524292 | tf_op jit(solution)/shard_map/reduce-window.2
  32.5 18.0 %reduce-window.14 = s32[64,8,128]{2,1,0:T(8,128)S(1)} reduce-window(s32[64,8,128]{2,1,0:T(8,128)S(1)} %and_convert_fusion, s32[]{:T(128)} %constant.128.clone.1), window={size=1x1x128 pad=0_0x0_0x127_0}, to_apply=%region_1.2 | reduce-window | flops 8323072 | bytes 524292 | tf_op jit(solution)/shard_map/reduce-window
  51.8 3.0 %fusion.14 = bf16[64,64,4]{1,2,0:T(4,128)(2,1)S(1)} fusion(s32[64,1024]{1,0:T(8,128)S(1)} %add_select_fusion.2, s32[64,1024]{1,0:T(8,128)S(1)} %bitcast.137, pred[64,1024]{1,0:T(8,128)(4,1)S(1)} %fusion.30), kind=kOutput, calls=%fused_computation.35 | convolution fusion | flops 38289408 | bytes 622592 | tf_op jit(solution)/shard_map/gpc,gpi->igc/dot_general | solution.py:91
  54.8 44.9 %collective-permute-done.4 = bf16[64,128,256]{2,1,0:T(8,128)(2,1)} collective-permute-done((bf16[64,128,256]{2,1,0:T(8,128)(2,1)}, bf16[64,128,256]{2,1,0:T(8,128)(2,1)}, u32[]{:S(2)}, u32[]{:S(2)}) %collective-permute-start.4) | collective-permute-done | bytes 4194336 | tf_op jit(solution)/shard_map/ppermute | solution.py:19
  99.8 5.0 %gather_fusion.1 = bf16[64,128,256]{2,1,0:T(8,128)(2,1)} fusion(bf16[64,128,256]{2,1,0:T(8,128)(2,1)} %collective-permute-done.4, s32[1024]{0:T(1024)S(1)} %pad_clamp_fusion), kind=kCustom, calls=%fused_computation.1 | custom fusion | bytes 8388864 | tf_op jit(solution)/shard_map/gather | solution.py:63
  104.8 5.9 %convolution_convert_fusion = bf16[64,128,256]{2,1,0:T(8,128)(2,1)S(1)} fusion(bf16[64,128,256]{2,1,0:T(8,128)(2,1)} %param.10, bf16[64,256,256]{2,1,0:T(8,128)(2,1)} %all-gather.2.cloned.1.call-done), kind=kOutput, calls=%fused_computation.34 | convolution fusion | flops 1075838976 | bytes 16777216 | tf_op jit(solution)/shard_map/frc,fcn->frn/dot_general | solution.py:57
  110.7 2.0 copy-done
  112.7 7.5 %fusion.6 = f32[64,128,256]{2,0,1:T(8,128)} fusion(bf16[64,128,256]{2,1,0:T(8,128)(2,1)S(1)} %convolution_convert_fusion, f32[64,64]{1,0:T(8,128)S(1)} %select_reduce_fusion.3), kind=kOutput, calls=%fused_computation.26 | convolution fusion | flops 1610612736 | bytes 12599296 | tf_op jit(solution)/shard_map/ij,jrn->irn/dot_general | solution.py:101
  120.2 11.2 %gather_fusion = bf16[256,128,256]{2,1,0:T(8,128)(2,1)} fusion(bf16[64,128,256]{2,1,0:T(8,128)(2,1)} %copy-done, s32[1024]{0:T(1024)S(1)} %pad_clamp_fusion.1), kind=kCustom, calls=%fused_computation | custom fusion | bytes 33555456 | tf_op jit(solution)/shard_map/gather | solution.py:82
  131.5 13.4 %fusion = bf16[64,4,128,256]{3,2,1,0:T(8,128)(2,1)S(1)} fusion(bf16[64,4,128,256]{3,2,1,0:T(8,128)(2,1)} %bitcast.127, f32[64,4]{1,0:T(8,128)S(1)} %copy.53), kind=kLoop, calls=%fused_computation.3 | loop fusion | flops 25165824 | bytes 33555456 | tf_op jit(solution)/shard_map/convert_element_type | solution.py:82
  144.9 6.7 %collective-permute-start.1 = (bf16[4,128,256]{2,1,0:T(8,128)(2,1)S(1)}, bf16[4,128,256]{2,1,0:T(8,128)(2,1)S(1)}, u32[]{:S(2)}, u32[]{:S(2)}) collective-permute-start(bf16[4,128,256]{2,1,0:T(8,128)(2,1)S(1)} %get-tuple-element.10), channel_id=1, source_target_pairs={{2,0},{4,2},{6,4},{8,6},{10,8},{12,10},{14,12},{16,14},{18,16},{20... | collective-permute-start | bytes 786440 | tf_op jit(solution)/shard_map/ppermute | solution.py:25
  151.6 1.6 multiply_reduce_fusion
  153.2 1.9 collective-permute-start
  155.1 3.6 %collective-permute-start.3 = (bf16[4,128,256]{2,1,0:T(8,128)(2,1)S(1)}, bf16[4,128,256]{2,1,0:T(8,128)(2,1)S(1)}, u32[]{:S(2)}, u32[]{:S(2)}) collective-permute-start(bf16[4,128,256]{2,1,0:T(8,128)(2,1)S(1)} %get-tuple-element.8), channel_id=1, source_target_pairs={{4,0},{6,2},{8,4},{10,6},{12,8},{14,10},{16,12},{18,14},{20,16},{2... | collective-permute-start | bytes 786440 | tf_op jit(solution)/shard_map/ppermute | solution.py:25
  158.8 3.2 %collective-permute-start.2 = (bf16[4,128,256]{2,1,0:T(8,128)(2,1)S(1)}, bf16[4,128,256]{2,1,0:T(8,128)(2,1)S(1)}, u32[]{:S(2)}, u32[]{:S(2)}) collective-permute-start(bf16[4,128,256]{2,1,0:T(8,128)(2,1)S(1)} %get-tuple-element.9), channel_id=1, source_target_pairs={{0,4},{2,6},{4,8},{6,10},{8,12},{10,14},{12,16},{14,18},{16,20},{1... | collective-permute-start | bytes 786440 | tf_op jit(solution)/shard_map/ppermute | solution.py:25
  162.0 5.0 %psum.7 = f32[64]{0:T(128)} all-reduce(f32[64]{0:T(128)S(1)} %broadcast_multiply_fusion), channel_id=1, replica_groups=mesh['frag'=64,'inner'=2] {'inner'}, use_global_device_ids=true, to_apply=%region_10.11 | all-reduce | flops 64 | bytes 512 | tf_op jit(solution)/shard_map/psum | solution.py:68
  167.0 4.5 %fusion.48 = f32[64,128,256]{2,0,1:T(8,128)} fusion(bf16[64,64,4]{1,2,0:T(4,128)(2,1)S(1)} %fusion.14, s32[]{:T(128)S(6)} %min.18, bf16[1,4,128,256]{3,2,1,0:T(8,128)(2,1)S(1)} %bitcast.135), kind=kOutput, calls=%fused_computation.123 | convolution fusion | flops 16777216 | bytes 8651780 | tf_op jit(solution)/shard_map/dot_general | solution.py:110
  171.5 2.1 collective-permute-done.2
  173.6 4.5 %fusion.51 = f32[64,128,256]{2,0,1:T(8,128)} fusion(bf16[64,64,4]{1,2,0:T(4,128)(2,1)S(1)} %fusion.14, s32[]{:T(128)S(6)} %min.19, bf16[1,4,128,256]{3,2,1,0:T(8,128)(2,1)S(1)} %bitcast.136), kind=kOutput, calls=%fused_computation.125 | convolution fusion | flops 16777216 | bytes 8651780 | tf_op jit(solution)/shard_map/dot_general | solution.py:110
  178.1 4.5 %fusion.54 = f32[64,128,256]{2,0,1:T(8,128)} fusion(bf16[64,64,4]{1,2,0:T(4,128)(2,1)S(1)} %fusion.14, s32[]{:T(128)S(6)} %min.20, bf16[1,4,128,256]{3,2,1,0:T(8,128)(2,1)S(1)} %bitcast.134), kind=kOutput, calls=%fused_computation.127 | convolution fusion | flops 16777216 | bytes 8651780 | tf_op jit(solution)/shard_map/dot_general | solution.py:110
  182.6 4.5 %fusion.45 = f32[64,128,256]{2,0,1:T(8,128)} fusion(bf16[64,64,4]{1,2,0:T(4,128)(2,1)S(1)} %fusion.14, s32[]{:T(128)S(6)} %min.17, bf16[1,4,128,256]{3,2,1,0:T(8,128)(2,1)S(1)} %bitcast.133), kind=kOutput, calls=%fused_computation.121 | convolution fusion | flops 16777216 | bytes 8651780 | tf_op jit(solution)/shard_map/dot_general | solution.py:110
  187.1 42.2 %fusion.4 = bf16[64,128,256]{2,1,0:T(8,128)(2,1)S(1)} fusion(f32[64,128,256]{2,0,1:T(8,128)} %fusion.54, f32[64,128,256]{2,0,1:T(8,128)} %fusion.51, f32[64,128,256]{2,0,1:T(8,128)} %fusion.48, f32[64,128,256]{2,0,1:T(8,128)} %fusion.45, f32[64,128,256]{2,0,1:T(8,128)} %fusion.6, bf16[64,128,256]{2,1,0:T(8,128)(2,1)} %param.8, ...), kind=kOutput, calls=%fused_computation.10 | convolution fusion | flops 1090519040 | bytes 62914560 | tf_op jit(solution)/shard_map/frc,fcn->frn/dot_general | solution.py:58
  229.4 8.7 %all_to_all.18 = bf16[64,128,256]{2,1,0:T(8,128)(2,1)S(1)} all-to-all(bf16[64,128,256]{2,1,0:T(8,128)(2,1)S(1)} %fusion.4), channel_id=1, replica_groups=mesh['frag'=64,'inner'=2] {'inner'}, dimensions={0} | all-to-all | bytes 8388608 | tf_op jit(solution)/shard_map/all_to_all | solution.py:115
  238.1 2.3 copy.59
  240.4 7.1 %copy.60 = f32[32,256,256]{1,2,0:T(8,128)} copy(bf16[32,256,256]{2,1,0:T(8,128)(2,1)} %bitcast.125) | data formatting | bytes 12582912 | tf_op jit(solution)/shard_map/convert_element_type | solution.py:33
  247.4 6.5 %select_reduce_fusion = f32[32]{0:T(128)S(1)} fusion(pred[256,256]{1,0:T(8,128)(4,1)S(1)} %iota_compare_fusion.6, f32[32,256,256]{1,2,0:T(8,128)} %copy.60, bf16[32,2,128,256]{3,2,1,0:T(8,128)(2,1)} %copy.59), kind=kLoop, calls=%fused_computation.24 | loop fusion | flops 10485728 | bytes 12648576 | tf_op jit(solution)/shard_map/jit(trace)/reduce_sum | solution.py:36
  255.6 2.7 multiply_reduce_fusion.1
  258.3 2.9 %subtract_convert_fusion.6 = bf16[32,256,256]{2,1,0:T(8,128)(2,1)S(1)} fusion(f32[32]{0:T(128)S(1)} %sqrt_multiply_fusion, f32[256,256]{1,0:T(8,128)S(1)} %fusion.32, f32[32]{0:T(128)S(1)} %broadcast_multiply_fusion.1, f32[256,256]{1,0:T(8,128)S(1)} %fusion.33, f32[32,256,256]{1,2,0:T(8,128)S(1)} %copy-done.2, bf16[32,2,128,256]{3,2,1,0:T(8,128)(2,1)S(1)} %copy-done.3), kind=kLoop, calls=%fused_computation.21 | loop fusion | flops 16777216 | bytes 17301760 | tf_op jit(solution)/shard_map/convert_element_type | solution.py:39
  262.5 1.4 subtract_convert_fusion.5
  273.1 1.6 subtract_convert_fusion.1
  276.0 3.4 %subtract_convert_fusion = bf16[32,256,256]{2,1,0:T(8,128)(2,1)} fusion(bf16[32,256,256]{2,1,0:T(8,128)(2,1)S(1)} %subtract_convert_fusion.1, bf16[32,256,256]{2,1,0:T(8,128)(2,1)S(1)} %fusion.72), kind=kOutput, calls=%fused_computation.15 | convolution fusion | flops 1084227584 | bytes 12582912 | tf_op jit(solution)/shard_map/fab,fbc->fac/dot_general | solution.py:44
  (85 shorter events, 20.0 us)
Async XLA Ops:
  7.2 2.0 copy-start.5
  7.2 97.6 %all-gather.2.cloned.1.call-start = ((), (), s32[]{:S(2)}) async-start(), calls=%async_computation.1 | async-start | bytes 12582912 | tf_op jit(solution)/shard_map/all_gather | solution.py:56
  7.9 4.4 %copy-start.6 = (f32[64,16]{0,1:T(8,128)S(1)}, f32[64,16]{0,1:T(8,128)}, u32[]{:S(2)}) copy-start(f32[64,16]{0,1:T(8,128)} %param.12) | copy-start | bytes 12292
  7.9 91.8 %collective-permute-start.4 = (bf16[64,128,256]{2,1,0:T(8,128)(2,1)}, bf16[64,128,256]{2,1,0:T(8,128)(2,1)}, u32[]{:S(2)}, u32[]{:S(2)}) collective-permute-start(bf16[64,128,256]{2,1,0:T(8,128)(2,1)} %param.7), channel_id=1, source_target_pairs={{0,2},{2,0},{4,6},{6,4},{8,10},{10,8},{12,14},{14,12},{16,18},{18,... | collective-permute-start | bytes 12582920 | tf_op jit(solution)/shard_map/ppermute | solution.py:19
  11.7 39.5 %copy-start.7 = (s32[64]{0:T(128)S(1)}, s32[64]{0:T(128)}, u32[]{:S(2)}) copy-start(s32[64]{0:T(128)} %param.13) | copy-start | bytes 772
  110.7 2.0 copy-start
  131.4 20.2 %copy-start.1 = (bf16[64,128,256]{2,1,0:T(8,128)(2,1)S(1)}, bf16[64,128,256]{2,1,0:T(8,128)(2,1)}, u32[]{:S(2)}) copy-start(bf16[64,128,256]{2,1,0:T(8,128)(2,1)} %copy-done) | copy-start | bytes 12582916
  131.4 20.2 %copy-start.4 = (bf16[64,128,256]{2,1,0:T(8,128)(2,1)S(1)}, bf16[64,128,256]{2,1,0:T(8,128)(2,1)}, u32[]{:S(2)}) copy-start(bf16[64,128,256]{2,1,0:T(8,128)(2,1)} %gather_fusion.1) | copy-start | bytes 12582916
  144.9 22.1 %collective-permute-start.1 = (bf16[4,128,256]{2,1,0:T(8,128)(2,1)S(1)}, bf16[4,128,256]{2,1,0:T(8,128)(2,1)S(1)}, u32[]{:S(2)}, u32[]{:S(2)}) collective-permute-start(bf16[4,128,256]{2,1,0:T(8,128)(2,1)S(1)} %get-tuple-element.10), channel_id=1, source_target_pairs={{2,0},{4,2},{6,4},{8,6},{10,8},{12,10},{14,12},{16,14},{18,16},{20... | collective-permute-start | bytes 786440 | tf_op jit(solution)/shard_map/ppermute | solution.py:25
  153.2 29.4 %collective-permute-start = (bf16[4,128,256]{2,1,0:T(8,128)(2,1)S(1)}, bf16[4,128,256]{2,1,0:T(8,128)(2,1)S(1)}, u32[]{:S(2)}, u32[]{:S(2)}) collective-permute-start(bf16[4,128,256]{2,1,0:T(8,128)(2,1)S(1)} %get-tuple-element.7), channel_id=1, source_target_pairs={{0,2},{2,4},{4,6},{6,8},{8,10},{10,12},{12,14},{14,16},{16,18},{18... | collective-permute-start | bytes 786440 | tf_op jit(solution)/shard_map/ppermute | solution.py:25
  155.1 22.9 %collective-permute-start.3 = (bf16[4,128,256]{2,1,0:T(8,128)(2,1)S(1)}, bf16[4,128,256]{2,1,0:T(8,128)(2,1)S(1)}, u32[]{:S(2)}, u32[]{:S(2)}) collective-permute-start(bf16[4,128,256]{2,1,0:T(8,128)(2,1)S(1)} %get-tuple-element.8), channel_id=1, source_target_pairs={{4,0},{6,2},{8,4},{10,6},{12,8},{14,10},{16,12},{18,14},{20,16},{2... | collective-permute-start | bytes 786440 | tf_op jit(solution)/shard_map/ppermute | solution.py:25
  158.8 14.8 %collective-permute-start.2 = (bf16[4,128,256]{2,1,0:T(8,128)(2,1)S(1)}, bf16[4,128,256]{2,1,0:T(8,128)(2,1)S(1)}, u32[]{:S(2)}, u32[]{:S(2)}) collective-permute-start(bf16[4,128,256]{2,1,0:T(8,128)(2,1)S(1)} %get-tuple-element.9), channel_id=1, source_target_pairs={{0,4},{2,6},{4,8},{6,10},{8,12},{10,14},{12,16},{14,18},{16,20},{1... | collective-permute-start | bytes 786440 | tf_op jit(solution)/shard_map/ppermute | solution.py:25
  178.1 9.0 %slice-start = ((s8[8388608]{0:T(1024)(128)(4,1)}), s8[4194304]{0:T(1024)(128)(4,1)S(1)}, s32[]{:S(2)}) async-start(s8[8388608]{0:T(1024)(128)(4,1)} %bitcast.123), calls=%async_computation.2 | async-start | bytes 8388608
  182.6 4.5 %slice-start.1 = ((s8[8388608]{0:T(1024)(128)(4,1)}), s8[4194304]{0:T(1024)(128)(4,1)S(1)}, s32[]{:S(2)}) async-start(s8[8388608]{0:T(1024)(128)(4,1)} %bitcast.123), calls=%async_computation.3 | async-start | bytes 8388608
  247.4 7.0 %copy-start.2 = (f32[32,256,256]{1,2,0:T(8,128)S(1)}, f32[32,256,256]{1,2,0:T(8,128)}, u32[]{:S(2)}) copy-start(f32[32,256,256]{1,2,0:T(8,128)} %copy.60) | copy-start | bytes 25165828
  247.4 8.2 %copy-start.3 = (bf16[32,2,128,256]{3,2,1,0:T(8,128)(2,1)S(1)}, bf16[32,2,128,256]{3,2,1,0:T(8,128)(2,1)}, u32[]{:S(2)}) copy-start(bf16[32,2,128,256]{3,2,1,0:T(8,128)(2,1)} %copy.59) | copy-start | bytes 12582916
Sparse Core Ops, SparseCore 0:
  9.7 24.4 all-gather.1
where the time goes:
time: 292 us; the launch traced here: 286 us
  matrix products  94.8 us (32%)
  other arithmetic  65.2 us (22%)
  waiting for transfers between devices  47.7 us (16%)
  local copies, waits for them, and re-layouts  33.6 us (12%)
  starting transfers between devices  16.7 us (6%)
  between operations  14.7 us (5%)
  blocking collectives  13.8 us (5%)
    ppermute x1, waiting for transfers between devices, partner_2(): return lax.ppermute(block, axis, route)  44.9 us
    dot_general x1, matrix products, body(): jnp.einsum('frc,fcn->frn', coulomb_kernel, gathered, preferred_element_ty...  42.2 us
    another operation x4, other arithmetic  36.3 us
    dot_general x4, matrix products, body(): jnp.dot(table_part, arrived.reshape(CAPG, flat_size), preferred_element_t...  18 us
    ppermute x4, starting transfers between devices, passed_along(): return lax.ppermute(array, axis, pairs)  15.4 us
    convert_element_type x1, other arithmetic, body(): (esp_image[source_slot].astype(jnp.float32) * weight_slot[:, :, None, Non...  13.4 us
    gather x1, local copies, waits for them, and re-layouts, body(): esp_image[source_slot].astype(jnp.float32) * weight_slot[:, :, None, None]  11.2 us
    dot_general x6, matrix products, purified(): jnp.einsum('fab,fbc->fac', square, estimate, preferred_element_type=jnp.f...  10.6 us
  transfers between devices with their start and end apart: 6, of which 2 were waited for; matrix products, arithmetic and copies ran while one was open for 23% of the time, Pallas kernels for 0%

commit v1 on v0

v1 whole, which is shorter than its diff:
```python
import functools

import jax
import jax.numpy as jnp
from jax import lax
from jax.experimental import pallas as pl
from jax.experimental.pallas import tpu as pltpu
from jax.sharding import PartitionSpec as P

NN = 16
CAPG = 4
NPUR = 6
OFFSETS = (1, -1, 2, -2)
SLOTS = len(OFFSETS) * CAPG
LOCAL_STEP = 4
ROW_STEP = 16
PURE_STEP = 4
ENERGY_STEP = 4
NONE = float(1 << 20)
SMEM = pl.BlockSpec(memory_space=pltpu.SMEM)
F32 = jnp.float32
BF16 = jnp.bfloat16


def dot(left, right):
    return jnp.dot(left, right, preferred_element_type=F32)


def params(mib=48):
    return pltpu.CompilerParams(vmem_limit_bytes=mib << 20)


def index_kernel(own_ref, low_ref, mid_ref, high_ref, coupling_ref, weight_ref, partner_ref, meta_ref, sent_ref, local_ref):
    own = own_ref[0]
    lists = jnp.concatenate([low_ref[...], mid_ref[...], high_ref[...]], axis=1)
    slot = lax.broadcasted_iota(jnp.int32, lists.shape, 0)
    lane = lax.broadcasted_iota(jnp.int32, lists.shape, 1)
    source = (own // 2 - 1) * 2 + (lane >> 6)
    target = lists >> 6
    key = (((slot * 64 + (lane & 63)) << 6) + (lists & 63)).astype(F32)
    leaving, arriving = [], []
    for offset in OFFSETS:
        leaving.append(jnp.where((source == own) & (target == own + offset), key, NONE))
        giver = own - offset
        giver = jnp.where((giver >= 0) & (giver < 64), giver, -999)
        arriving.append(jnp.where((source == giver) & (target == own), key, NONE))
    for rank in range(CAPG):
        for place in range(len(OFFSETS)):
            at = place * CAPG + rank
            least = jnp.min(leaving[place])
            leaving[place] = jnp.where(leaving[place] > least, leaving[place], NONE)
            code = jnp.where(least < NONE, least, 0.0).astype(jnp.int32)
            fragment = (code >> 6) & 63
            meta_ref[at] = fragment
            sent_ref[at] = weight_ref[code >> 12, fragment]
            least = jnp.min(arriving[place])
            arriving[place] = jnp.where(arriving[place] > least, arriving[place], NONE)
            code = jnp.where(least < NONE, least, -1.0).astype(jnp.int32)
            meta_ref[SLOTS + at] = jnp.where(code >= 0, code & 63, -1)

    def invert(step, carry):
        meta_ref[2 * SLOTS + (partner_ref[step] & 63)] = step
        return carry

    lax.fori_loop(0, 64, invert, 0)
    middle = mid_ref[...]
    half = lax.broadcasted_iota(jnp.int32, middle.shape, 1) >> 6
    middle = jnp.where(half == own % 2, middle - own * 64, -1)
    coupling = jnp.concatenate([coupling_ref[...], coupling_ref[...]], axis=1)
    row = lax.broadcasted_iota(jnp.int32, (64, 128), 0)
    wide = jnp.zeros((64, 128), F32)
    for k in range(NN):
        wide = wide + jnp.where(middle[k : k + 1] == row, coupling[k : k + 1], 0.0)
    weights = wide[:, :64] + wide[:, 64:]
    first = weights.astype(BF16)
    rest = weights - first.astype(F32)
    second = rest.astype(BF16)
    local_ref[:, 0:64] = first
    local_ref[:, 64:128] = second
    local_ref[:, 128:192] = (rest - second.astype(F32)).astype(BF16)


def make_index(own, contacts, coupling, partner):
    def block(shift):
        return pl.BlockSpec((NN, 128), lambda i, s: (0, jnp.clip(s[0] // 2 + shift, 0, 31)))

    return pl.pallas_call(
        index_kernel,
        grid_spec=pltpu.PrefetchScalarGridSpec(
            num_scalar_prefetch=1,
            grid=(1,),
            in_specs=[block(-1), block(0), block(1), pl.BlockSpec((NN, 64), lambda i, s: (0, 0)), SMEM, SMEM],
            out_specs=[SMEM, SMEM, pl.BlockSpec((64, 192), lambda i, s: (0, 0))],
        ),
        out_shape=[
            jax.ShapeDtypeStruct((2 * SLOTS + 64,), jnp.int32),
            jax.ShapeDtypeStruct((SLOTS,), F32),
            jax.ShapeDtypeStruct((64, 192), BF16),
        ],
        name="slots",
    )(own, contacts, contacts, contacts, coupling, coupling, partner)


def assemble(whole, inner, own, other):
    whole[pl.ds(pl.multiple_of(inner * 128, 128), 128), :] = own
    whole[pl.ds(pl.multiple_of(128 - inner * 128, 128), 128), :] = other


def outgoing_kernel(meta_ref, inner_ref, sent_ref, *refs):
    count = len(OFFSETS)
    kernels, own, other, outs, whole = (
        refs[:count], refs[count : 2 * count], refs[2 * count : 3 * count], refs[3 * count : 4 * count], refs[-1]
    )
    step = pl.program_id(0)
    for place in range(count):
        assemble(whole.at[place], inner_ref[0], own[place][0], other[place][0])
        image = dot(kernels[place][0], whole[place]).astype(BF16)
        weight = sent_ref[place * CAPG + step]
        outs[place][0] = (image.astype(F32) * weight).astype(BF16)


def make_outgoing(meta, inner, sent, esp_kernel, density, other):
    count = len(OFFSETS)

    def block(place):
        return pl.BlockSpec((1, 128, 256), lambda c, m, i: (m[place * CAPG + c], 0, 0))

    blocks = [block(place) for place in range(count)]
    return pl.pallas_call(
        outgoing_kernel,
        grid_spec=pltpu.PrefetchScalarGridSpec(
            num_scalar_prefetch=2,
            grid=(CAPG,),
            in_specs=[SMEM] + blocks * 3,
            out_specs=[pl.BlockSpec((1, 128, 256), lambda c, m, i: (c, 0, 0))] * count,
            scratch_shapes=[pltpu.VMEM((count, 256, 256), BF16)],
        ),
        out_shape=[jax.ShapeDtypeStruct((CAPG, 128, 256), BF16)] * count,
        compiler_params=params(),
        cost_estimate=pl.CostEstimate(flops=16 * 2 * 128 * 256 * 256, bytes_accessed=4 << 20, transcendentals=0),
        name="outgoing",
    )(meta, inner, sent, *[esp_kernel] * count, *[density] * count, *[other] * count)


def local_kernel(inner_ref, own, other, esp, response, core, weights, image_out, sum_out, wide, sums, whole):
    step = pl.program_id(0)
    loads = 64 // LOCAL_STEP

    @pl.when(step < loads)
    def _():
        for f in range(LOCAL_STEP):
            assemble(whole.at[f], inner_ref[0], own[f], other[f])
            both = jnp.concatenate([esp[f], response[f]], axis=0)
            result = dot(both, whole[f])
            image = result[:128].astype(BF16)
            image_out[f] = image
            rows = pl.ds(pl.multiple_of((step * LOCAL_STEP + f) * 128, 128), 128)
            image = image.astype(F32)
            total = result[128:] + core[f].astype(F32)
            for side in range(2):
                wide[side, rows, :] = image[:, side * 128 : side * 128 + 128]
                sums[side, rows, :] = total[:, side * 128 : side * 128 + 128]

    @pl.when(step >= loads)
    def _():
        matrix = weights[...]
        base = (step - loads) * ROW_STEP
        out = sum_out
        for r in range(ROW_STEP):
            at = pl.ds(base + r, 64, stride=128)
            tile = jnp.concatenate([wide[0, at, :], wide[1, at, :]], axis=1).astype(BF16)
            mixed = dot(matrix, jnp.concatenate([tile, tile, tile], axis=0))
            for side in range(2):
                out[side, pl.ds(r, 64, stride=ROW_STEP), :] = (
                    mixed[:, side * 128 : side * 128 + 128] + sums[side, at, :]
                )


def make_local(inner, density, other, esp_kernel, coulomb_kernel, core_hamiltonian, weights):
    loads, rows = 64 // LOCAL_STEP, 128 // ROW_STEP
    block = pl.BlockSpec((LOCAL_STEP, 128, 256), lambda t, i: (jnp.minimum(t, loads - 1), 0, 0))
    return pl.pallas_call(
        local_kernel,
        grid_spec=pltpu.PrefetchScalarGridSpec(
            num_scalar_prefetch=1,
            grid=(loads + rows,),
            in_specs=[block] * 5 + [pl.BlockSpec((64, 192), lambda t, i: (0, 0))],
            out_specs=[block, pl.BlockSpec((2, 64 * ROW_STEP, 128), lambda t, i: (0, jnp.maximum(t - loads, 0), 0))],
            scratch_shapes=[
                pltpu.VMEM((2, 64 * 128, 128), F32),
                pltpu.VMEM((2, 64 * 128, 128), F32),
                pltpu.VMEM((LOCAL_STEP, 256, 256), BF16),
            ],
        ),
        out_shape=[
            jax.ShapeDtypeStruct((64, 128, 256), BF16),
            jax.ShapeDtypeStruct((2, rows * 64 * ROW_STEP, 128), F32),
        ],
        compiler_params=params(),
        cost_estimate=pl.CostEstimate(flops=64 * 2 * 256 * 256 * 256, bytes_accessed=32 << 20, transcendentals=0),
        name="local",
    )(inner, density, other, esp_kernel, coulomb_kernel, core_hamiltonian, weights)


def fock_kernel(meta_ref, first_ref, sums, *refs):
    arrived, out, total = refs[:-2], refs[-2], refs[-1]
    step = pl.program_id(0)
    count = out.shape[0]
    for side in range(2):
        total[:, :, side * 128 : side * 128 + 128] = jnp.concatenate(
            [sums[side, tile].reshape(count, ROW_STEP, 128) for tile in range(128 // ROW_STEP)], axis=1
        )
    start = first_ref[0] + step * count
    for slot in range(SLOTS):
        place = meta_ref[SLOTS + slot] - start

        @pl.when((place >= 0) & (place < count))
        def _(slot=slot, place=place):
            total[place] += arrived[slot // CAPG][slot % CAPG].astype(F32)

    out[...] = total[...].astype(BF16)


def make_fock(meta, first, sums, arrived, number, count=8):
    tiles = 128 // ROW_STEP
    blocked = sums.reshape(2, tiles, 64 * ROW_STEP, 128)
    whole = pl.BlockSpec((CAPG, 128, 256), lambda t, m, f: (0, 0, 0))
    return pl.pallas_call(
        fock_kernel,
        grid_spec=pltpu.PrefetchScalarGridSpec(
            num_scalar_prefetch=2,
            grid=(number // count,),
            in_specs=[pl.BlockSpec((2, tiles, count * ROW_STEP, 128), lambda t, m, f: (0, 0, f[0] // count + t, 0))]
            + [whole] * len(OFFSETS),
            out_specs=pl.BlockSpec((count, 128, 256), lambda t, m, f: (t, 0, 0)),
            scratch_shapes=[pltpu.VMEM((count, 128, 256), F32)],
        ),
        out_shape=jax.ShapeDtypeStruct((number, 128, 256), BF16),
        compiler_params=params(),
        cost_estimate=pl.CostEstimate(flops=1 << 22, bytes_accessed=number * 3 << 16, transcendentals=0),
        name="fock_rows",
    )(meta, first, blocked, *arrived)


def pure_kernel(inner_ref, own, other, fock_out, density_out):
    row = lax.broadcasted_iota(jnp.int32, (256, 256), 0)
    column = lax.broadcasted_iota(jnp.int32, (256, 256), 1)
    diagonal = row == column
    identity = diagonal.astype(F32)
    turn = identity.astype(BF16)
    estimates = []
    for f in range(PURE_STEP):
        assemble(fock_out.at[f], inner_ref[0], own[f], other[f])
    for f in range(PURE_STEP):
        rows = fock_out[f]
        turned = lax.dot_general(turn, rows, (((1,), (1,)), ((), ())), preferred_element_type=F32)
        symmetric = 0.5 * (rows.astype(F32) + turned)
        centre = jnp.sum(jnp.where(diagonal, symmetric, 0.0), axis=(0, 1), keepdims=True) * (1.0 / 256)
        centred = symmetric - centre * identity
        spread = jnp.sqrt(jnp.sum(centred * centred, axis=(0, 1), keepdims=True) + 1e-6)
        estimates.append((0.5 * identity - centred * (0.5 / spread)).astype(BF16))
    for iteration in range(NPUR):
        squares = [dot(e, e).astype(BF16) for e in estimates]
        cubes = [dot(s, e) for s, e in zip(squares, estimates)]
        estimates = [(3.0 * s.astype(F32) - 2.0 * c).astype(BF16) for s, c in zip(squares, cubes)]
    for f in range(PURE_STEP):
        density_out[f] = estimates[f]


def make_pure(inner, own, other):
    number = own.shape[0]
    rows = pl.BlockSpec((PURE_STEP, 128, 256), lambda t, i: (t, 0, 0))
    whole = pl.BlockSpec((PURE_STEP, 256, 256), lambda t, i: (t, 0, 0))
    return pl.pallas_call(
        pure_kernel,
        grid_spec=pltpu.PrefetchScalarGridSpec(
            num_scalar_prefetch=1,
            grid=(number // PURE_STEP,),
            in_specs=[rows, rows],
            out_specs=[whole, whole],
        ),
        out_shape=[jax.ShapeDtypeStruct((number, 256, 256), BF16)] * 2,
        compiler_params=params(),
        cost_estimate=pl.CostEstimate(flops=number * 13 * 2 * 256**3, bytes_accessed=number * 3 << 17, transcendentals=0),
        name="purify",
    )(inner, own, other)


def energy_kernel(meta_ref, first, swapped, *refs):
    images, out = refs[:-1], refs[-1]
    step = pl.program_id(0)

    @pl.when(step == 0)
    def _():
        out[...] = jnp.zeros_like(out)

    for f in range(ENERGY_STEP):
        product = swapped[f].astype(F32) * images[f][0].astype(F32)
        line = jnp.sum(product, axis=0, keepdims=True)
        place = meta_ref[2 * SLOTS + first + step * ENERGY_STEP + f]
        out[pl.ds(place, 1), :] = line[:, :128] + line[:, 128:]


def make_energy(meta, first, swapped, image):
    number = swapped.shape[0]

    def block(f):
        return pl.BlockSpec((1, 128, 256), lambda t, m: (m[2 * SLOTS + first + t * ENERGY_STEP + f], 0, 0))

    return pl.pallas_call(
        lambda meta_ref, *refs: energy_kernel(meta_ref, first, *refs),
        grid_spec=pltpu.PrefetchScalarGridSpec(
            num_scalar_prefetch=1,
            grid=(number // ENERGY_STEP,),
            in_specs=[pl.BlockSpec((ENERGY_STEP, 128, 256), lambda t, m: (t, 0, 0))]
            + [block(f) for f in range(ENERGY_STEP)],
            out_specs=pl.BlockSpec((64, 128), lambda t, m: (0, 0)),
        ),
        out_shape=jax.ShapeDtypeStruct((64, 128), F32),
        cost_estimate=pl.CostEstimate(flops=number << 16, bytes_accessed=number << 17, transcendentals=0),
        name="energy",
    )(meta, swapped, *[image] * ENERGY_STEP)


def along(array, axis, by):
    length = lax.axis_size(axis)
    return lax.ppermute(array, axis, [(i, i + by) for i in range(length) if 0 <= i + by < length])


def exchanged(array, axis):
    return lax.ppermute(array, axis, [(i, i ^ 1) for i in range(lax.axis_size(axis))])


CUTS = (0, 48, 64)


def body(density, core_hamiltonian, coulomb_kernel, esp_kernel, contacts, coupling, partner):
    own = lax.axis_index("frag").astype(jnp.int32).reshape(1)
    inner = lax.axis_index("inner").astype(jnp.int32).reshape(1)
    other = exchanged(density, "inner")
    swapped = [exchanged(density[a:b], "frag") for a, b in zip(CUTS, CUTS[1:])]
    meta, sent, weights = make_index(own, contacts.T, coupling.T, partner)
    outgoing = make_outgoing(meta, inner, sent, esp_kernel, density, other)
    arrived = [along(block, "frag", by) for block, by in zip(outgoing, OFFSETS)]
    image, sums = make_local(inner, density, other, esp_kernel, coulomb_kernel, core_hamiltonian, weights)
    leave = make_fock(meta, 32 - inner * 32, sums, arrived, 32)
    stay = make_fock(meta, inner * 32, sums, arrived, 32)
    came = exchanged(leave, "inner")
    fock, new_density = make_pure(inner, stay, came)
    lines = sum(make_energy(meta, a, part, image) for a, part in zip(CUTS, swapped))
    energy = lax.psum(jnp.sum(lines, axis=1) * (1.0 / 256), "inner")
    return (fock, new_density, energy)


def solution(mesh):
    rows = P("frag", "inner", None)
    whole = P(("frag", "inner"), None, None)
    return jax.shard_map(
        body,
        mesh=mesh,
        in_specs=(rows, rows, rows, rows, P(), P("frag", None), P("frag")),
        out_specs=(whole, whole, P("frag")),
        check_vma=False,
    )
```

time: 292 us -> 176 us (0.60); the launches traced: 286 us -> 174 us
  matrix products: 94.8 us -> 0 us
  Pallas kernels: 0 us -> 82.6 us
  other arithmetic: 65.2 us -> 0.87 us
  local copies, waits for them, and re-layouts: 33.6 us -> 10.6 us
  between operations: 14.7 us -> 0.77 us
  blocking collectives: 13.8 us -> 3.43 us
  waiting for transfers between devices: 47.7 us -> 53.5 us
  starting transfers between devices: 16.7 us -> 22.2 us
    dot_general x20 -> x0, matrix products: 94.8 us -> none  [the longest x1 42.2 us: body(): jnp.einsum('frc,fcn->frn', coulomb_kernel, gathered, preferred_element_ty...]
    pallas_call x0 -> x8, Pallas kernels: none -> 82.6 us  [the longest x1 28.2 us: make_pure(): pl.pallas_call(pure_kernel, grid_spec=pltpu.PrefetchScalarGridSpec(num_sc...]
    another operation x4 -> x0, other arithmetic: 36.3 us -> none
    convert_element_type x5 -> x0, other arithmetic: 16.5 us -> none  [the longest x1 13.4 us: body(): (esp_image[source_slot].astype(jnp.float32) * weight_slot[:, :, None, Non...]
    gather x2 -> x0, local copies, waits for them, and re-layouts: 16.2 us -> none  [the longest x1 11.2 us: body(): esp_image[source_slot].astype(jnp.float32) * weight_slot[:, :, None, None]]
    reduce_sum x6 -> x1, other arithmetic: 11.6 us -> 0.86 us  [body(): energy = lax.psum(jnp.sum(lines, axis=1) * (1.0 / 256), 'inner')]
    all_to_all x1 -> x0, blocking collectives: 8.74 us -> none  [body(): lax.all_to_all(fock_rows, 'inner', split_axis=0, concat_axis=1, tiled=True)]
    convert_element_type x1 -> x0, local copies, waits for them, and re-layouts: 7.05 us -> none  [purified(): wide = fock_whole.astype(jnp.float32)]
  transfers between devices with their start and end apart: 6 -> 8, of which waited for: 2 -> 5; matrix products, arithmetic and copies ran while one was open for 23% -> 3% of each run, Pallas kernels for 0% -> 31%
where the time goes in v1:
time: 176 us; the launch traced here: 174 us
  Pallas kernels  82.6 us (47%)
  waiting for transfers between devices  53.5 us (30%)
  starting transfers between devices  22.2 us (13%)
  local copies, waits for them, and re-layouts  10.6 us (6%)
  blocking collectives  3.43 us (2%)
    ppermute x4, waiting for transfers between devices, along(): lax.ppermute(array, axis, [(i, i + by) for i in range(length) if 0 <= i +...  28.6 us
    pallas_call x1, Pallas kernels, make_pure(): pl.pallas_call(pure_kernel, grid_spec=pltpu.PrefetchScalarGridSpec(num_sc...  28.2 us
    pallas_call x1, Pallas kernels, make_local(): pl.pallas_call(local_kernel, grid_spec=pltpu.PrefetchScalarGridSpec(num_s...  27.5 us
    ppermute x4, waiting for transfers between devices, exchanged(): lax.ppermute(array, axis, [(i, i ^ 1) for i in range(lax.axis_size(axis))])  24.9 us
    ppermute x4, starting transfers between devices, along(): lax.ppermute(array, axis, [(i, i + by) for i in range(length) if 0 <= i +...  19.3 us
    pallas_call x2, Pallas kernels, make_energy(): pl.pallas_call(lambda meta_ref, *refs: energy_kernel(meta_ref, first, *re...  11.9 us
    pallas_call x2, Pallas kernels, make_fock(): pl.pallas_call(fock_kernel, grid_spec=pltpu.PrefetchScalarGridSpec(num_sc...  8.1 us
    unnamed x14, local copies, waits for them, and re-layouts  5.42 us
  transfers between devices with their start and end apart: 8, of which 5 were waited for; matrix products, arithmetic and copies ran while one was open for 3% of the time, Pallas kernels for 31%

profile of v1, /device:TPU:97, one launch (start us, length us, event | category | flops | bytes accessed | tf_op | source)
XLA Modules:
  0.0 174.0 jit_solution(7237699065043039632)
XLA Ops:
  0.6 0.8 collective-permute-start
  1.4 3.9 %slice.6 = bf16[48,128,256]{2,1,0:T(8,128)(2,1)} slice(bf16[64,128,256]{2,1,0:T(8,128)(2,1)} %refs_7_.1), slice={[0:48], [0:128], [0:256]} | slice | bytes 6291456 | tf_op jit(solution)/shard_map/slice | solution.py:341
  5.3 1.2 collective-permute-start.6
  6.5 3.0 %slots.1 = (s32[96]{0:T(128)}, f32[16]{0:T(128)}, bf16[64,192]{1,0:T(8,128)(2,1)}) custom-call(s32[1]{0:T(128)} %bitcast.1.own_ref, s32[16,4096]{1,0:T(8,128)} %bitcast.7, s32[16,4096]{1,0:T(8,128)} %bitcast.8, s32[16,4096]{1,0:T(8,128)} %bitcast.9, f32[16,64]{1,0:T(8,128)} %bitcast.10, f32[16,64]{1,0:T(8,128)} %bitcast.11, s32[64]{0:T(128)} %partner_ref.1), custom_call_target="tpu_custom_call" | custom-call | tf_op jit(solution)/shard_map/slots/pallas_call | solution.py:87
  9.6 0.0 collective-permute-done.other.refs_8_.refs_9_.refs_10_.refs_11_
  9.6 0.0 copy-start.1
  9.6 2.2 %copy-done.1 = bf16[64,128,256]{2,1,0:T(8,128)(2,1)S(1)} copy-done((bf16[64,128,256]{2,1,0:T(8,128)(2,1)S(1)}, bf16[64,128,256]{2,1,0:T(8,128)(2,1)}, u32[]{:S(2)}) %copy-start.1) | copy-done | bytes 4194328
  11.8 0.6 copy-done.3
  12.4 0.6 copy-done.5
  13.0 3.9 %outgoing.1 = (bf16[4,128,256]{2,1,0:T(8,128)(2,1)S(1)}, bf16[4,128,256]{2,1,0:T(8,128)(2,1)S(1)}, bf16[4,128,256]{2,1,0:T(8,128)(2,1)S(1)}, bf16[4,128,256]{2,1,0:T(8,128)(2,1)S(1)}) custom-call(s32[96]{0:T(128)S(1)} %copy-done.3, s32[1]{0:T(128)} %bitcast.inner_ref, f32[16]{0:T(128)S(1)} %copy-done.5, bf16[64,128,256]{2,1,0:T(8,128)(2,1)S(1)} %copy-done.1, ...), custom_call_target="tpu_custom_call" | custom-call | flops 268435456 | bytes 4194304 | tf_op jit(solution)/shard_map/outgoing/pallas_call | solution.py:129
  16.8 2.1 %collective-permute-start.1 = (bf16[4,128,256]{2,1,0:T(8,128)(2,1)S(1)}, bf16[4,128,256]{2,1,0:T(8,128)(2,1)S(1)}, u32[]{:S(2)}, u32[]{:S(2)}) collective-permute-start(bf16[4,128,256]{2,1,0:T(8,128)(2,1)S(1)} %get-tuple-element.18), channel_id=1, source_target_pairs={{0,2},{2,4},{4,6},{6,8},{8,10},{10,12},{12,14},{14,16},{16,18},{18... | collective-permute-start | bytes 786440 | tf_op jit(solution)/shard_map/ppermute | solution.py:327
  18.9 7.4 %collective-permute-start.2 = (bf16[4,128,256]{2,1,0:T(8,128)(2,1)S(1)}, bf16[4,128,256]{2,1,0:T(8,128)(2,1)S(1)}, u32[]{:S(2)}, u32[]{:S(2)}) collective-permute-start(bf16[4,128,256]{2,1,0:T(8,128)(2,1)S(1)} %get-tuple-element.19), channel_id=1, source_target_pairs={{2,0},{4,2},{6,4},{8,6},{10,8},{12,10},{14,12},{16,14},{18,16},{20... | collective-permute-start | bytes 786440 | tf_op jit(solution)/shard_map/ppermute | solution.py:327
  26.4 1.9 %collective-permute-start.3 = (bf16[4,128,256]{2,1,0:T(8,128)(2,1)S(1)}, bf16[4,128,256]{2,1,0:T(8,128)(2,1)S(1)}, u32[]{:S(2)}, u32[]{:S(2)}) collective-permute-start(bf16[4,128,256]{2,1,0:T(8,128)(2,1)S(1)} %get-tuple-element.20), channel_id=1, source_target_pairs={{0,4},{2,6},{4,8},{6,10},{8,12},{10,14},{12,16},{14,18},{16,20},{1... | collective-permute-start | bytes 786440 | tf_op jit(solution)/shard_map/ppermute | solution.py:327
  28.3 7.9 %collective-permute-start.4 = (bf16[4,128,256]{2,1,0:T(8,128)(2,1)S(1)}, bf16[4,128,256]{2,1,0:T(8,128)(2,1)S(1)}, u32[]{:S(2)}, u32[]{:S(2)}) collective-permute-start(bf16[4,128,256]{2,1,0:T(8,128)(2,1)S(1)} %get-tuple-element.21), channel_id=1, source_target_pairs={{4,0},{6,2},{8,4},{10,6},{12,8},{14,10},{16,12},{18,14},{20,16},{2... | collective-permute-start | bytes 786440 | tf_op jit(solution)/shard_map/ppermute | solution.py:327
  36.2 27.5 %local.1 = (bf16[64,128,256]{2,1,0:T(8,128)(2,1)S(1)}, f32[2,8192,128]{2,1,0:T(8,128)}) custom-call(s32[1]{0:T(128)} %bitcast.inner_ref, bf16[64,128,256]{2,1,0:T(8,128)(2,1)} %refs_7_.1, bf16[64,128,256]{2,1,0:T(8,128)(2,1)} %collective-permute-done.other.refs_8_.refs_9_.refs_10_.refs_11_, bf16[64,128,256]{2,1,0:T(8,128)(2,1)} %refs_3_.1, ...), custom_call_target="tpu_custom_call" | custom-call | flops 2147483648 | bytes 33554432 | tf_op jit(solution)/shard_map/local/pallas_call | solution.py:182
  63.7 2.0 %copy-done = bf16[64,128,256]{2,1,0:T(8,128)(2,1)} copy-done((bf16[64,128,256]{2,1,0:T(8,128)(2,1)}, bf16[64,128,256]{2,1,0:T(8,128)(2,1)S(1)}, u32[]{:S(2)}) %copy-start) | copy-done | bytes 4194328
  65.7 14.2 %collective-permute-done.1.refs_0_ = bf16[4,128,256]{2,1,0:T(8,128)(2,1)S(1)} collective-permute-done((bf16[4,128,256]{2,1,0:T(8,128)(2,1)S(1)}, bf16[4,128,256]{2,1,0:T(8,128)(2,1)S(1)}, u32[]{:S(2)}, u32[]{:S(2)}) %collective-permute-start.1) | collective-permute-done | bytes 262176 | tf_op jit(solution)/shard_map/ppermute | solution.py:327
  79.8 1.0 collective-permute-done.2.refs_1_
  80.8 10.1 %collective-permute-done.3.refs_2_ = bf16[4,128,256]{2,1,0:T(8,128)(2,1)S(1)} collective-permute-done((bf16[4,128,256]{2,1,0:T(8,128)(2,1)S(1)}, bf16[4,128,256]{2,1,0:T(8,128)(2,1)S(1)}, u32[]{:S(2)}, u32[]{:S(2)}) %collective-permute-start.3) | collective-permute-done | bytes 262176 | tf_op jit(solution)/shard_map/ppermute | solution.py:327
  90.9 3.3 %collective-permute-done.4.refs_3_ = bf16[4,128,256]{2,1,0:T(8,128)(2,1)S(1)} collective-permute-done((bf16[4,128,256]{2,1,0:T(8,128)(2,1)S(1)}, bf16[4,128,256]{2,1,0:T(8,128)(2,1)S(1)}, u32[]{:S(2)}, u32[]{:S(2)}) %collective-permute-start.4) | collective-permute-done | bytes 262176 | tf_op jit(solution)/shard_map/ppermute | solution.py:327
  94.3 4.1 %fock_rows.3 = bf16[32,128,256]{2,1,0:T(8,128)(2,1)S(1)} custom-call(s32[96]{0:T(128)S(1)} %copy-done.3, s32[1]{0:T(128)S(6)} %sub.3.first_ref, f32[2,8,1024,128]{3,2,1,0:T(8,128)} %bitcast.5, bf16[4,128,256]{2,1,0:T(8,128)(2,1)S(1)} %collective-permute-done.1.refs_0_, bf16[4,128,256]{2,1,0:T(8,128)(2,1)S(1)} %collective-permute-done.2.refs_1_, ...), custom_call_target="tpu_custom_call" | custom-call | flops 4194304 | bytes 6291456 | tf_op jit(solution)/shard_map/fock_rows/pallas_call | solution.py:228
  98.3 0.9 collective-permute-start.5
  99.2 1.3 slice.7
  100.5 0.1 collective-permute-start.7
  100.6 24.9 %collective-permute-done.7.refs_0_ = bf16[16,128,256]{2,1,0:T(8,128)(2,1)} collective-permute-done((bf16[16,128,256]{2,1,0:T(8,128)(2,1)S(1)}, bf16[16,128,256]{2,1,0:T(8,128)(2,1)}, u32[]{:S(2)}, u32[]{:S(2)}) %collective-permute-start.7) | collective-permute-done | bytes 1048608 | tf_op jit(solution)/shard_map/ppermute | solution.py:331
  125.5 3.6 %energy.3 = f32[64,128]{1,0:T(8,128)} custom-call(s32[96]{0:T(128)} %get-tuple-element.14.meta_ref, bf16[16,128,256]{2,1,0:T(8,128)(2,1)} %collective-permute-done.7.refs_0_, bf16[64,128,256]{2,1,0:T(8,128)(2,1)} %copy-done, bf16[64,128,256]{2,1,0:T(8,128)(2,1)} %copy-done, bf16[64,128,256]{2,1,0:T(8,128)(2,1)} %copy-done, bf16[64,128,256]{2,1,0:T(8,128)(2,1)} %copy-done), custom_call_target="tpu_custom_call" | custom-call | flops 1048576 | bytes 2097152 | tf_op jit(solution)/shard_map/energy/pallas_call | solution.py:310
  129.1 0.0 collective-permute-done.6.refs_0_
  129.1 8.3 %energy.2 = f32[64,128]{1,0:T(8,128)} custom-call(s32[96]{0:T(128)} %get-tuple-element.14.meta_ref, bf16[48,128,256]{2,1,0:T(8,128)(2,1)} %collective-permute-done.6.refs_0_, bf16[64,128,256]{2,1,0:T(8,128)(2,1)} %copy-done, bf16[64,128,256]{2,1,0:T(8,128)(2,1)} %copy-done, bf16[64,128,256]{2,1,0:T(8,128)(2,1)} %copy-done, bf16[64,128,256]{2,1,0:T(8,128)(2,1)} %copy-done), custom_call_target="tpu_custom_call" | custom-call | flops 3145728 | bytes 6291456 | tf_op jit(solution)/shard_map/energy/pallas_call | solution.py:310
  137.4 0.9 add_reduce_fusion
  138.2 3.4 %psum.7 = f32[64]{0:T(128)} all-reduce(f32[64]{0:T(128)S(1)} %broadcast_multiply_fusion), channel_id=1, replica_groups=mesh['frag'=64,'inner'=2] {'inner'}, use_global_device_ids=true, to_apply=%region_1.0 | all-reduce | flops 64 | bytes 512 | tf_op jit(solution)/shard_map/psum | solution.py:351
  141.7 4.0 %fock_rows.2.own = bf16[32,128,256]{2,1,0:T(8,128)(2,1)S(1)} custom-call(s32[96]{0:T(128)S(1)} %copy-done.4, s32[1]{0:T(128)S(6)} %mul.10.first_ref, f32[2,8,1024,128]{3,2,1,0:T(8,128)} %bitcast.6, bf16[4,128,256]{2,1,0:T(8,128)(2,1)S(1)} %collective-permute-done.1.refs_0_, bf16[4,128,256]{2,1,0:T(8,128)(2,1)S(1)} %collective-permute-done.2.refs_1_, ...), custom_call_target="tpu_custom_call" | custom-call | flops 4194304 | bytes 6291456 | tf_op jit(solution)/shard_map/fock_rows/pallas_call | solution.py:228
  145.7 28.2 %purify.1 = (bf16[32,256,256]{2,1,0:T(8,128)(2,1)}, bf16[32,256,256]{2,1,0:T(8,128)(2,1)}) custom-call(s32[1]{0:T(128)} %bitcast.inner_ref, bf16[32,128,256]{2,1,0:T(8,128)(2,1)S(1)} %fock_rows.2.own, bf16[32,128,256]{2,1,0:T(8,128)(2,1)} %collective-permute-done.5.other), custom_call_target="tpu_custom_call" | custom-call | flops 13958643712 | bytes 12582912 | tf_op jit(solution)/shard_map/purify/pallas_call | solution.py:274
  (11 shorter events, 0.0 us)
Async XLA Ops:
  0.6 8.9 %collective-permute-start = (bf16[64,128,256]{2,1,0:T(8,128)(2,1)}, bf16[64,128,256]{2,1,0:T(8,128)(2,1)}, u32[]{:S(2)}, u32[]{:S(2)}) collective-permute-start(bf16[64,128,256]{2,1,0:T(8,128)(2,1)} %refs_7_.1), channel_id=1, source_target_pairs={{0,1},{1,0},{2,3},{3,2},{4,5},{5,4},{6,7},{7,6},{8,9},{9,8},{10,11... | collective-permute-start | bytes 12582920 | tf_op jit(solution)/shard_map/ppermute | solution.py:331
  5.3 123.8 %collective-permute-start.6 = (bf16[48,128,256]{2,1,0:T(8,128)(2,1)}, bf16[48,128,256]{2,1,0:T(8,128)(2,1)}, u32[]{:S(2)}, u32[]{:S(2)}) collective-permute-start(bf16[48,128,256]{2,1,0:T(8,128)(2,1)} %slice.6), channel_id=1, source_target_pairs={{0,2},{2,0},{4,6},{6,4},{8,10},{10,8},{12,14},{14,12},{16,18},{18,... | collective-permute-start | bytes 9437192 | tf_op jit(solution)/shard_map/ppermute | solution.py:331
  9.6 2.2 %copy-start.1 = (bf16[64,128,256]{2,1,0:T(8,128)(2,1)S(1)}, bf16[64,128,256]{2,1,0:T(8,128)(2,1)}, u32[]{:S(2)}) copy-start(bf16[64,128,256]{2,1,0:T(8,128)(2,1)} %refs_3_.1) | copy-start | bytes 12582916
  11.8 0.6 copy-start.3
  12.4 0.6 copy-start.5
  13.0 23.2 %copy-start.2 = (bf16[64,192]{1,0:T(8,128)(2,1)S(1)}, bf16[64,192]{1,0:T(8,128)(2,1)}, u32[]{:S(2)}) copy-start(bf16[64,192]{1,0:T(8,128)(2,1)} %get-tuple-element.15.weights) | copy-start | bytes 73732
  16.8 63.0 %collective-permute-start.1 = (bf16[4,128,256]{2,1,0:T(8,128)(2,1)S(1)}, bf16[4,128,256]{2,1,0:T(8,128)(2,1)S(1)}, u32[]{:S(2)}, u32[]{:S(2)}) collective-permute-start(bf16[4,128,256]{2,1,0:T(8,128)(2,1)S(1)} %get-tuple-element.18), channel_id=1, source_target_pairs={{0,2},{2,4},{4,6},{6,8},{8,10},{10,12},{12,14},{14,16},{16,18},{18... | collective-permute-start | bytes 786440 | tf_op jit(solution)/shard_map/ppermute | solution.py:327
  18.9 61.9 %collective-permute-start.2 = (bf16[4,128,256]{2,1,0:T(8,128)(2,1)S(1)}, bf16[4,128,256]{2,1,0:T(8,128)(2,1)S(1)}, u32[]{:S(2)}, u32[]{:S(2)}) collective-permute-start(bf16[4,128,256]{2,1,0:T(8,128)(2,1)S(1)} %get-tuple-element.19), channel_id=1, source_target_pairs={{2,0},{4,2},{6,4},{8,6},{10,8},{12,10},{14,12},{16,14},{18,16},{20... | collective-permute-start | bytes 786440 | tf_op jit(solution)/shard_map/ppermute | solution.py:327
  26.4 64.6 %collective-permute-start.3 = (bf16[4,128,256]{2,1,0:T(8,128)(2,1)S(1)}, bf16[4,128,256]{2,1,0:T(8,128)(2,1)S(1)}, u32[]{:S(2)}, u32[]{:S(2)}) collective-permute-start(bf16[4,128,256]{2,1,0:T(8,128)(2,1)S(1)} %get-tuple-element.20), channel_id=1, source_target_pairs={{0,4},{2,6},{4,8},{6,10},{8,12},{10,14},{12,16},{14,18},{16,20},{1... | collective-permute-start | bytes 786440 | tf_op jit(solution)/shard_map/ppermute | solution.py:327
  28.3 66.0 %collective-permute-start.4 = (bf16[4,128,256]{2,1,0:T(8,128)(2,1)S(1)}, bf16[4,128,256]{2,1,0:T(8,128)(2,1)S(1)}, u32[]{:S(2)}, u32[]{:S(2)}) collective-permute-start(bf16[4,128,256]{2,1,0:T(8,128)(2,1)S(1)} %get-tuple-element.21), channel_id=1, source_target_pairs={{4,0},{6,2},{8,4},{10,6},{12,8},{14,10},{16,12},{18,14},{20,16},{2... | collective-permute-start | bytes 786440 | tf_op jit(solution)/shard_map/ppermute | solution.py:327
  63.7 2.0 %copy-start = (bf16[64,128,256]{2,1,0:T(8,128)(2,1)}, bf16[64,128,256]{2,1,0:T(8,128)(2,1)S(1)}, u32[]{:S(2)}) copy-start(bf16[64,128,256]{2,1,0:T(8,128)(2,1)S(1)} %get-tuple-element.24.refs_1_.refs_2_.refs_3_.refs_4_) | copy-start | bytes 12582916
  98.3 47.4 %collective-permute-start.5 = (bf16[32,128,256]{2,1,0:T(8,128)(2,1)S(1)}, bf16[32,128,256]{2,1,0:T(8,128)(2,1)}, u32[]{:S(2)}, u32[]{:S(2)}) collective-permute-start(bf16[32,128,256]{2,1,0:T(8,128)(2,1)S(1)} %fock_rows.3), channel_id=1, source_target_pairs={{0,1},{1,0},{2,3},{3,2},{4,5},{5,4},{6,7},{7,6},{8,9},{9,8},{10,11... | collective-permute-start | bytes 6291464 | tf_op jit(solution)/shard_map/ppermute | solution.py:331
  100.5 25.0 %collective-permute-start.7 = (bf16[16,128,256]{2,1,0:T(8,128)(2,1)S(1)}, bf16[16,128,256]{2,1,0:T(8,128)(2,1)}, u32[]{:S(2)}, u32[]{:S(2)}) collective-permute-start(bf16[16,128,256]{2,1,0:T(8,128)(2,1)S(1)} %slice.7), channel_id=1, source_target_pairs={{0,2},{2,0},{4,6},{6,4},{8,10},{10,8},{12,14},{14,12},{16,18},{18,... | collective-permute-start | bytes 3145736 | tf_op jit(solution)/shard_map/ppermute | solution.py:331
  129.1 8.3 %copy-start.6 = (f32[64,128]{1,0:T(8,128)S(1)}, f32[64,128]{1,0:T(8,128)}, u32[]{:S(2)}) copy-start(f32[64,128]{1,0:T(8,128)} %energy.3) | copy-start | bytes 98308
  129.1 12.6 %copy-start.4 = (s32[96]{0:T(128)S(1)}, s32[96]{0:T(128)}, u32[]{:S(2)}) copy-start(s32[96]{0:T(128)} %get-tuple-element.14.meta_ref) | copy-start | bytes 1156

commit v2 on v1

--- a/solution.py
+++ b/solution.py
@@ -12,12 +12,17 @@
 NPUR = 6
 OFFSETS = (1, -1, 2, -2)
 SLOTS = len(OFFSETS) * CAPG
-LOCAL_STEP = 4
-ROW_STEP = 16
-PURE_STEP = 4
-ENERGY_STEP = 4
+LOCAL_STEP = 8
+ROW_STEP = 8
+PITCH = 136
+PURE_STEP = 8
+ENERGY_STEP = 8
+FIRST = 24
+SECOND = 32
+ANY = pl.BlockSpec(memory_space=pl.ANY)
 NONE = float(1 << 20)
 SMEM = pl.BlockSpec(memory_space=pltpu.SMEM)
+SMALL = pl.CostEstimate(flops=1 << 16, bytes_accessed=1 << 12, transcendentals=0)
 F32 = jnp.float32
 BF16 = jnp.bfloat16
 
@@ -26,7 +31,7 @@
     return jnp.dot(left, right, preferred_element_type=F32)
 
 
-def params(mib=48):
+def params(mib):
     return pltpu.CompilerParams(vmem_limit_bytes=mib << 20)
 
 
@@ -136,15 +141,19 @@
             scratch_shapes=[pltpu.VMEM((count, 256, 256), BF16)],
         ),
         out_shape=[jax.ShapeDtypeStruct((CAPG, 128, 256), BF16)] * count,
-        compiler_params=params(),
-        cost_estimate=pl.CostEstimate(flops=16 * 2 * 128 * 256 * 256, bytes_accessed=4 << 20, transcendentals=0),
+        compiler_params=params(56),
+        cost_estimate=SMALL,
         name="outgoing",
     )(meta, inner, sent, *[esp_kernel] * count, *[density] * count, *[other] * count)
 
 
-def local_kernel(inner_ref, own, other, esp, response, core, weights, image_out, sum_out, wide, sums, whole):
+def local_kernel(inner_ref, own, other, esp, response, core, weights, after, image_out, sum_out, part_out, wide, sums, whole):
     step = pl.program_id(0)
     loads = 64 // LOCAL_STEP
+
+    @pl.when((step * LOCAL_STEP >= FIRST) & (step * LOCAL_STEP < FIRST + SECOND))
+    def _():
+        part_out[...] = own[...]
 
     @pl.when(step < loads)
     def _():
@@ -154,7 +163,7 @@
             result = dot(both, whole[f])
             image = result[:128].astype(BF16)
             image_out[f] = image
-            rows = pl.ds(pl.multiple_of((step * LOCAL_STEP + f) * 128, 128), 128)
+            rows = pl.ds(pl.multiple_of((step * LOCAL_STEP + f) * PITCH, 8), 128)
             image = image.astype(F32)
             total = result[128:] + core[f].astype(F32)
             for side in range(2):
@@ -167,7 +176,7 @@
         base = (step - loads) * ROW_STEP
         out = sum_out
         for r in range(ROW_STEP):
-            at = pl.ds(base + r, 64, stride=128)
+            at = pl.ds(base + r, 64, stride=PITCH)
             tile = jnp.concatenate([wide[0, at, :], wide[1, at, :]], axis=1).astype(BF16)
             mixed = dot(matrix, jnp.concatenate([tile, tile, tile], axis=0))
             for side in range(2):
@@ -176,7 +185,7 @@
                 )
 
 
-def make_local(inner, density, other, esp_kernel, coulomb_kernel, core_hamiltonian, weights):
+def make_local(inner, density, other, esp_kernel, coulomb_kernel, core_hamiltonian, weights, after):
     loads, rows = 64 // LOCAL_STEP, 128 // ROW_STEP
     block = pl.BlockSpec((LOCAL_STEP, 128, 256), lambda t, i: (jnp.minimum(t, loads - 1), 0, 0))
     return pl.pallas_call(
@@ -184,25 +193,33 @@
         grid_spec=pltpu.PrefetchScalarGridSpec(
             num_scalar_prefetch=1,
             grid=(loads + rows,),
-            in_specs=[block] * 5 + [pl.BlockSpec((64, 192), lambda t, i: (0, 0))],
-            out_specs=[block, pl.BlockSpec((2, 64 * ROW_STEP, 128), lambda t, i: (0, jnp.maximum(t - loads, 0), 0))],
+            in_specs=[block] * 5 + [pl.BlockSpec((64, 192), lambda t, i: (0, 0)), ANY],
+            out_specs=[
+                block,
+                pl.BlockSpec((2, 64 * ROW_STEP, 128), lambda t, i: (0, jnp.maximum(t - loads, 0), 0)),
+                pl.BlockSpec(
+                    (LOCAL_STEP, 128, 256),
+                    lambda t, i: (jnp.clip(t - FIRST // LOCAL_STEP, 0, SECOND // LOCAL_STEP - 1), 0, 0),
+                ),
+            ],
             scratch_shapes=[
-                pltpu.VMEM((2, 64 * 128, 128), F32),
-                pltpu.VMEM((2, 64 * 128, 128), F32),
+                pltpu.VMEM((2, 64 * PITCH, 128), F32),
+                pltpu.VMEM((2, 64 * PITCH, 128), F32),
                 pltpu.VMEM((LOCAL_STEP, 256, 256), BF16),
             ],
         ),
         out_shape=[
             jax.ShapeDtypeStruct((64, 128, 256), BF16),
             jax.ShapeDtypeStruct((2, rows * 64 * ROW_STEP, 128), F32),
+            jax.ShapeDtypeStruct((SECOND, 128, 256), BF16),
         ],
-        compiler_params=params(),
-        cost_estimate=pl.CostEstimate(flops=64 * 2 * 256 * 256 * 256, bytes_accessed=32 << 20, transcendentals=0),
+        compiler_params=params(32),
+        cost_estimate=SMALL,
         name="local",
-    )(inner, density, other, esp_kernel, coulomb_kernel, core_hamiltonian, weights)
-
-
-def fock_kernel(meta_ref, first_ref, sums, *refs):
+    )(inner, density, other, esp_kernel, coulomb_kernel, core_hamiltonian, weights, after)
+
+
+def fock_kernel(meta_ref, first_ref, began, sums, *refs):
     arrived, out, total = refs[:-2], refs[-2], refs[-1]
     step = pl.program_id(0)
     count = out.shape[0]
@@ -221,7 +238,7 @@
     out[...] = total[...].astype(BF16)
 
 
-def make_fock(meta, first, sums, arrived, number, count=8):
+def make_fock(meta, first, sums, arrived, began, number=32, count=8):
     tiles = 128 // ROW_STEP
     blocked = sums.reshape(2, tiles, 64 * ROW_STEP, 128)
     whole = pl.BlockSpec((CAPG, 128, 256), lambda t, m, f: (0, 0, 0))
@@ -230,19 +247,21 @@
         grid_spec=pltpu.PrefetchScalarGridSpec(
             num_scalar_prefetch=2,
             grid=(number // count,),
-            in_specs=[pl.BlockSpec((2, tiles, count * ROW_STEP, 128), lambda t, m, f: (0, 0, f[0] // count + t, 0))]
+            in_specs=[ANY, pl.BlockSpec((2, tiles, count * ROW_STEP, 128), lambda t, m, f: (0, 0, f[0] // count + t, 0))]
             + [whole] * len(OFFSETS),
             out_specs=pl.BlockSpec((count, 128, 256), lambda t, m, f: (t, 0, 0)),
             scratch_shapes=[pltpu.VMEM((count, 128, 256), F32)],
         ),
         out_shape=jax.ShapeDtypeStruct((number, 128, 256), BF16),
-        compiler_params=params(),
-        cost_estimate=pl.CostEstimate(flops=1 << 22, bytes_accessed=number * 3 << 16, transcendentals=0),
+        compiler_params=params(48),
+        cost_estimate=SMALL,
         name="fock_rows",
-    )(meta, first, blocked, *arrived)
-
-
-def pure_kernel(inner_ref, own, other, fock_out, density_out):
+    )(meta, first, began, blocked, *arrived)
+
+
+def pure_kernel(inner_ref, own, other, part, lines, fock_out, density_out, part_out, lines_out):
+    part_out[...] = part[...]
+    lines_out[...] = lines[...]
     row = lax.broadcasted_iota(jnp.int32, (256, 256), 0)
     column = lax.broadcasted_iota(jnp.int32, (256, 256), 1)
     diagonal = row == column
@@ -267,32 +286,37 @@
         density_out[f] = estimates[f]
 
 
-def make_pure(inner, own, other):
+def make_pure(inner, own, other, density, lines):
     number = own.shape[0]
+    last = 64 - FIRST - SECOND
+    part = last // (number // PURE_STEP)
+    skip = (FIRST + SECOND) // part
     rows = pl.BlockSpec((PURE_STEP, 128, 256), lambda t, i: (t, 0, 0))
+    flat = pl.BlockSpec((64, 128), lambda t, i: (0, 0))
     whole = pl.BlockSpec((PURE_STEP, 256, 256), lambda t, i: (t, 0, 0))
     return pl.pallas_call(
         pure_kernel,
         grid_spec=pltpu.PrefetchScalarGridSpec(
             num_scalar_prefetch=1,
             grid=(number // PURE_STEP,),
-            in_specs=[rows, rows],
-            out_specs=[whole, whole],
-        ),
-        out_shape=[jax.ShapeDtypeStruct((number, 256, 256), BF16)] * 2,
-        compiler_params=params(),
-        cost_estimate=pl.CostEstimate(flops=number * 13 * 2 * 256**3, bytes_accessed=number * 3 << 17, transcendentals=0),
+            in_specs=[rows, rows, pl.BlockSpec((part, 128, 256), lambda t, i: (skip + t, 0, 0)), flat],
+            out_specs=[whole, whole, pl.BlockSpec((part, 128, 256), lambda t, i: (t, 0, 0)), flat],
+        ),
+        out_shape=[jax.ShapeDtypeStruct((number, 256, 256), BF16)] * 2
+        + [jax.ShapeDtypeStruct((last, 128, 256), BF16), jax.ShapeDtypeStruct((64, 128), F32)],
+        compiler_params=params(28),
+        cost_estimate=SMALL,
         name="purify",
-    )(inner, own, other)
-
-
-def energy_kernel(meta_ref, first, swapped, *refs):
+    )(inner, own, other, density, lines)
+
+
+def energy_kernel(meta_ref, first, swapped, before, *refs):
     images, out = refs[:-1], refs[-1]
     step = pl.program_id(0)
 
     @pl.when(step == 0)
     def _():
-        out[...] = jnp.zeros_like(out)
+        out[...] = before[...]
 
     for f in range(ENERGY_STEP):
         product = swapped[f].astype(F32) * images[f][0].astype(F32)
@@ -301,7 +325,7 @@
         out[pl.ds(place, 1), :] = line[:, :128] + line[:, 128:]
 
 
-def make_energy(meta, first, swapped, image):
+def make_energy(meta, first, swapped, image, before):
     number = swapped.shape[0]
 
     def block(f):
@@ -312,14 +336,17 @@
         grid_spec=pltpu.PrefetchScalarGridSpec(
             num_scalar_prefetch=1,
             grid=(number // ENERGY_STEP,),
-            in_specs=[pl.BlockSpec((ENERGY_STEP, 128, 256), lambda t, m: (t, 0, 0))]
+            in_specs=[
+                pl.BlockSpec((ENERGY_STEP, 128, 256), lambda t, m: (t, 0, 0)),
+                pl.BlockSpec((64, 128), lambda t, m: (0, 0)),
+            ]
             + [block(f) for f in range(ENERGY_STEP)],
             out_specs=pl.BlockSpec((64, 128), lambda t, m: (0, 0)),
         ),
         out_shape=jax.ShapeDtypeStruct((64, 128), F32),
-        cost_estimate=pl.CostEstimate(flops=number << 16, bytes_accessed=number << 17, transcendentals=0),
+        cost_estimate=SMALL,
         name="energy",
-    )(meta, swapped, *[image] * ENERGY_STEP)
+    )(meta, swapped, before, *[image] * ENERGY_STEP)
 
 
 def along(array, axis, by):
@@ -331,23 +358,26 @@
     return lax.ppermute(array, axis, [(i, i ^ 1) for i in range(lax.axis_size(axis))])
 
 
-CUTS = (0, 48, 64)
-
-
 def body(density, core_hamiltonian, coulomb_kernel, esp_kernel, contacts, coupling, partner):
     own = lax.axis_index("frag").astype(jnp.int32).reshape(1)
     inner = lax.axis_index("inner").astype(jnp.int32).reshape(1)
+    first = exchanged(density[:FIRST], "frag")
     other = exchanged(density, "inner")
-    swapped = [exchanged(density[a:b], "frag") for a, b in zip(CUTS, CUTS[1:])]
     meta, sent, weights = make_index(own, contacts.T, coupling.T, partner)
     outgoing = make_outgoing(meta, inner, sent, esp_kernel, density, other)
     arrived = [along(block, "frag", by) for block, by in zip(outgoing, OFFSETS)]
-    image, sums = make_local(inner, density, other, esp_kernel, coulomb_kernel, core_hamiltonian, weights)
-    leave = make_fock(meta, 32 - inner * 32, sums, arrived, 32)
-    stay = make_fock(meta, inner * 32, sums, arrived, 32)
+    image, sums, part = make_local(
+        inner, density, other, esp_kernel, coulomb_kernel, core_hamiltonian, weights, outgoing[-1]
+    )
+    second = exchanged(part, "frag")
+    leave = make_fock(meta, 32 - inner * 32, sums, arrived, first)
+    stay = make_fock(meta, inner * 32, sums, arrived, first)
     came = exchanged(leave, "inner")
-    fock, new_density = make_pure(inner, stay, came)
-    lines = sum(make_energy(meta, a, part, image) for a, part in zip(CUTS, swapped))
+    lines = make_energy(meta, 0, first, image, jnp.zeros((64, 128), F32))
+    fock, new_density, part, lines = make_pure(inner, stay, came, density, lines)
+    third = exchanged(part, "frag")
+    lines = make_energy(meta, FIRST, second, image, lines)
+    lines = make_energy(meta, FIRST + SECOND, third, image, lines)
     energy = lax.psum(jnp.sum(lines, axis=1) * (1.0 / 256), "inner")
     return (fock, new_density, energy)
 

time: 176 us -> 135 us (0.77)
  waiting for transfers between devices: 53.5 us -> 25 us
  Pallas kernels: 82.6 us -> 71.5 us
    ppermute x4, waiting for transfers between devices: 28.6 us -> 5.76 us  [along(): lax.ppermute(array, axis, [(i, i + by) for i in range(length) if 0 <= i +...]
    pallas_call x1, Pallas kernels: 27.5 us -> 18.4 us  [make_local(): pl.pallas_call(local_kernel, grid_spec=pltpu.PrefetchScalarGridSpec(num_s...]
    ppermute x4 -> x5, waiting for transfers between devices: 24.9 us -> 19.3 us  [exchanged(): lax.ppermute(array, axis, [(i, i ^ 1) for i in range(lax.axis_size(axis))])]
    pallas_call x1, Pallas kernels: 28.2 us -> 24.2 us  [make_pure(): pl.pallas_call(pure_kernel, grid_spec=pltpu.PrefetchScalarGridSpec(num_sc...]
    slice x2 -> x1, local copies, waits for them, and re-layouts: 5.2 us -> 2.7 us  [body(): first = exchanged(density[:FIRST], 'frag')]
    ppermute x4 -> x5, starting transfers between devices: 2.92 us -> 4.25 us  [exchanged(): lax.ppermute(array, axis, [(i, i ^ 1) for i in range(lax.axis_size(axis))])]
    unnamed x14 -> x26, local copies, waits for them, and re-layouts: 5.42 us -> 6.53 us
    pallas_call x2 -> x3, Pallas kernels: 11.9 us -> 10.8 us  [make_energy(): pl.pallas_call(lambda meta_ref, *refs: energy_kernel(meta_ref, first, *re...]
  transfers between devices with their start and end apart: 8 -> 9, of which waited for: 5 -> 4; matrix products, arithmetic and copies ran while one was open for 3% -> 2% of each run, Pallas kernels for 31% -> 48%
where the time goes in v2:
time: 135 us; the launch traced here: 134 us
  Pallas kernels  71.5 us (53%)
  waiting for transfers between devices  25 us (19%)
  starting transfers between devices  22.6 us (17%)
  local copies, waits for them, and re-layouts  9.85 us (7%)
  blocking collectives  3.41 us (3%)
    pallas_call x1, Pallas kernels, make_pure(): pl.pallas_call(pure_kernel, grid_spec=pltpu.PrefetchScalarGridSpec(num_sc...  24.2 us
    ppermute x5, waiting for transfers between devices, exchanged(): lax.ppermute(array, axis, [(i, i ^ 1) for i in range(lax.axis_size(axis))])  19.3 us
    pallas_call x1, Pallas kernels, make_local(): pl.pallas_call(local_kernel, grid_spec=pltpu.PrefetchScalarGridSpec(num_s...  18.4 us
    ppermute x4, starting transfers between devices, along(): lax.ppermute(array, axis, [(i, i + by) for i in range(length) if 0 <= i +...  18.3 us
    pallas_call x3, Pallas kernels, make_energy(): pl.pallas_call(lambda meta_ref, *refs: energy_kernel(meta_ref, first, *re...  10.8 us
    pallas_call x2, Pallas kernels, make_fock(): pl.pallas_call(fock_kernel, grid_spec=pltpu.PrefetchScalarGridSpec(num_sc...  9.6 us
    unnamed x26, local copies, waits for them, and re-layouts  6.53 us
    ppermute x4, waiting for transfers between devices, along(): lax.ppermute(array, axis, [(i, i + by) for i in range(length) if 0 <= i +...  5.76 us
  transfers between devices with their start and end apart: 9, of which 4 were waited for; matrix products, arithmetic and copies ran while one was open for 2% of the time, Pallas kernels for 48%

profile of v2, /device:TPU:97, one launch (start us, length us, event | category | flops | bytes accessed | tf_op | source)
XLA Modules:
  0.0 134.0 jit_solution(10601518294671071078)
XLA Ops:
  0.6 0.8 collective-permute-start.1
  1.4 2.7 %slice.3 = bf16[24,128,256]{2,1,0:T(8,128)(2,1)} slice(bf16[64,128,256]{2,1,0:T(8,128)(2,1)} %part.1), slice={[0:24], [0:128], [0:256]} | slice | bytes 3145728 | tf_op jit(solution)/shard_map/slice | solution.py:364
  4.1 1.2 collective-permute-start
  5.3 3.0 %slots.1 = (s32[96]{0:T(128)}, f32[16]{0:T(128)}, bf16[64,192]{1,0:T(8,128)(2,1)}) custom-call(s32[1]{0:T(128)} %bitcast.1.own_ref, s32[16,4096]{1,0:T(8,128)} %bitcast.7, s32[16,4096]{1,0:T(8,128)} %bitcast.8, s32[16,4096]{1,0:T(8,128)} %bitcast.9, f32[16,64]{1,0:T(8,128)} %bitcast.10, f32[16,64]{1,0:T(8,128)} %bitcast.11, s32[64]{0:T(128)} %partner_ref.1), custom_call_target="tpu_custom_call" | custom-call | tf_op jit(solution)/shard_map/slots/pallas_call | solution.py:92
  8.4 0.2 collective-permute-done.1.refs_8_.refs_9_.refs_10_.refs_11_.other
  8.5 5.4 %outgoing.1 = (bf16[4,128,256]{2,1,0:T(8,128)(2,1)}, bf16[4,128,256]{2,1,0:T(8,128)(2,1)}, bf16[4,128,256]{2,1,0:T(8,128)(2,1)}, bf16[4,128,256]{2,1,0:T(8,128)(2,1)}) custom-call(s32[96]{0:T(128)} %get-tuple-element.17.meta_ref, s32[1]{0:T(128)} %bitcast.inner_ref, f32[16]{0:T(128)} %get-tuple-element.19.sent_ref, bf16[64,128,256]{2,1,0:T(8,128)(2,1)} %esp.1, ...), custom_call_target="tpu_custom_call" | custom-call | flops 65536 | bytes 4096 | tf_op jit(solution)/shard_map/outgoing/pallas_call | solution.py:134
  14.0 6.9 %collective-permute-start.5 = (bf16[4,128,256]{2,1,0:T(8,128)(2,1)}, bf16[4,128,256]{2,1,0:T(8,128)(2,1)S(1)}, u32[]{:S(2)}, u32[]{:S(2)}) collective-permute-start(bf16[4,128,256]{2,1,0:T(8,128)(2,1)} %get-tuple-element.20.after), channel_id=1, source_target_pairs={{4,0},{6,2},{8,4},{10,6},{12,8},{14,10},{16,12},{18,14},{20,16},{2... | collective-permute-start | bytes 786440 | tf_op jit(solution)/shard_map/ppermute | solution.py:354
  20.9 2.2 %collective-permute-start.2 = (bf16[4,128,256]{2,1,0:T(8,128)(2,1)}, bf16[4,128,256]{2,1,0:T(8,128)(2,1)S(1)}, u32[]{:S(2)}, u32[]{:S(2)}) collective-permute-start(bf16[4,128,256]{2,1,0:T(8,128)(2,1)} %get-tuple-element.22), channel_id=1, source_target_pairs={{0,2},{2,4},{4,6},{6,8},{8,10},{10,12},{12,14},{14,16},{16,18},{18... | collective-permute-start | bytes 786440 | tf_op jit(solution)/shard_map/ppermute | solution.py:354
  23.0 7.3 %collective-permute-start.3 = (bf16[4,128,256]{2,1,0:T(8,128)(2,1)}, bf16[4,128,256]{2,1,0:T(8,128)(2,1)S(1)}, u32[]{:S(2)}, u32[]{:S(2)}) collective-permute-start(bf16[4,128,256]{2,1,0:T(8,128)(2,1)} %get-tuple-element.23), channel_id=1, source_target_pairs={{2,0},{4,2},{6,4},{8,6},{10,8},{12,10},{14,12},{16,14},{18,16},{20... | collective-permute-start | bytes 786440 | tf_op jit(solution)/shard_map/ppermute | solution.py:354
  30.4 1.9 %collective-permute-start.4 = (bf16[4,128,256]{2,1,0:T(8,128)(2,1)}, bf16[4,128,256]{2,1,0:T(8,128)(2,1)S(1)}, u32[]{:S(2)}, u32[]{:S(2)}) collective-permute-start(bf16[4,128,256]{2,1,0:T(8,128)(2,1)} %get-tuple-element.24), channel_id=1, source_target_pairs={{0,4},{2,6},{4,8},{6,10},{8,12},{10,14},{12,16},{14,18},{16,20},{1... | collective-permute-start | bytes 786440 | tf_op jit(solution)/shard_map/ppermute | solution.py:354
  32.3 0.0 copy-start.3
  32.3 2.2 %copy-done.3 = bf16[64,128,256]{2,1,0:T(8,128)(2,1)S(1)} copy-done((bf16[64,128,256]{2,1,0:T(8,128)(2,1)S(1)}, bf16[64,128,256]{2,1,0:T(8,128)(2,1)}, u32[]{:S(2)}) %copy-start.3) | copy-done | bytes 4194328
  34.5 0.9 copy-done.6
  35.5 18.4 %local.1 = (bf16[64,128,256]{2,1,0:T(8,128)(2,1)S(1)}, f32[2,8192,128]{2,1,0:T(8,128)}, bf16[32,128,256]{2,1,0:T(8,128)(2,1)}) custom-call(s32[1]{0:T(128)} %bitcast.inner_ref, bf16[64,128,256]{2,1,0:T(8,128)(2,1)S(1)} %copy-done.1, bf16[64,128,256]{2,1,0:T(8,128)(2,1)} %collective-permute-done.1.refs_8_.refs_9_.refs_10_.refs_11_.other, ...), custom_call_target="tpu_custom_call" | custom-call | flops 65536 | bytes 4096 | tf_op jit(solution)/shard_map/local/pallas_call | solution.py:191
  53.9 2.0 %copy-done = bf16[64,128,256]{2,1,0:T(8,128)(2,1)} copy-done((bf16[64,128,256]{2,1,0:T(8,128)(2,1)}, bf16[64,128,256]{2,1,0:T(8,128)(2,1)S(1)}, u32[]{:S(2)}) %copy-start) | copy-done | bytes 4194328
  55.9 5.7 %collective-permute-done.4.refs_2_ = bf16[4,128,256]{2,1,0:T(8,128)(2,1)S(1)} collective-permute-done((bf16[4,128,256]{2,1,0:T(8,128)(2,1)}, bf16[4,128,256]{2,1,0:T(8,128)(2,1)S(1)}, u32[]{:S(2)}, u32[]{:S(2)}) %collective-permute-start.4) | collective-permute-done | bytes 262176 | tf_op jit(solution)/shard_map/ppermute | solution.py:354
  61.6 5.3 %fock_rows.3 = bf16[32,128,256]{2,1,0:T(8,128)(2,1)} custom-call(s32[96]{0:T(128)S(1)} %copy-done.10, s32[1]{0:T(128)S(6)} %sub.3.first_ref, bf16[24,128,256]{2,1,0:T(8,128)(2,1)S(1)} %collective-permute-done.began.refs_0_, f32[2,16,512,128]{3,2,1,0:T(8,128)} %bitcast.5, bf16[4,128,256]{2,1,0:T(8,128)(2,1)S(1)} %collective-permute-done.2.refs_0_, ...), custom_call_target="tpu_custom_call" | custom-call | flops 65536 | bytes 4096 | tf_op jit(solution)/shard_map/fock_rows/pallas_call | solution.py:245
  66.9 0.8 collective-permute-start.6
  67.7 0.6 broadcast_in_dim.3.refs_1_
  68.3 4.0 %energy.3.lines = f32[64,128]{1,0:T(8,128)} custom-call(s32[96]{0:T(128)} %get-tuple-element.17.meta_ref, bf16[24,128,256]{2,1,0:T(8,128)(2,1)} %copy-done.4, f32[64,128]{1,0:T(8,128)} %broadcast_in_dim.3.refs_1_, bf16[64,128,256]{2,1,0:T(8,128)(2,1)} %copy-done, bf16[64,128,256]{2,1,0:T(8,128)(2,1)} %copy-done, bf16[64,128,256]{2,1,0:T(8,128)(2,1)} %copy-done, ...), custom_call_target="tpu_custom_call" | custom-call | flops 65536 | bytes 4096 | tf_op jit(solution)/shard_map/energy/pallas_call | solution.py:334
  72.4 0.0 copy-start.2
  72.4 4.3 %fock_rows.2.own = bf16[32,128,256]{2,1,0:T(8,128)(2,1)S(1)} custom-call(s32[96]{0:T(128)S(1)} %copy-done.11, s32[1]{0:T(128)S(6)} %mul.10.first_ref, bf16[24,128,256]{2,1,0:T(8,128)(2,1)S(1)} %copy-done.5, f32[2,16,512,128]{3,2,1,0:T(8,128)} %bitcast.6, bf16[4,128,256]{2,1,0:T(8,128)(2,1)S(1)} %collective-permute-done.2.refs_0_, ...), custom_call_target="tpu_custom_call" | custom-call | flops 65536 | bytes 4096 | tf_op jit(solution)/shard_map/fock_rows/pallas_call | solution.py:245
  76.8 24.2 %purify.1 = (bf16[32,256,256]{2,1,0:T(8,128)(2,1)}, bf16[32,256,256]{2,1,0:T(8,128)(2,1)}, bf16[8,128,256]{2,1,0:T(8,128)(2,1)S(1)}, f32[64,128]{1,0:T(8,128)S(1)}) custom-call(s32[1]{0:T(128)} %bitcast.inner_ref, bf16[32,128,256]{2,1,0:T(8,128)(2,1)S(1)} %fock_rows.2.own, bf16[32,128,256]{2,1,0:T(8,128)(2,1)} %collective-permute-done.6.other, ...), custom_call_target="tpu_custom_call" | custom-call | flops 65536 | bytes 4096 | tf_op jit(solution)/shard_map/purify/pallas_call | solution.py:297
  101.0 0.6 copy-done.9
  101.6 1.5 %collective-permute-start.7 = (bf16[8,128,256]{2,1,0:T(8,128)(2,1)S(1)}, bf16[8,128,256]{2,1,0:T(8,128)(2,1)S(1)}, u32[]{:S(2)}, u32[]{:S(2)}) collective-permute-start(bf16[8,128,256]{2,1,0:T(8,128)(2,1)S(1)} %get-tuple-element.28), channel_id=1, source_target_pairs={{0,2},{2,0},{4,6},{6,4},{8,10},{10,8},{12,14},{14,12},{16,18},{18,... | collective-permute-start | bytes 1572872 | tf_op jit(solution)/shard_map/ppermute | solution.py:358
  103.1 12.2 %collective-permute-done.8.refs_0_ = bf16[32,128,256]{2,1,0:T(8,128)(2,1)} collective-permute-done((bf16[32,128,256]{2,1,0:T(8,128)(2,1)}, bf16[32,128,256]{2,1,0:T(8,128)(2,1)}, u32[]{:S(2)}, u32[]{:S(2)}) %collective-permute-start.8) | collective-permute-done | bytes 2097184 | tf_op jit(solution)/shard_map/ppermute | solution.py:358
  115.3 4.2 %energy.4.refs_1_ = f32[64,128]{1,0:T(8,128)} custom-call(s32[96]{0:T(128)} %get-tuple-element.17.meta_ref, bf16[32,128,256]{2,1,0:T(8,128)(2,1)} %collective-permute-done.8.refs_0_, f32[64,128]{1,0:T(8,128)} %copy-done.9, bf16[64,128,256]{2,1,0:T(8,128)(2,1)} %copy-done, bf16[64,128,256]{2,1,0:T(8,128)(2,1)} %copy-done, bf16[64,128,256]{2,1,0:T(8,128)(2,1)} %copy-done, ...), custom_call_target="tpu_custom_call" | custom-call | flops 65536 | bytes 4096 | tf_op jit(solution)/shard_map/energy/pallas_call | solution.py:334
  119.5 6.9 %collective-permute-done.7.refs_0_ = bf16[8,128,256]{2,1,0:T(8,128)(2,1)S(1)} collective-permute-done((bf16[8,128,256]{2,1,0:T(8,128)(2,1)S(1)}, bf16[8,128,256]{2,1,0:T(8,128)(2,1)S(1)}, u32[]{:S(2)}, u32[]{:S(2)}) %collective-permute-start.7) | collective-permute-done | bytes 524320 | tf_op jit(solution)/shard_map/ppermute | solution.py:358
  126.4 0.8 copy-done.12
  127.2 2.5 %energy.5 = f32[64,128]{1,0:T(8,128)} custom-call(s32[96]{0:T(128)} %get-tuple-element.17.meta_ref, bf16[8,128,256]{2,1,0:T(8,128)(2,1)} %copy-done.12, f32[64,128]{1,0:T(8,128)} %energy.4.refs_1_, bf16[64,128,256]{2,1,0:T(8,128)(2,1)} %copy-done, bf16[64,128,256]{2,1,0:T(8,128)(2,1)} %copy-done, bf16[64,128,256]{2,1,0:T(8,128)(2,1)} %copy-done, ...), custom_call_target="tpu_custom_call" | custom-call | flops 65536 | bytes 4096 | tf_op jit(solution)/shard_map/energy/pallas_call | solution.py:334
  129.7 0.9 reduce_sum.9
  130.6 3.4 %psum.7 = f32[64]{0:T(128)} all-reduce(f32[64]{0:T(128)S(1)} %broadcast_multiply_fusion), channel_id=1, replica_groups=mesh['frag'=64,'inner'=2] {'inner'}, use_global_device_ids=true, to_apply=%region_1.0 | all-reduce | flops 64 | bytes 512 | tf_op jit(solution)/shard_map/psum | solution.py:381
  (26 shorter events, 0.1 us)
Async XLA Ops:
  0.6 7.9 %collective-permute-start.1 = (bf16[64,128,256]{2,1,0:T(8,128)(2,1)}, bf16[64,128,256]{2,1,0:T(8,128)(2,1)}, u32[]{:S(2)}, u32[]{:S(2)}) collective-permute-start(bf16[64,128,256]{2,1,0:T(8,128)(2,1)} %part.1), channel_id=1, source_target_pairs={{0,1},{1,0},{2,3},{3,2},{4,5},{5,4},{6,7},{7,6},{8,9},{9,8},{10,11... | collective-permute-start | bytes 12582920 | tf_op jit(solution)/shard_map/ppermute | solution.py:358
  4.1 51.8 %collective-permute-start = (bf16[24,128,256]{2,1,0:T(8,128)(2,1)}, bf16[24,128,256]{2,1,0:T(8,128)(2,1)S(1)}, u32[]{:S(2)}, u32[]{:S(2)}) collective-permute-start(bf16[24,128,256]{2,1,0:T(8,128)(2,1)} %slice.3), channel_id=1, source_target_pairs={{0,2},{2,0},{4,6},{6,4},{8,10},{10,8},{12,14},{14,12},{16,18},{18,... | collective-permute-start | bytes 4718600 | tf_op jit(solution)/shard_map/ppermute | solution.py:358
  8.5 23.8 %copy-start.1 = (bf16[64,128,256]{2,1,0:T(8,128)(2,1)S(1)}, bf16[64,128,256]{2,1,0:T(8,128)(2,1)}, u32[]{:S(2)}) copy-start(bf16[64,128,256]{2,1,0:T(8,128)(2,1)} %part.1) | copy-start | bytes 12582916
  8.5 23.8 %copy-start.8 = (bf16[64,192]{1,0:T(8,128)(2,1)S(1)}, bf16[64,192]{1,0:T(8,128)(2,1)}, u32[]{:S(2)}) copy-start(bf16[64,192]{1,0:T(8,128)(2,1)} %get-tuple-element.18.weights) | copy-start | bytes 73732
  14.0 41.9 %collective-permute-start.5 = (bf16[4,128,256]{2,1,0:T(8,128)(2,1)}, bf16[4,128,256]{2,1,0:T(8,128)(2,1)S(1)}, u32[]{:S(2)}, u32[]{:S(2)}) collective-permute-start(bf16[4,128,256]{2,1,0:T(8,128)(2,1)} %get-tuple-element.20.after), channel_id=1, source_target_pairs={{4,0},{6,2},{8,4},{10,6},{12,8},{14,10},{16,12},{18,14},{20,16},{2... | collective-permute-start | bytes 786440 | tf_op jit(solution)/shard_map/ppermute | solution.py:354
  20.9 35.0 %collective-permute-start.2 = (bf16[4,128,256]{2,1,0:T(8,128)(2,1)}, bf16[4,128,256]{2,1,0:T(8,128)(2,1)S(1)}, u32[]{:S(2)}, u32[]{:S(2)}) collective-permute-start(bf16[4,128,256]{2,1,0:T(8,128)(2,1)} %get-tuple-element.22), channel_id=1, source_target_pairs={{0,2},{2,4},{4,6},{6,8},{8,10},{10,12},{12,14},{14,16},{16,18},{18... | collective-permute-start | bytes 786440 | tf_op jit(solution)/shard_map/ppermute | solution.py:354
  23.0 32.9 %collective-permute-start.3 = (bf16[4,128,256]{2,1,0:T(8,128)(2,1)}, bf16[4,128,256]{2,1,0:T(8,128)(2,1)S(1)}, u32[]{:S(2)}, u32[]{:S(2)}) collective-permute-start(bf16[4,128,256]{2,1,0:T(8,128)(2,1)} %get-tuple-element.23), channel_id=1, source_target_pairs={{2,0},{4,2},{6,4},{8,6},{10,8},{12,10},{14,12},{16,14},{18,16},{20... | collective-permute-start | bytes 786440 | tf_op jit(solution)/shard_map/ppermute | solution.py:354
  30.4 31.3 %collective-permute-start.4 = (bf16[4,128,256]{2,1,0:T(8,128)(2,1)}, bf16[4,128,256]{2,1,0:T(8,128)(2,1)S(1)}, u32[]{:S(2)}, u32[]{:S(2)}) collective-permute-start(bf16[4,128,256]{2,1,0:T(8,128)(2,1)} %get-tuple-element.24), channel_id=1, source_target_pairs={{0,4},{2,6},{4,8},{6,10},{8,12},{10,14},{12,16},{14,18},{16,20},{1... | collective-permute-start | bytes 786440 | tf_op jit(solution)/shard_map/ppermute | solution.py:354
  32.3 2.2 %copy-start.3 = (bf16[64,128,256]{2,1,0:T(8,128)(2,1)S(1)}, bf16[64,128,256]{2,1,0:T(8,128)(2,1)}, u32[]{:S(2)}) copy-start(bf16[64,128,256]{2,1,0:T(8,128)(2,1)} %esp.1) | copy-start | bytes 12582916
  34.5 0.9 copy-start.6
  35.5 26.2 %copy-start.10 = (s32[96]{0:T(128)S(1)}, s32[96]{0:T(128)}, u32[]{:S(2)}) copy-start(s32[96]{0:T(128)} %get-tuple-element.17.meta_ref) | copy-start | bytes 1156
  53.9 2.0 %copy-start = (bf16[64,128,256]{2,1,0:T(8,128)(2,1)}, bf16[64,128,256]{2,1,0:T(8,128)(2,1)S(1)}, u32[]{:S(2)}) copy-start(bf16[64,128,256]{2,1,0:T(8,128)(2,1)S(1)} %get-tuple-element.25.refs_2_.refs_3_.refs_4_.refs_5_.refs_6_.refs_7_.refs_8_.refs_9_) | copy-start | bytes 12582916
  55.9 11.1 %copy-start.4 = (bf16[24,128,256]{2,1,0:T(8,128)(2,1)}, bf16[24,128,256]{2,1,0:T(8,128)(2,1)S(1)}, u32[]{:S(2)}) copy-start(bf16[24,128,256]{2,1,0:T(8,128)(2,1)S(1)} %collective-permute-done.began.refs_0_) | copy-start | bytes 4718596
  66.9 9.8 %collective-permute-start.6 = (bf16[32,128,256]{2,1,0:T(8,128)(2,1)}, bf16[32,128,256]{2,1,0:T(8,128)(2,1)}, u32[]{:S(2)}, u32[]{:S(2)}) collective-permute-start(bf16[32,128,256]{2,1,0:T(8,128)(2,1)} %fock_rows.3), channel_id=1, source_target_pairs={{0,1},{1,0},{2,3},{3,2},{4,5},{5,4},{6,7},{7,6},{8,9},{9,8},{10,11... | collective-permute-start | bytes 6291464 | tf_op jit(solution)/shard_map/ppermute | solution.py:358
  67.7 47.6 %collective-permute-start.8 = (bf16[32,128,256]{2,1,0:T(8,128)(2,1)}, bf16[32,128,256]{2,1,0:T(8,128)(2,1)}, u32[]{:S(2)}, u32[]{:S(2)}) collective-permute-start(bf16[32,128,256]{2,1,0:T(8,128)(2,1)} %get-tuple-element.29), channel_id=1, source_target_pairs={{0,2},{2,0},{4,6},{6,4},{8,10},{10,8},{12,14},{14,12},{16,18},{18,... | collective-permute-start | bytes 6291464 | tf_op jit(solution)/shard_map/ppermute | solution.py:358
  68.3 4.0 %copy-start.5 = (bf16[24,128,256]{2,1,0:T(8,128)(2,1)S(1)}, bf16[24,128,256]{2,1,0:T(8,128)(2,1)}, u32[]{:S(2)}) copy-start(bf16[24,128,256]{2,1,0:T(8,128)(2,1)} %copy-done.4) | copy-start | bytes 4718596
  68.3 4.1 %copy-start.11 = (s32[96]{0:T(128)S(1)}, s32[96]{0:T(128)}, u32[]{:S(2)}) copy-start(s32[96]{0:T(128)} %get-tuple-element.17.meta_ref) | copy-start | bytes 1156
  72.4 4.4 %copy-start.2 = (bf16[64,128,256]{2,1,0:T(8,128)(2,1)S(1)}, bf16[64,128,256]{2,1,0:T(8,128)(2,1)}, u32[]{:S(2)}) copy-start(bf16[64,128,256]{2,1,0:T(8,128)(2,1)} %part.1) | copy-start | bytes 12582916
  72.4 4.4 %copy-start.7 = (f32[64,128]{1,0:T(8,128)S(1)}, f32[64,128]{1,0:T(8,128)}, u32[]{:S(2)}) copy-start(f32[64,128]{1,0:T(8,128)} %energy.3.lines) | copy-start | bytes 98308
  101.0 0.6 copy-start.9
  101.6 24.8 %collective-permute-start.7 = (bf16[8,128,256]{2,1,0:T(8,128)(2,1)S(1)}, bf16[8,128,256]{2,1,0:T(8,128)(2,1)S(1)}, u32[]{:S(2)}, u32[]{:S(2)}) collective-permute-start(bf16[8,128,256]{2,1,0:T(8,128)(2,1)S(1)} %get-tuple-element.28), channel_id=1, source_target_pairs={{0,2},{2,0},{4,6},{6,4},{8,10},{10,8},{12,14},{14,12},{16,18},{18,... | collective-permute-start | bytes 1572872 | tf_op jit(solution)/shard_map/ppermute | solution.py:358
  126.4 0.8 copy-start.12

commit v3 on v2

--- a/solution.py
+++ b/solution.py
@@ -19,6 +19,7 @@
 ENERGY_STEP = 8
 FIRST = 24
 SECOND = 32
+SHARES = (3, 1)
 ANY = pl.BlockSpec(memory_space=pl.ANY)
 NONE = float(1 << 20)
 SMEM = pl.BlockSpec(memory_space=pltpu.SMEM)
@@ -219,10 +220,10 @@
     )(inner, density, other, esp_kernel, coulomb_kernel, core_hamiltonian, weights, after)
 
 
-def fock_kernel(meta_ref, first_ref, began, sums, *refs):
-    arrived, out, total = refs[:-2], refs[-2], refs[-1]
+def fock_kernel(shares, meta_ref, first_ref, began, sums, *refs):
+    arrived, outs, total = refs[: len(OFFSETS)], refs[len(OFFSETS) : -1], refs[-1]
     step = pl.program_id(0)
-    count = out.shape[0]
+    count = total.shape[0]
     for side in range(2):
         total[:, :, side * 128 : side * 128 + 128] = jnp.concatenate(
             [sums[side, tile].reshape(count, ROW_STEP, 128) for tile in range(128 // ROW_STEP)], axis=1
@@ -235,31 +236,41 @@
         def _(slot=slot, place=place):
             total[place] += arrived[slot // CAPG][slot % CAPG].astype(F32)
 
-    out[...] = total[...].astype(BF16)
-
-
-def make_fock(meta, first, sums, arrived, began, number=32, count=8):
+    for part, out in enumerate(outs):
+        low = sum(shares[:part])
+
+        @pl.when((step >= low) & (step < low + shares[part]))
+        def _(out=out):
+            out[...] = total[...].astype(BF16)
+
+
+def make_fock(meta, first, sums, arrived, began, shares, count=8):
+    def out_block(part):
+        low, steps = sum(shares[:part]), shares[part]
+        return pl.BlockSpec((count, 128, 256), lambda t, m, f: (jnp.clip(t - low, 0, steps - 1), 0, 0))
+
     tiles = 128 // ROW_STEP
     blocked = sums.reshape(2, tiles, 64 * ROW_STEP, 128)
     whole = pl.BlockSpec((CAPG, 128, 256), lambda t, m, f: (0, 0, 0))
     return pl.pallas_call(
-        fock_kernel,
+        functools.partial(fock_kernel, shares),
         grid_spec=pltpu.PrefetchScalarGridSpec(
             num_scalar_prefetch=2,
-            grid=(number // count,),
+            grid=(sum(shares),),
             in_specs=[ANY, pl.BlockSpec((2, tiles, count * ROW_STEP, 128), lambda t, m, f: (0, 0, f[0] // count + t, 0))]
             + [whole] * len(OFFSETS),
-            out_specs=pl.BlockSpec((count, 128, 256), lambda t, m, f: (t, 0, 0)),
+            out_specs=[out_block(part) for part in range(len(shares))],
             scratch_shapes=[pltpu.VMEM((count, 128, 256), F32)],
         ),
-        out_shape=jax.ShapeDtypeStruct((number, 128, 256), BF16),
+        out_shape=[jax.ShapeDtypeStruct((share * count, 128, 256), BF16) for share in shares],
         compiler_params=params(48),
         cost_estimate=SMALL,
         name="fock_rows",
     )(meta, first, began, blocked, *arrived)
 
 
-def pure_kernel(inner_ref, own, other, part, lines, fock_out, density_out, part_out, lines_out):
+def pure_kernel(inner_ref, own, low, high, part, lines, fock_out, density_out, part_out, lines_out):
+    early = pl.program_id(0) < SHARES[0]
     part_out[...] = part[...]
     lines_out[...] = lines[...]
     row = lax.broadcasted_iota(jnp.int32, (256, 256), 0)
@@ -269,7 +280,7 @@
     turn = identity.astype(BF16)
     estimates = []
     for f in range(PURE_STEP):
-        assemble(fock_out.at[f], inner_ref[0], own[f], other[f])
+        assemble(fock_out.at[f], inner_ref[0], own[f], jnp.where(early, low[f], high[f]))
     for f in range(PURE_STEP):
         rows = fock_out[f]
         turned = lax.dot_general(turn, rows, (((1,), (1,)), ((), ())), preferred_element_type=F32)
@@ -286,20 +297,23 @@
         density_out[f] = estimates[f]
 
 
-def make_pure(inner, own, other, density, lines):
+def make_pure(inner, own, low, high, density, lines):
     number = own.shape[0]
     last = 64 - FIRST - SECOND
     part = last // (number // PURE_STEP)
     skip = (FIRST + SECOND) // part
     rows = pl.BlockSpec((PURE_STEP, 128, 256), lambda t, i: (t, 0, 0))
     flat = pl.BlockSpec((64, 128), lambda t, i: (0, 0))
+    half = SHARES[0]
+    low_rows = pl.BlockSpec((PURE_STEP, 128, 256), lambda t, i: (jnp.minimum(t, half - 1), 0, 0))
+    high_rows = pl.BlockSpec((PURE_STEP, 128, 256), lambda t, i: (jnp.maximum(t - half, 0), 0, 0))
     whole = pl.BlockSpec((PURE_STEP, 256, 256), lambda t, i: (t, 0, 0))
     return pl.pallas_call(
         pure_kernel,
         grid_spec=pltpu.PrefetchScalarGridSpec(
             num_scalar_prefetch=1,
             grid=(number // PURE_STEP,),
-            in_specs=[rows, rows, pl.BlockSpec((part, 128, 256), lambda t, i: (skip + t, 0, 0)), flat],
+            in_specs=[rows, low_rows, high_rows, pl.BlockSpec((part, 128, 256), lambda t, i: (skip + t, 0, 0)), flat],
             out_specs=[whole, whole, pl.BlockSpec((part, 128, 256), lambda t, i: (t, 0, 0)), flat],
         ),
         out_shape=[jax.ShapeDtypeStruct((number, 256, 256), BF16)] * 2
@@ -307,7 +321,7 @@
         compiler_params=params(28),
         cost_estimate=SMALL,
         name="purify",
-    )(inner, own, other, density, lines)
+    )(inner, own, low, high, density, lines)
 
 
 def energy_kernel(meta_ref, first, swapped, before, *refs):
@@ -347,6 +361,53 @@
         cost_estimate=SMALL,
         name="energy",
     )(meta, swapped, before, *[image] * ENERGY_STEP)
+
+
+def picked_kernel(meta_ref, *refs):
+    for f, image in enumerate(refs[:-1]):
+        refs[-1][f] = image[0]
+
+
+def make_picked(meta, first, number, image):
+    def block(f):
+        return pl.BlockSpec((1, 128, 256), lambda t, m: (m[2 * SLOTS + first + f], 0, 0))
+
+    return pl.pallas_call(
+        picked_kernel,
+        grid_spec=pltpu.PrefetchScalarGridSpec(
+            num_scalar_prefetch=1,
+            grid=(1,),
+            in_specs=[block(f) for f in range(number)],
+            out_specs=pl.BlockSpec((number, 128, 256), lambda t, m: (0, 0, 0)),
+        ),
+        out_shape=jax.ShapeDtypeStruct((number, 128, 256), BF16),
+        cost_estimate=SMALL,
+        name="picked",
+    )(meta, *[image] * number)
+
+
+def last_energy_kernel(meta_ref, first, swapped, before, image, out, lines):
+    lines[0:64] = before[...]
+    lines[64:128] = jnp.zeros((64, 128), F32)
+    for f in range(swapped.shape[0]):
+        place = meta_ref[2 * SLOTS + first + f]
+        line = jnp.sum(swapped[f].astype(F32) * image[f].astype(F32), axis=0, keepdims=True)
+        lines[pl.ds(place, 1), :] = line[:, :128] + line[:, 128:]
+    out[...] = jnp.sum(lines[...].T, axis=0, keepdims=True)[:, :64] * (1.0 / 256)
+
+
+def make_last_energy(meta, first, swapped, image, before):
+    vmem = pl.BlockSpec(memory_space=pltpu.VMEM)
+    return pl.pallas_call(
+        lambda meta_ref, *refs: last_energy_kernel(meta_ref, first, *refs),
+        in_specs=[SMEM, vmem, vmem, vmem],
+        out_specs=vmem,
+        out_shape=jax.ShapeDtypeStruct((1, 64), F32),
+        scratch_shapes=[pltpu.VMEM((128, 128), F32)],
+        cost_estimate=SMALL,
+        compiler_params=params(16),
+        name="energies",
+    )(meta, swapped, before, image)
 
 
 def along(array, axis, by):
@@ -370,15 +431,16 @@
         inner, density, other, esp_kernel, coulomb_kernel, core_hamiltonian, weights, outgoing[-1]
     )
     second = exchanged(part, "frag")
-    leave = make_fock(meta, 32 - inner * 32, sums, arrived, first)
-    stay = make_fock(meta, inner * 32, sums, arrived, first)
-    came = exchanged(leave, "inner")
+    low, high = make_fock(meta, 32 - inner * 32, sums, arrived, first, SHARES)
+    (stay,) = make_fock(meta, inner * 32, sums, arrived, first, (sum(SHARES),))
+    low, high = exchanged(low, "inner"), exchanged(high, "inner")
     lines = make_energy(meta, 0, first, image, jnp.zeros((64, 128), F32))
-    fock, new_density, part, lines = make_pure(inner, stay, came, density, lines)
+    fock, new_density, part, lines = make_pure(inner, stay, low, high, density, lines)
     third = exchanged(part, "frag")
     lines = make_energy(meta, FIRST, second, image, lines)
-    lines = make_energy(meta, FIRST + SECOND, third, image, lines)
-    energy = lax.psum(jnp.sum(lines, axis=1) * (1.0 / 256), "inner")
+    picked = make_picked(meta, FIRST + SECOND, third.shape[0], image)
+    partial = make_last_energy(meta, FIRST + SECOND, third, picked, lines)
+    energy = lax.psum(partial.reshape(64), "inner")
     return (fock, new_density, energy)
 
 

time: 135 us -> 125 us (0.926)
  waiting for transfers between devices: 25 us -> 12.3 us
  local copies, waits for them, and re-layouts: 9.85 us -> 12.7 us
    ppermute x5 -> x6, waiting for transfers between devices: 19.3 us -> 6.52 us  [exchanged(): lax.ppermute(array, axis, [(i, i ^ 1) for i in range(lax.axis_size(axis))])]
    pallas_call x2 -> x4, Pallas kernels: 9.6 us -> 13.1 us  [the longest x2 9.81 us: make_fock(): pl.pallas_call(functools.partial(fock_kernel, shares), grid_spec=pltpu.Pr...]
    unnamed x26 -> x42, local copies, waits for them, and re-layouts: 6.53 us -> 9.38 us
    pallas_call x3 -> x2, Pallas kernels: 10.8 us -> 8.37 us  [make_energy(): pl.pallas_call(lambda meta_ref, *refs: energy_kernel(meta_ref, first, *re...]
    ppermute x5 -> x6, starting transfers between devices: 4.25 us -> 2.94 us  [exchanged(): lax.ppermute(array, axis, [(i, i ^ 1) for i in range(lax.axis_size(axis))])]
  transfers between devices with their start and end apart: 9 -> 10, of which waited for: 4 -> 3; matrix products, arithmetic and copies ran while one was open for 2% -> 3% of each run, Pallas kernels for 48% -> 58%
where the time goes in v3:
time: 125 us; the launch traced here: 124 us
  Pallas kernels  72.5 us (58%)
  starting transfers between devices  21.3 us (17%)
  local copies, waits for them, and re-layouts  12.7 us (10%)
  waiting for transfers between devices  12.3 us (10%)
  blocking collectives  3.9 us (3%)
    pallas_call x1, Pallas kernels, make_pure(): pl.pallas_call(pure_kernel, grid_spec=pltpu.PrefetchScalarGridSpec(num_sc...  24.3 us
    ppermute x4, starting transfers between devices, along(): lax.ppermute(array, axis, [(i, i + by) for i in range(length) if 0 <= i +...  18.4 us
    pallas_call x1, Pallas kernels, make_local(): pl.pallas_call(local_kernel, grid_spec=pltpu.PrefetchScalarGridSpec(num_s...  18.4 us
    pallas_call x2, Pallas kernels, make_fock(): pl.pallas_call(functools.partial(fock_kernel, shares), grid_spec=pltpu.Pr...  9.81 us
    unnamed x42, local copies, waits for them, and re-layouts  9.38 us
    pallas_call x2, Pallas kernels, make_energy(): pl.pallas_call(lambda meta_ref, *refs: energy_kernel(meta_ref, first, *re...  8.37 us
    ppermute x6, waiting for transfers between devices, exchanged(): lax.ppermute(array, axis, [(i, i ^ 1) for i in range(lax.axis_size(axis))])  6.52 us
    ppermute x4, waiting for transfers between devices, along(): lax.ppermute(array, axis, [(i, i + by) for i in range(length) if 0 <= i +...  5.83 us
  transfers between devices with their start and end apart: 10, of which 3 were waited for; matrix products, arithmetic and copies ran while one was open for 3% of the time, Pallas kernels for 58%

profile of v3, /device:TPU:97, one launch (start us, length us, event | category | flops | bytes accessed | tf_op | source)
XLA Modules:
  0.0 123.6 jit_solution(168611647259972362)
XLA Ops:
  0.6 0.8 collective-permute-start.1
  1.4 2.7 %slice.3 = bf16[24,128,256]{2,1,0:T(8,128)(2,1)} slice(bf16[64,128,256]{2,1,0:T(8,128)(2,1)} %part.1), slice={[0:24], [0:128], [0:256]} | slice | bytes 3145728 | tf_op jit(solution)/shard_map/slice | solution.py:425
  4.1 1.2 collective-permute-start
  5.3 3.0 %slots.1 = (s32[96]{0:T(128)}, f32[16]{0:T(128)}, bf16[64,192]{1,0:T(8,128)(2,1)}) custom-call(s32[1]{0:T(128)} %bitcast.1.own_ref, s32[16,4096]{1,0:T(8,128)} %bitcast.9, s32[16,4096]{1,0:T(8,128)} %bitcast.10, s32[16,4096]{1,0:T(8,128)} %bitcast.11, f32[16,64]{1,0:T(8,128)} %bitcast.12, f32[16,64]{1,0:T(8,128)} %bitcast.13, s32[64]{0:T(128)} %partner_ref.1), custom_call_target="tpu_custom_call" | custom-call | tf_op jit(solution)/shard_map/slots/pallas_call | solution.py:93
  8.3 0.2 collective-permute-done.1.refs_8_.refs_9_.refs_10_.refs_11_.other
  8.5 5.3 %outgoing.1 = (bf16[4,128,256]{2,1,0:T(8,128)(2,1)}, bf16[4,128,256]{2,1,0:T(8,128)(2,1)}, bf16[4,128,256]{2,1,0:T(8,128)(2,1)}, bf16[4,128,256]{2,1,0:T(8,128)(2,1)}) custom-call(s32[96]{0:T(128)} %get-tuple-element.19.meta_ref, s32[1]{0:T(128)} %bitcast.inner_ref, f32[16]{0:T(128)} %get-tuple-element.21.sent_ref, bf16[64,128,256]{2,1,0:T(8,128)(2,1)} %esp.1, ...), custom_call_target="tpu_custom_call" | custom-call | flops 65536 | bytes 4096 | tf_op jit(solution)/shard_map/outgoing/pallas_call | solution.py:135
  13.8 7.0 %collective-permute-start.5 = (bf16[4,128,256]{2,1,0:T(8,128)(2,1)}, bf16[4,128,256]{2,1,0:T(8,128)(2,1)S(1)}, u32[]{:S(2)}, u32[]{:S(2)}) collective-permute-start(bf16[4,128,256]{2,1,0:T(8,128)(2,1)} %get-tuple-element.22.after), channel_id=1, source_target_pairs={{4,0},{6,2},{8,4},{10,6},{12,8},{14,10},{16,12},{18,14},{20,16},{2... | collective-permute-start | bytes 786440 | tf_op jit(solution)/shard_map/ppermute | solution.py:415
  20.8 2.2 %collective-permute-start.2 = (bf16[4,128,256]{2,1,0:T(8,128)(2,1)}, bf16[4,128,256]{2,1,0:T(8,128)(2,1)S(1)}, u32[]{:S(2)}, u32[]{:S(2)}) collective-permute-start(bf16[4,128,256]{2,1,0:T(8,128)(2,1)} %get-tuple-element.24), channel_id=1, source_target_pairs={{0,2},{2,4},{4,6},{6,8},{8,10},{10,12},{12,14},{14,16},{16,18},{18... | collective-permute-start | bytes 786440 | tf_op jit(solution)/shard_map/ppermute | solution.py:415
  23.0 7.3 %collective-permute-start.3 = (bf16[4,128,256]{2,1,0:T(8,128)(2,1)}, bf16[4,128,256]{2,1,0:T(8,128)(2,1)S(1)}, u32[]{:S(2)}, u32[]{:S(2)}) collective-permute-start(bf16[4,128,256]{2,1,0:T(8,128)(2,1)} %get-tuple-element.25), channel_id=1, source_target_pairs={{2,0},{4,2},{6,4},{8,6},{10,8},{12,10},{14,12},{16,14},{18,16},{20... | collective-permute-start | bytes 786440 | tf_op jit(solution)/shard_map/ppermute | solution.py:415
  30.3 1.9 %collective-permute-start.4 = (bf16[4,128,256]{2,1,0:T(8,128)(2,1)}, bf16[4,128,256]{2,1,0:T(8,128)(2,1)S(1)}, u32[]{:S(2)}, u32[]{:S(2)}) collective-permute-start(bf16[4,128,256]{2,1,0:T(8,128)(2,1)} %get-tuple-element.26), channel_id=1, source_target_pairs={{0,4},{2,6},{4,8},{6,10},{8,12},{10,14},{12,16},{14,18},{16,20},{1... | collective-permute-start | bytes 786440 | tf_op jit(solution)/shard_map/ppermute | solution.py:415
  32.3 2.2 %copy-done.3 = bf16[64,128,256]{2,1,0:T(8,128)(2,1)S(1)} copy-done((bf16[64,128,256]{2,1,0:T(8,128)(2,1)S(1)}, bf16[64,128,256]{2,1,0:T(8,128)(2,1)}, u32[]{:S(2)}) %copy-start.3) | copy-done | bytes 4194328
  34.5 0.9 copy-done.13
  35.4 18.4 %local.1 = (bf16[64,128,256]{2,1,0:T(8,128)(2,1)S(1)}, f32[2,8192,128]{2,1,0:T(8,128)}, bf16[32,128,256]{2,1,0:T(8,128)(2,1)}) custom-call(s32[1]{0:T(128)} %bitcast.inner_ref, bf16[64,128,256]{2,1,0:T(8,128)(2,1)S(1)} %copy-done.1, bf16[64,128,256]{2,1,0:T(8,128)(2,1)} %collective-permute-done.1.refs_8_.refs_9_.refs_10_.refs_11_.other, ...), custom_call_target="tpu_custom_call" | custom-call | flops 65536 | bytes 4096 | tf_op jit(solution)/shard_map/local/pallas_call | solution.py:192
  53.8 2.0 %copy-done = bf16[64,128,256]{2,1,0:T(8,128)(2,1)} copy-done((bf16[64,128,256]{2,1,0:T(8,128)(2,1)}, bf16[64,128,256]{2,1,0:T(8,128)(2,1)S(1)}, u32[]{:S(2)}) %copy-start) | copy-done | bytes 4194328
  55.8 5.8 %collective-permute-done.4.refs_2_ = bf16[4,128,256]{2,1,0:T(8,128)(2,1)S(1)} collective-permute-done((bf16[4,128,256]{2,1,0:T(8,128)(2,1)}, bf16[4,128,256]{2,1,0:T(8,128)(2,1)S(1)}, u32[]{:S(2)}, u32[]{:S(2)}) %collective-permute-start.4) | collective-permute-done | bytes 262176 | tf_op jit(solution)/shard_map/ppermute | solution.py:415
  61.6 5.5 %fock_rows.3 = (bf16[24,128,256]{2,1,0:T(8,128)(2,1)}, bf16[8,128,256]{2,1,0:T(8,128)(2,1)}) custom-call(s32[96]{0:T(128)S(1)} %copy-done.18, s32[1]{0:T(128)S(6)} %sub.3.first_ref, bf16[24,128,256]{2,1,0:T(8,128)(2,1)S(1)} %collective-permute-done.began.refs_0_, f32[2,16,512,128]{3,2,1,0:T(8,128)} %bitcast.7, ...), custom_call_target="tpu_custom_call" | custom-call | flops 65536 | bytes 4096 | tf_op jit(solution)/shard_map/fock_rows/pallas_call | solution.py:255
  67.2 0.9 collective-permute-start.6
  68.0 0.1 collective-permute-start.7
  68.1 0.6 broadcast_in_dim.3.refs_1_
  68.7 4.0 %energy.2.lines = f32[64,128]{1,0:T(8,128)} custom-call(s32[96]{0:T(128)} %get-tuple-element.19.meta_ref, bf16[24,128,256]{2,1,0:T(8,128)(2,1)} %copy-done.4, f32[64,128]{1,0:T(8,128)} %broadcast_in_dim.3.refs_1_, bf16[64,128,256]{2,1,0:T(8,128)(2,1)} %copy-done, bf16[64,128,256]{2,1,0:T(8,128)(2,1)} %copy-done, bf16[64,128,256]{2,1,0:T(8,128)(2,1)} %copy-done, ...), custom_call_target="tpu_custom_call" | custom-call | flops 65536 | bytes 4096 | tf_op jit(solution)/shard_map/energy/pallas_call | solution.py:348
  72.8 0.9 copy-done.8
  73.7 0.9 copy-done.10
  74.7 0.9 copy-done.12
  75.6 4.3 %fock_rows.2.own = bf16[32,128,256]{2,1,0:T(8,128)(2,1)S(1)} custom-call(s32[96]{0:T(128)S(1)} %copy-done.19, s32[1]{0:T(128)S(6)} %mul.4.first_ref, bf16[24,128,256]{2,1,0:T(8,128)(2,1)S(1)} %copy-done.5, f32[2,16,512,128]{3,2,1,0:T(8,128)} %bitcast.8, bf16[4,128,256]{2,1,0:T(8,128)(2,1)S(1)} %copy-done.8, bf16[4,128,256]{2,1,0:T(8,128)(2,1)S(1)} %copy-done.10, ...), custom_call_target="tpu_custom_call" | custom-call | flops 65536 | bytes 4096 | tf_op jit(solution)/shard_map/fock_rows/pallas_call | solution.py:255
  80.0 24.3 %purify.1 = (bf16[32,256,256]{2,1,0:T(8,128)(2,1)}, bf16[32,256,256]{2,1,0:T(8,128)(2,1)}, bf16[8,128,256]{2,1,0:T(8,128)(2,1)}, f32[64,128]{1,0:T(8,128)S(1)}) custom-call(s32[1]{0:T(128)} %bitcast.inner_ref, bf16[32,128,256]{2,1,0:T(8,128)(2,1)S(1)} %fock_rows.2.own, bf16[24,128,256]{2,1,0:T(8,128)(2,1)S(1)} %collective-permute-done.6.low, ...), custom_call_target="tpu_custom_call" | custom-call | flops 65536 | bytes 4096 | tf_op jit(solution)/shard_map/purify/pallas_call | solution.py:311
  104.3 0.6 copy-done.17
  104.9 2.6 %picked.1.refs_2_ = bf16[8,128,256]{2,1,0:T(8,128)(2,1)} custom-call(s32[96]{0:T(128)} %get-tuple-element.19.meta_ref, bf16[64,128,256]{2,1,0:T(8,128)(2,1)} %copy-done, bf16[64,128,256]{2,1,0:T(8,128)(2,1)} %copy-done, bf16[64,128,256]{2,1,0:T(8,128)(2,1)} %copy-done, bf16[64,128,256]{2,1,0:T(8,128)(2,1)} %copy-done, bf16[64,128,256]{2,1,0:T(8,128)(2,1)} %copy-done, ...), custom_call_target="tpu_custom_call" | custom-call | flops 65536 | bytes 4096 | tf_op jit(solution)/shard_map/picked/pallas_call | solution.py:375
  107.5 4.4 %energy.3.refs_1_ = f32[64,128]{1,0:T(8,128)} custom-call(s32[96]{0:T(128)} %get-tuple-element.19.meta_ref, bf16[32,128,256]{2,1,0:T(8,128)(2,1)} %collective-permute-done.9.refs_0_, f32[64,128]{1,0:T(8,128)} %copy-done.17, bf16[64,128,256]{2,1,0:T(8,128)(2,1)} %copy-done, bf16[64,128,256]{2,1,0:T(8,128)(2,1)} %copy-done, bf16[64,128,256]{2,1,0:T(8,128)(2,1)} %copy-done, ...), custom_call_target="tpu_custom_call" | custom-call | flops 65536 | bytes 4096 | tf_op jit(solution)/shard_map/energy/pallas_call | solution.py:348
  111.9 6.3 %collective-permute-done.8.refs_0_ = bf16[8,128,256]{2,1,0:T(8,128)(2,1)S(1)} collective-permute-done((bf16[8,128,256]{2,1,0:T(8,128)(2,1)}, bf16[8,128,256]{2,1,0:T(8,128)(2,1)S(1)}, u32[]{:S(2)}, u32[]{:S(2)}) %collective-permute-start.8) | collective-permute-done | bytes 524320 | tf_op jit(solution)/shard_map/ppermute | solution.py:419
  118.2 0.8 copy-done.15
  119.0 0.7 energies.1
  119.7 3.9 %psum.7 = f32[64]{0:T(128)} all-reduce(f32[64]{0:T(128)S(1)} %bitcast.6), channel_id=1, replica_groups=mesh['frag'=64,'inner'=2] {'inner'}, use_global_device_ids=true, to_apply=%region_0.0 | all-reduce | flops 64 | bytes 512 | tf_op jit(solution)/shard_map/psum | solution.py:443
  (43 shorter events, 0.1 us)
Async XLA Ops:
  0.6 7.9 %collective-permute-start.1 = (bf16[64,128,256]{2,1,0:T(8,128)(2,1)}, bf16[64,128,256]{2,1,0:T(8,128)(2,1)}, u32[]{:S(2)}, u32[]{:S(2)}) collective-permute-start(bf16[64,128,256]{2,1,0:T(8,128)(2,1)} %part.1), channel_id=1, source_target_pairs={{0,1},{1,0},{2,3},{3,2},{4,5},{5,4},{6,7},{7,6},{8,9},{9,8},{10,11... | collective-permute-start | bytes 12582920 | tf_op jit(solution)/shard_map/ppermute | solution.py:419
  4.1 51.7 %collective-permute-start = (bf16[24,128,256]{2,1,0:T(8,128)(2,1)}, bf16[24,128,256]{2,1,0:T(8,128)(2,1)S(1)}, u32[]{:S(2)}, u32[]{:S(2)}) collective-permute-start(bf16[24,128,256]{2,1,0:T(8,128)(2,1)} %slice.3), channel_id=1, source_target_pairs={{0,2},{2,0},{4,6},{6,4},{8,10},{10,8},{12,14},{14,12},{16,18},{18,... | collective-permute-start | bytes 4718600 | tf_op jit(solution)/shard_map/ppermute | solution.py:419
  8.5 23.7 %copy-start.1 = (bf16[64,128,256]{2,1,0:T(8,128)(2,1)S(1)}, bf16[64,128,256]{2,1,0:T(8,128)(2,1)}, u32[]{:S(2)}) copy-start(bf16[64,128,256]{2,1,0:T(8,128)(2,1)} %part.1) | copy-start | bytes 12582916
  8.5 23.7 %copy-start.16 = (bf16[64,192]{1,0:T(8,128)(2,1)S(1)}, bf16[64,192]{1,0:T(8,128)(2,1)}, u32[]{:S(2)}) copy-start(bf16[64,192]{1,0:T(8,128)(2,1)} %get-tuple-element.20.weights) | copy-start | bytes 73732
  13.8 41.9 %collective-permute-start.5 = (bf16[4,128,256]{2,1,0:T(8,128)(2,1)}, bf16[4,128,256]{2,1,0:T(8,128)(2,1)S(1)}, u32[]{:S(2)}, u32[]{:S(2)}) collective-permute-start(bf16[4,128,256]{2,1,0:T(8,128)(2,1)} %get-tuple-element.22.after), channel_id=1, source_target_pairs={{4,0},{6,2},{8,4},{10,6},{12,8},{14,10},{16,12},{18,14},{20,16},{2... | collective-permute-start | bytes 786440 | tf_op jit(solution)/shard_map/ppermute | solution.py:415
  20.8 35.0 %collective-permute-start.2 = (bf16[4,128,256]{2,1,0:T(8,128)(2,1)}, bf16[4,128,256]{2,1,0:T(8,128)(2,1)S(1)}, u32[]{:S(2)}, u32[]{:S(2)}) collective-permute-start(bf16[4,128,256]{2,1,0:T(8,128)(2,1)} %get-tuple-element.24), channel_id=1, source_target_pairs={{0,2},{2,4},{4,6},{6,8},{8,10},{10,12},{12,14},{14,16},{16,18},{18... | collective-permute-start | bytes 786440 | tf_op jit(solution)/shard_map/ppermute | solution.py:415
  23.0 32.8 %collective-permute-start.3 = (bf16[4,128,256]{2,1,0:T(8,128)(2,1)}, bf16[4,128,256]{2,1,0:T(8,128)(2,1)S(1)}, u32[]{:S(2)}, u32[]{:S(2)}) collective-permute-start(bf16[4,128,256]{2,1,0:T(8,128)(2,1)} %get-tuple-element.25), channel_id=1, source_target_pairs={{2,0},{4,2},{6,4},{8,6},{10,8},{12,10},{14,12},{16,14},{18,16},{20... | collective-permute-start | bytes 786440 | tf_op jit(solution)/shard_map/ppermute | solution.py:415
  30.3 31.3 %collective-permute-start.4 = (bf16[4,128,256]{2,1,0:T(8,128)(2,1)}, bf16[4,128,256]{2,1,0:T(8,128)(2,1)S(1)}, u32[]{:S(2)}, u32[]{:S(2)}) collective-permute-start(bf16[4,128,256]{2,1,0:T(8,128)(2,1)} %get-tuple-element.26), channel_id=1, source_target_pairs={{0,4},{2,6},{4,8},{6,10},{8,12},{10,14},{12,16},{14,18},{16,20},{1... | collective-permute-start | bytes 786440 | tf_op jit(solution)/shard_map/ppermute | solution.py:415
  32.3 2.2 %copy-start.3 = (bf16[64,128,256]{2,1,0:T(8,128)(2,1)S(1)}, bf16[64,128,256]{2,1,0:T(8,128)(2,1)}, u32[]{:S(2)}) copy-start(bf16[64,128,256]{2,1,0:T(8,128)(2,1)} %esp.1) | copy-start | bytes 12582916
  34.4 0.9 copy-start.13
  35.4 26.2 %copy-start.18 = (s32[96]{0:T(128)S(1)}, s32[96]{0:T(128)}, u32[]{:S(2)}) copy-start(s32[96]{0:T(128)} %get-tuple-element.19.meta_ref) | copy-start | bytes 1156
  53.8 2.0 %copy-start = (bf16[64,128,256]{2,1,0:T(8,128)(2,1)}, bf16[64,128,256]{2,1,0:T(8,128)(2,1)S(1)}, u32[]{:S(2)}) copy-start(bf16[64,128,256]{2,1,0:T(8,128)(2,1)S(1)} %get-tuple-element.29.refs_2_.refs_3_.refs_4_.refs_5_.refs_6_.refs_7_.refs_8_.refs_9_.refs_0_.refs_1_) | copy-start | bytes 12582916
  55.8 11.4 %copy-start.4 = (bf16[24,128,256]{2,1,0:T(8,128)(2,1)}, bf16[24,128,256]{2,1,0:T(8,128)(2,1)S(1)}, u32[]{:S(2)}) copy-start(bf16[24,128,256]{2,1,0:T(8,128)(2,1)S(1)} %collective-permute-done.began.refs_0_) | copy-start | bytes 4718596
  55.8 51.7 %collective-permute-start.9 = (bf16[32,128,256]{2,1,0:T(8,128)(2,1)}, bf16[32,128,256]{2,1,0:T(8,128)(2,1)}, u32[]{:S(2)}, u32[]{:S(2)}) collective-permute-start(bf16[32,128,256]{2,1,0:T(8,128)(2,1)} %get-tuple-element.33), channel_id=1, source_target_pairs={{0,2},{2,0},{4,6},{6,4},{8,10},{10,8},{12,14},{14,12},{16,18},{18,... | collective-permute-start | bytes 6291464 | tf_op jit(solution)/shard_map/ppermute | solution.py:419
  55.8 11.3 %copy-start.7 = (bf16[4,128,256]{2,1,0:T(8,128)(2,1)}, bf16[4,128,256]{2,1,0:T(8,128)(2,1)S(1)}, u32[]{:S(2)}) copy-start(bf16[4,128,256]{2,1,0:T(8,128)(2,1)S(1)} %collective-permute-done.2.refs_0_) | copy-start | bytes 786436
  55.8 11.3 %copy-start.9 = (bf16[4,128,256]{2,1,0:T(8,128)(2,1)}, bf16[4,128,256]{2,1,0:T(8,128)(2,1)S(1)}, u32[]{:S(2)}) copy-start(bf16[4,128,256]{2,1,0:T(8,128)(2,1)S(1)} %collective-permute-done.3.refs_1_) | copy-start | bytes 786436
  61.6 5.5 %copy-start.11 = (bf16[4,128,256]{2,1,0:T(8,128)(2,1)}, bf16[4,128,256]{2,1,0:T(8,128)(2,1)S(1)}, u32[]{:S(2)}) copy-start(bf16[4,128,256]{2,1,0:T(8,128)(2,1)S(1)} %collective-permute-done.4.refs_2_) | copy-start | bytes 786436
  67.2 12.8 %collective-permute-start.6 = (bf16[24,128,256]{2,1,0:T(8,128)(2,1)}, bf16[24,128,256]{2,1,0:T(8,128)(2,1)S(1)}, u32[]{:S(2)}, u32[]{:S(2)}) collective-permute-start(bf16[24,128,256]{2,1,0:T(8,128)(2,1)} %get-tuple-element.27), channel_id=1, source_target_pairs={{0,1},{1,0},{2,3},{3,2},{4,5},{5,4},{6,7},{7,6},{8,9},{9,8},{10,11... | collective-permute-start | bytes 4718600 | tf_op jit(solution)/shard_map/ppermute | solution.py:419
  68.0 11.9 %collective-permute-start.7 = (bf16[8,128,256]{2,1,0:T(8,128)(2,1)}, bf16[8,128,256]{2,1,0:T(8,128)(2,1)}, u32[]{:S(2)}, u32[]{:S(2)}) collective-permute-start(bf16[8,128,256]{2,1,0:T(8,128)(2,1)} %get-tuple-element.28), channel_id=1, source_target_pairs={{0,1},{1,0},{2,3},{3,2},{4,5},{5,4},{6,7},{7,6},{8,9},{9,8},{10,11... | collective-permute-start | bytes 1572872 | tf_op jit(solution)/shard_map/ppermute | solution.py:419
  68.7 4.0 %copy-start.5 = (bf16[24,128,256]{2,1,0:T(8,128)(2,1)S(1)}, bf16[24,128,256]{2,1,0:T(8,128)(2,1)}, u32[]{:S(2)}) copy-start(bf16[24,128,256]{2,1,0:T(8,128)(2,1)} %copy-done.4) | copy-start | bytes 4718596
  68.7 4.0 %copy-start.19 = (s32[96]{0:T(128)S(1)}, s32[96]{0:T(128)}, u32[]{:S(2)}) copy-start(s32[96]{0:T(128)} %get-tuple-element.19.meta_ref) | copy-start | bytes 1156
  72.8 1.0 copy-start.8
  73.7 0.9 copy-start.10
  74.7 0.9 copy-start.12
  75.6 4.4 %copy-start.2 = (bf16[64,128,256]{2,1,0:T(8,128)(2,1)S(1)}, bf16[64,128,256]{2,1,0:T(8,128)(2,1)}, u32[]{:S(2)}) copy-start(bf16[64,128,256]{2,1,0:T(8,128)(2,1)} %part.1) | copy-start | bytes 12582916
  75.6 4.4 %copy-start.14 = (f32[64,128]{1,0:T(8,128)S(1)}, f32[64,128]{1,0:T(8,128)}, u32[]{:S(2)}) copy-start(f32[64,128]{1,0:T(8,128)} %energy.2.lines) | copy-start | bytes 98308
  104.3 0.6 copy-start.17
  104.9 13.3 %collective-permute-start.8 = (bf16[8,128,256]{2,1,0:T(8,128)(2,1)}, bf16[8,128,256]{2,1,0:T(8,128)(2,1)S(1)}, u32[]{:S(2)}, u32[]{:S(2)}) collective-permute-start(bf16[8,128,256]{2,1,0:T(8,128)(2,1)} %get-tuple-element.32), channel_id=1, source_target_pairs={{0,2},{2,0},{4,6},{6,4},{8,10},{10,8},{12,14},{14,12},{16,18},{18,... | collective-permute-start | bytes 1572872 | tf_op jit(solution)/shard_map/ppermute | solution.py:419
  107.5 10.7 %copy-start.6 = (bf16[8,128,256]{2,1,0:T(8,128)(2,1)S(1)}, bf16[8,128,256]{2,1,0:T(8,128)(2,1)}, u32[]{:S(2)}) copy-start(bf16[8,128,256]{2,1,0:T(8,128)(2,1)} %picked.1.refs_2_) | copy-start | bytes 1572868
  107.5 10.7 %copy-start.20 = (s32[96]{0:T(128)S(1)}, s32[96]{0:T(128)}, u32[]{:S(2)}) copy-start(s32[96]{0:T(128)} %get-tuple-element.19.meta_ref) | copy-start | bytes 1156
  118.2 0.8 copy-start.15

commit v4 on v3

--- a/solution.py
+++ b/solution.py
@@ -220,7 +220,7 @@
     )(inner, density, other, esp_kernel, coulomb_kernel, core_hamiltonian, weights, after)
 
 
-def fock_kernel(shares, meta_ref, first_ref, began, sums, *refs):
+def fock_kernel(shares, meta_ref, first_ref, lines, sums, *refs):
     arrived, outs, total = refs[: len(OFFSETS)], refs[len(OFFSETS) : -1], refs[-1]
     step = pl.program_id(0)
     count = total.shape[0]
@@ -244,7 +244,7 @@
             out[...] = total[...].astype(BF16)
 
 
-def make_fock(meta, first, sums, arrived, began, shares, count=8):
+def make_fock(meta, first, sums, arrived, lines, shares, count=8):
     def out_block(part):
         low, steps = sum(shares[:part]), shares[part]
         return pl.BlockSpec((count, 128, 256), lambda t, m, f: (jnp.clip(t - low, 0, steps - 1), 0, 0))
@@ -266,7 +266,7 @@
         compiler_params=params(48),
         cost_estimate=SMALL,
         name="fock_rows",
-    )(meta, first, began, blocked, *arrived)
+    )(meta, first, lines, blocked, *arrived)
 
 
 def pure_kernel(inner_ref, own, low, high, part, lines, fock_out, density_out, part_out, lines_out):
@@ -410,6 +410,29 @@
     )(meta, swapped, before, image)
 
 
+def taken_kernel(whole, out, done):
+    copies = []
+    for part in range(4):
+        rows = pl.ds(part * (FIRST // 4), FIRST // 4)
+        copies.append(pltpu.make_async_copy(whole.at[rows], out.at[rows], done.at[part]))
+        copies[-1].start()
+    for copy in copies:
+        copy.wait()
+
+
+def make_taken(density):
+    return pl.pallas_call(
+        taken_kernel,
+        in_specs=[ANY],
+        out_specs=pl.BlockSpec(memory_space=pltpu.VMEM),
+        out_shape=jax.ShapeDtypeStruct((FIRST, 128, 256), BF16),
+        scratch_shapes=[pltpu.SemaphoreType.DMA((4,))],
+        cost_estimate=SMALL,
+        compiler_params=params(60),
+        name="taken",
+    )(density)
+
+
 def along(array, axis, by):
     length = lax.axis_size(axis)
     return lax.ppermute(array, axis, [(i, i + by) for i in range(length) if 0 <= i + by < length])
@@ -422,7 +445,7 @@
 def body(density, core_hamiltonian, coulomb_kernel, esp_kernel, contacts, coupling, partner):
     own = lax.axis_index("frag").astype(jnp.int32).reshape(1)
     inner = lax.axis_index("inner").astype(jnp.int32).reshape(1)
-    first = exchanged(density[:FIRST], "frag")
+    first = exchanged(make_taken(density), "frag")
     other = exchanged(density, "inner")
     meta, sent, weights = make_index(own, contacts.T, coupling.T, partner)
     outgoing = make_outgoing(meta, inner, sent, esp_kernel, density, other)
@@ -431,14 +454,14 @@
         inner, density, other, esp_kernel, coulomb_kernel, core_hamiltonian, weights, outgoing[-1]
     )
     second = exchanged(part, "frag")
-    low, high = make_fock(meta, 32 - inner * 32, sums, arrived, first, SHARES)
-    (stay,) = make_fock(meta, inner * 32, sums, arrived, first, (sum(SHARES),))
+    lines = make_energy(meta, 0, first, image, jnp.zeros((64, 128), F32))
+    low, high = make_fock(meta, 32 - inner * 32, sums, arrived, lines, SHARES)
+    (stay,) = make_fock(meta, inner * 32, sums, arrived, lines, (sum(SHARES),))
     low, high = exchanged(low, "inner"), exchanged(high, "inner")
-    lines = make_energy(meta, 0, first, image, jnp.zeros((64, 128), F32))
     fock, new_density, part, lines = make_pure(inner, stay, low, high, density, lines)
     third = exchanged(part, "frag")
+    picked = make_picked(meta, FIRST + SECOND, third.shape[0], image)
     lines = make_energy(meta, FIRST, second, image, lines)
-    picked = make_picked(meta, FIRST + SECOND, third.shape[0], image)
     partial = make_last_energy(meta, FIRST + SECOND, third, picked, lines)
     energy = lax.psum(partial.reshape(64), "inner")
     return (fock, new_density, energy)

time: 125 us -> 121 us (0.968)
  local copies, waits for them, and re-layouts: 12.7 us -> 7.89 us
    ppermute x4, waiting for transfers between devices: 5.83 us -> 1.74 us  [along(): lax.ppermute(array, axis, [(i, i + by) for i in range(length) if 0 <= i +...]
    ppermute x6, waiting for transfers between devices: 6.52 us -> 9.51 us  [exchanged(): lax.ppermute(array, axis, [(i, i ^ 1) for i in range(lax.axis_size(axis))])]
    slice x1 -> x0, local copies, waits for them, and re-layouts: 2.7 us -> none  [body(): first = exchanged(density[:FIRST], 'frag')]
    pallas_call x0 -> x1, Pallas kernels: none -> 2.53 us  [make_taken(): pl.pallas_call(taken_kernel, in_specs=[ANY], out_specs=pl.BlockSpec(memor...]
    unnamed x42 -> x24, local copies, waits for them, and re-layouts: 9.38 us -> 7.28 us
    pallas_call x2, Pallas kernels: 9.81 us -> 8.46 us  [make_fock(): pl.pallas_call(functools.partial(fock_kernel, shares), grid_spec=pltpu.Pr...]
  transfers between devices with their start and end apart: 10 -> 10, of which waited for: 3 -> 4; matrix products, arithmetic and copies ran while one was open for 3% -> 1% of each run, Pallas kernels for 58% -> 60%
where the time goes in v4:
time: 121 us; the launch traced here: 119 us
  Pallas kernels  72 us (60%)
  starting transfers between devices  21.9 us (18%)
  waiting for transfers between devices  11.2 us (9%)
  local copies, waits for them, and re-layouts  7.89 us (7%)
  blocking collectives  4.76 us (4%)
    pallas_call x1, Pallas kernels, make_pure(): pl.pallas_call(pure_kernel, grid_spec=pltpu.PrefetchScalarGridSpec(num_sc...  23.3 us
    ppermute x4, starting transfers between devices, along(): lax.ppermute(array, axis, [(i, i + by) for i in range(length) if 0 <= i +...  18.4 us
    pallas_call x1, Pallas kernels, make_local(): pl.pallas_call(local_kernel, grid_spec=pltpu.PrefetchScalarGridSpec(num_s...  17.7 us
    ppermute x6, waiting for transfers between devices, exchanged(): lax.ppermute(array, axis, [(i, i ^ 1) for i in range(lax.axis_size(axis))])  9.51 us
    pallas_call x2, Pallas kernels, make_fock(): pl.pallas_call(functools.partial(fock_kernel, shares), grid_spec=pltpu.Pr...  8.46 us
    pallas_call x2, Pallas kernels, make_energy(): pl.pallas_call(lambda meta_ref, *refs: energy_kernel(meta_ref, first, *re...  8.36 us
    unnamed x24, local copies, waits for them, and re-layouts  7.28 us
    pallas_call x1, Pallas kernels, make_outgoing(): pl.pallas_call(outgoing_kernel, grid_spec=pltpu.PrefetchScalarGridSpec(nu...  5.35 us
  transfers between devices with their start and end apart: 10, of which 4 were waited for; matrix products, arithmetic and copies ran while one was open for 1% of the time, Pallas kernels for 60%

profile of v4, /device:TPU:97, one launch (start us, length us, event | category | flops | bytes accessed | tf_op | source)
XLA Modules:
  0.0 118.5 jit_solution(16567505591769302596)
XLA Ops:
  0.6 0.8 collective-permute-start.1
  1.4 2.5 %taken.1 = bf16[24,128,256]{2,1,0:T(8,128)(2,1)} custom-call(bf16[64,128,256]{2,1,0:T(8,128)(2,1)} %part.1), custom_call_target="tpu_custom_call" | custom-call | flops 65536 | bytes 4096 | tf_op jit(solution)/shard_map/taken/pallas_call | solution.py:424
  3.9 1.3 %collective-permute-start = (bf16[24,128,256]{2,1,0:T(8,128)(2,1)}, bf16[24,128,256]{2,1,0:T(8,128)(2,1)}, u32[]{:S(2)}, u32[]{:S(2)}) collective-permute-start(bf16[24,128,256]{2,1,0:T(8,128)(2,1)} %taken.1), channel_id=1, source_target_pairs={{0,2},{2,0},{4,6},{6,4},{8,10},{10,8},{12,14},{14,12},{16,18},{18,... | collective-permute-start | bytes 4718600 | tf_op jit(solution)/shard_map/ppermute | solution.py:442
  5.2 3.0 %slots.1 = (s32[96]{0:T(128)}, f32[16]{0:T(128)}, bf16[64,192]{1,0:T(8,128)(2,1)}) custom-call(s32[1]{0:T(128)} %bitcast.1.own_ref, s32[16,4096]{1,0:T(8,128)} %bitcast.9, s32[16,4096]{1,0:T(8,128)} %bitcast.10, s32[16,4096]{1,0:T(8,128)} %bitcast.11, f32[16,64]{1,0:T(8,128)} %bitcast.12, f32[16,64]{1,0:T(8,128)} %bitcast.13, s32[64]{0:T(128)} %partner_ref.1), custom_call_target="tpu_custom_call" | custom-call | tf_op jit(solution)/shard_map/slots/pallas_call | solution.py:93
  8.3 0.2 collective-permute-done.1.refs_8_.refs_9_.refs_10_.refs_11_.other
  8.5 5.3 %outgoing.1 = (bf16[4,128,256]{2,1,0:T(8,128)(2,1)}, bf16[4,128,256]{2,1,0:T(8,128)(2,1)}, bf16[4,128,256]{2,1,0:T(8,128)(2,1)}, bf16[4,128,256]{2,1,0:T(8,128)(2,1)}) custom-call(s32[96]{0:T(128)} %get-tuple-element.19.meta_ref, s32[1]{0:T(128)} %bitcast.inner_ref, f32[16]{0:T(128)} %get-tuple-element.21.sent_ref, bf16[64,128,256]{2,1,0:T(8,128)(2,1)} %esp.1, ...), custom_call_target="tpu_custom_call" | custom-call | flops 65536 | bytes 4096 | tf_op jit(solution)/shard_map/outgoing/pallas_call | solution.py:135
  13.9 7.0 %collective-permute-start.5 = (bf16[4,128,256]{2,1,0:T(8,128)(2,1)}, bf16[4,128,256]{2,1,0:T(8,128)(2,1)S(1)}, u32[]{:S(2)}, u32[]{:S(2)}) collective-permute-start(bf16[4,128,256]{2,1,0:T(8,128)(2,1)} %get-tuple-element.22.after), channel_id=1, source_target_pairs={{4,0},{6,2},{8,4},{10,6},{12,8},{14,10},{16,12},{18,14},{20,16},{2... | collective-permute-start | bytes 786440 | tf_op jit(solution)/shard_map/ppermute | solution.py:438
  20.9 2.2 %collective-permute-start.2 = (bf16[4,128,256]{2,1,0:T(8,128)(2,1)}, bf16[4,128,256]{2,1,0:T(8,128)(2,1)S(1)}, u32[]{:S(2)}, u32[]{:S(2)}) collective-permute-start(bf16[4,128,256]{2,1,0:T(8,128)(2,1)} %get-tuple-element.25), channel_id=1, source_target_pairs={{0,2},{2,4},{4,6},{6,8},{8,10},{10,12},{12,14},{14,16},{16,18},{18... | collective-permute-start | bytes 786440 | tf_op jit(solution)/shard_map/ppermute | solution.py:438
  23.0 7.3 %collective-permute-start.3 = (bf16[4,128,256]{2,1,0:T(8,128)(2,1)}, bf16[4,128,256]{2,1,0:T(8,128)(2,1)S(1)}, u32[]{:S(2)}, u32[]{:S(2)}) collective-permute-start(bf16[4,128,256]{2,1,0:T(8,128)(2,1)} %get-tuple-element.26), channel_id=1, source_target_pairs={{2,0},{4,2},{6,4},{8,6},{10,8},{12,10},{14,12},{16,14},{18,16},{20... | collective-permute-start | bytes 786440 | tf_op jit(solution)/shard_map/ppermute | solution.py:438
  30.4 1.9 %collective-permute-start.4 = (bf16[4,128,256]{2,1,0:T(8,128)(2,1)}, bf16[4,128,256]{2,1,0:T(8,128)(2,1)S(1)}, u32[]{:S(2)}, u32[]{:S(2)}) collective-permute-start(bf16[4,128,256]{2,1,0:T(8,128)(2,1)} %get-tuple-element.27), channel_id=1, source_target_pairs={{0,4},{2,6},{4,8},{6,10},{8,12},{10,14},{12,16},{14,18},{16,20},{1... | collective-permute-start | bytes 786440 | tf_op jit(solution)/shard_map/ppermute | solution.py:438
  32.4 2.2 %copy-done.3 = bf16[64,128,256]{2,1,0:T(8,128)(2,1)S(1)} copy-done((bf16[64,128,256]{2,1,0:T(8,128)(2,1)S(1)}, bf16[64,128,256]{2,1,0:T(8,128)(2,1)}, u32[]{:S(2)}) %copy-start.3) | copy-done | bytes 4194328
  34.5 0.9 copy-done.6
  35.5 17.7 %local.1 = (bf16[64,128,256]{2,1,0:T(8,128)(2,1)S(1)}, f32[2,8192,128]{2,1,0:T(8,128)}, bf16[32,128,256]{2,1,0:T(8,128)(2,1)S(1)}) custom-call(s32[1]{0:T(128)} %bitcast.inner_ref, bf16[64,128,256]{2,1,0:T(8,128)(2,1)S(1)} %copy-done.1, bf16[64,128,256]{2,1,0:T(8,128)(2,1)} %collective-permute-done.1.refs_8_.refs_9_.refs_10_.refs_11_.other, ...), custom_call_target="tpu_custom_call" | custom-call | flops 65536 | bytes 4096 | tf_op jit(solution)/shard_map/local/pallas_call | solution.py:192
  53.2 2.0 %copy-done = bf16[64,128,256]{2,1,0:T(8,128)(2,1)} copy-done((bf16[64,128,256]{2,1,0:T(8,128)(2,1)}, bf16[64,128,256]{2,1,0:T(8,128)(2,1)S(1)}, u32[]{:S(2)}) %copy-start) | copy-done | bytes 4194328
  55.2 0.6 broadcast_in_dim.3.refs_1_
  55.8 4.0 %energy.2.lines = f32[64,128]{1,0:T(8,128)} custom-call(s32[96]{0:T(128)} %get-tuple-element.19.meta_ref, bf16[24,128,256]{2,1,0:T(8,128)(2,1)} %collective-permute-done.refs_0_, f32[64,128]{1,0:T(8,128)} %broadcast_in_dim.3.refs_1_, bf16[64,128,256]{2,1,0:T(8,128)(2,1)} %copy-done, bf16[64,128,256]{2,1,0:T(8,128)(2,1)} %copy-done, ...), custom_call_target="tpu_custom_call" | custom-call | flops 65536 | bytes 4096 | tf_op jit(solution)/shard_map/energy/pallas_call | solution.py:348
  59.8 1.7 %collective-permute-done.4.refs_2_ = bf16[4,128,256]{2,1,0:T(8,128)(2,1)S(1)} collective-permute-done((bf16[4,128,256]{2,1,0:T(8,128)(2,1)}, bf16[4,128,256]{2,1,0:T(8,128)(2,1)S(1)}, u32[]{:S(2)}, u32[]{:S(2)}) %collective-permute-start.4) | collective-permute-done | bytes 262176 | tf_op jit(solution)/shard_map/ppermute | solution.py:438
  61.6 0.8 copy-done.5
  62.3 4.1 %fock_rows.3 = (bf16[24,128,256]{2,1,0:T(8,128)(2,1)S(1)}, bf16[8,128,256]{2,1,0:T(8,128)(2,1)S(1)}) custom-call(s32[96]{0:T(128)S(1)} %copy-done.10, s32[1]{0:T(128)S(6)} %sub.3.first_ref, f32[64,128]{1,0:T(8,128)S(1)} %copy-done.5, f32[2,16,512,128]{3,2,1,0:T(8,128)} %bitcast.7, bf16[4,128,256]{2,1,0:T(8,128)(2,1)S(1)} %collective-permute-done.2.refs_0_, ...), custom_call_target="tpu_custom_call" | custom-call | flops 65536 | bytes 4096 | tf_op jit(solution)/shard_map/fock_rows/pallas_call | solution.py:255
  66.4 0.9 collective-permute-start.6
  67.3 0.1 collective-permute-start.7
  67.4 4.4 %fock_rows.2.own = bf16[32,128,256]{2,1,0:T(8,128)(2,1)S(1)} custom-call(s32[96]{0:T(128)S(1)} %copy-done.10, s32[1]{0:T(128)S(6)} %mul.4.first_ref, f32[64,128]{1,0:T(8,128)S(1)} %copy-done.5, f32[2,16,512,128]{3,2,1,0:T(8,128)} %bitcast.8, bf16[4,128,256]{2,1,0:T(8,128)(2,1)S(1)} %collective-permute-done.2.refs_0_, ...), custom_call_target="tpu_custom_call" | custom-call | flops 65536 | bytes 4096 | tf_op jit(solution)/shard_map/fock_rows/pallas_call | solution.py:255
  71.8 23.3 %purify.1 = (bf16[32,256,256]{2,1,0:T(8,128)(2,1)}, bf16[32,256,256]{2,1,0:T(8,128)(2,1)}, bf16[8,128,256]{2,1,0:T(8,128)(2,1)}, f32[64,128]{1,0:T(8,128)S(1)}) custom-call(s32[1]{0:T(128)} %bitcast.inner_ref, bf16[32,128,256]{2,1,0:T(8,128)(2,1)S(1)} %fock_rows.2.own, bf16[24,128,256]{2,1,0:T(8,128)(2,1)S(1)} %collective-permute-done.6.low, ...), custom_call_target="tpu_custom_call" | custom-call | flops 65536 | bytes 4096 | tf_op jit(solution)/shard_map/purify/pallas_call | solution.py:311
  95.1 0.6 copy-done.9
  95.7 0.4 collective-permute-start.8
  96.1 2.6 %picked.1.refs_2_ = bf16[8,128,256]{2,1,0:T(8,128)(2,1)} custom-call(s32[96]{0:T(128)} %get-tuple-element.19.meta_ref, bf16[64,128,256]{2,1,0:T(8,128)(2,1)} %copy-done, bf16[64,128,256]{2,1,0:T(8,128)(2,1)} %copy-done, bf16[64,128,256]{2,1,0:T(8,128)(2,1)} %copy-done, bf16[64,128,256]{2,1,0:T(8,128)(2,1)} %copy-done, bf16[64,128,256]{2,1,0:T(8,128)(2,1)} %copy-done, ...), custom_call_target="tpu_custom_call" | custom-call | flops 65536 | bytes 4096 | tf_op jit(solution)/shard_map/picked/pallas_call | solution.py:375
  98.7 2.5 %collective-permute-done.9.refs_0_ = bf16[32,128,256]{2,1,0:T(8,128)(2,1)} collective-permute-done((bf16[32,128,256]{2,1,0:T(8,128)(2,1)S(1)}, bf16[32,128,256]{2,1,0:T(8,128)(2,1)}, u32[]{:S(2)}, u32[]{:S(2)}) %collective-permute-start.9) | collective-permute-done | bytes 2097184 | tf_op jit(solution)/shard_map/ppermute | solution.py:442
  101.2 4.3 %energy.3.refs_1_ = f32[64,128]{1,0:T(8,128)} custom-call(s32[96]{0:T(128)} %get-tuple-element.19.meta_ref, bf16[32,128,256]{2,1,0:T(8,128)(2,1)} %collective-permute-done.9.refs_0_, f32[64,128]{1,0:T(8,128)} %copy-done.9, bf16[64,128,256]{2,1,0:T(8,128)(2,1)} %copy-done, bf16[64,128,256]{2,1,0:T(8,128)(2,1)} %copy-done, bf16[64,128,256]{2,1,0:T(8,128)(2,1)} %copy-done, ...), custom_call_target="tpu_custom_call" | custom-call | flops 65536 | bytes 4096 | tf_op jit(solution)/shard_map/energy/pallas_call | solution.py:348
  105.5 6.8 %collective-permute-done.8.refs_0_ = bf16[8,128,256]{2,1,0:T(8,128)(2,1)S(1)} collective-permute-done((bf16[8,128,256]{2,1,0:T(8,128)(2,1)}, bf16[8,128,256]{2,1,0:T(8,128)(2,1)S(1)}, u32[]{:S(2)}, u32[]{:S(2)}) %collective-permute-start.8) | collective-permute-done | bytes 524320 | tf_op jit(solution)/shard_map/ppermute | solution.py:442
  112.3 0.8 copy-done.7
  113.1 0.7 energies.1
  113.8 4.8 %psum.7 = f32[64]{0:T(128)} all-reduce(f32[64]{0:T(128)S(1)} %bitcast.6), channel_id=1, replica_groups=mesh['frag'=64,'inner'=2] {'inner'}, use_global_device_ids=true, to_apply=%region_0.0 | all-reduce | flops 64 | bytes 512 | tf_op jit(solution)/shard_map/psum | solution.py:466
  (25 shorter events, 0.1 us)
Async XLA Ops:
  0.6 7.9 %collective-permute-start.1 = (bf16[64,128,256]{2,1,0:T(8,128)(2,1)}, bf16[64,128,256]{2,1,0:T(8,128)(2,1)}, u32[]{:S(2)}, u32[]{:S(2)}) collective-permute-start(bf16[64,128,256]{2,1,0:T(8,128)(2,1)} %part.1), channel_id=1, source_target_pairs={{0,1},{1,0},{2,3},{3,2},{4,5},{5,4},{6,7},{7,6},{8,9},{9,8},{10,11... | collective-permute-start | bytes 12582920 | tf_op jit(solution)/shard_map/ppermute | solution.py:442
  3.9 51.2 %collective-permute-start = (bf16[24,128,256]{2,1,0:T(8,128)(2,1)}, bf16[24,128,256]{2,1,0:T(8,128)(2,1)}, u32[]{:S(2)}, u32[]{:S(2)}) collective-permute-start(bf16[24,128,256]{2,1,0:T(8,128)(2,1)} %taken.1), channel_id=1, source_target_pairs={{0,2},{2,0},{4,6},{6,4},{8,10},{10,8},{12,14},{14,12},{16,18},{18,... | collective-permute-start | bytes 4718600 | tf_op jit(solution)/shard_map/ppermute | solution.py:442
  8.5 23.8 %copy-start.1 = (bf16[64,128,256]{2,1,0:T(8,128)(2,1)S(1)}, bf16[64,128,256]{2,1,0:T(8,128)(2,1)}, u32[]{:S(2)}) copy-start(bf16[64,128,256]{2,1,0:T(8,128)(2,1)} %part.1) | copy-start | bytes 12582916
  8.5 23.8 %copy-start.8 = (bf16[64,192]{1,0:T(8,128)(2,1)S(1)}, bf16[64,192]{1,0:T(8,128)(2,1)}, u32[]{:S(2)}) copy-start(bf16[64,192]{1,0:T(8,128)(2,1)} %get-tuple-element.20.weights) | copy-start | bytes 73732
  13.9 45.9 %collective-permute-start.5 = (bf16[4,128,256]{2,1,0:T(8,128)(2,1)}, bf16[4,128,256]{2,1,0:T(8,128)(2,1)S(1)}, u32[]{:S(2)}, u32[]{:S(2)}) collective-permute-start(bf16[4,128,256]{2,1,0:T(8,128)(2,1)} %get-tuple-element.22.after), channel_id=1, source_target_pairs={{4,0},{6,2},{8,4},{10,6},{12,8},{14,10},{16,12},{18,14},{20,16},{2... | collective-permute-start | bytes 786440 | tf_op jit(solution)/shard_map/ppermute | solution.py:438
  20.9 38.9 %collective-permute-start.2 = (bf16[4,128,256]{2,1,0:T(8,128)(2,1)}, bf16[4,128,256]{2,1,0:T(8,128)(2,1)S(1)}, u32[]{:S(2)}, u32[]{:S(2)}) collective-permute-start(bf16[4,128,256]{2,1,0:T(8,128)(2,1)} %get-tuple-element.25), channel_id=1, source_target_pairs={{0,2},{2,4},{4,6},{6,8},{8,10},{10,12},{12,14},{14,16},{16,18},{18... | collective-permute-start | bytes 786440 | tf_op jit(solution)/shard_map/ppermute | solution.py:438
  23.0 36.8 %collective-permute-start.3 = (bf16[4,128,256]{2,1,0:T(8,128)(2,1)}, bf16[4,128,256]{2,1,0:T(8,128)(2,1)S(1)}, u32[]{:S(2)}, u32[]{:S(2)}) collective-permute-start(bf16[4,128,256]{2,1,0:T(8,128)(2,1)} %get-tuple-element.26), channel_id=1, source_target_pairs={{2,0},{4,2},{6,4},{8,6},{10,8},{12,10},{14,12},{16,14},{18,16},{20... | collective-permute-start | bytes 786440 | tf_op jit(solution)/shard_map/ppermute | solution.py:438
  30.4 31.2 %collective-permute-start.4 = (bf16[4,128,256]{2,1,0:T(8,128)(2,1)}, bf16[4,128,256]{2,1,0:T(8,128)(2,1)S(1)}, u32[]{:S(2)}, u32[]{:S(2)}) collective-permute-start(bf16[4,128,256]{2,1,0:T(8,128)(2,1)} %get-tuple-element.27), channel_id=1, source_target_pairs={{0,4},{2,6},{4,8},{6,10},{8,12},{10,14},{12,16},{14,18},{16,20},{1... | collective-permute-start | bytes 786440 | tf_op jit(solution)/shard_map/ppermute | solution.py:438
  32.3 2.2 %copy-start.3 = (bf16[64,128,256]{2,1,0:T(8,128)(2,1)S(1)}, bf16[64,128,256]{2,1,0:T(8,128)(2,1)}, u32[]{:S(2)}) copy-start(bf16[64,128,256]{2,1,0:T(8,128)(2,1)} %esp.1) | copy-start | bytes 12582916
  34.5 0.9 copy-start.6
  53.2 2.0 %copy-start = (bf16[64,128,256]{2,1,0:T(8,128)(2,1)}, bf16[64,128,256]{2,1,0:T(8,128)(2,1)S(1)}, u32[]{:S(2)}) copy-start(bf16[64,128,256]{2,1,0:T(8,128)(2,1)S(1)} %get-tuple-element.23.refs_2_.refs_3_.refs_4_.refs_5_.refs_6_.refs_7_.refs_8_.refs_9_.refs_0_.refs_1_) | copy-start | bytes 12582916
  55.2 46.0 %collective-permute-start.9 = (bf16[32,128,256]{2,1,0:T(8,128)(2,1)S(1)}, bf16[32,128,256]{2,1,0:T(8,128)(2,1)}, u32[]{:S(2)}, u32[]{:S(2)}) collective-permute-start(bf16[32,128,256]{2,1,0:T(8,128)(2,1)S(1)} %get-tuple-element.33), channel_id=1, source_target_pairs={{0,2},{2,0},{4,6},{6,4},{8,10},{10,8},{12,14},{14,12},{16,18},{18,... | collective-permute-start | bytes 6291464 | tf_op jit(solution)/shard_map/ppermute | solution.py:442
  55.8 5.8 %copy-start.10 = (s32[96]{0:T(128)S(1)}, s32[96]{0:T(128)}, u32[]{:S(2)}) copy-start(s32[96]{0:T(128)} %get-tuple-element.19.meta_ref) | copy-start | bytes 1156
  61.6 0.8 copy-start.5
  66.4 5.4 %collective-permute-start.6 = (bf16[24,128,256]{2,1,0:T(8,128)(2,1)S(1)}, bf16[24,128,256]{2,1,0:T(8,128)(2,1)S(1)}, u32[]{:S(2)}, u32[]{:S(2)}) collective-permute-start(bf16[24,128,256]{2,1,0:T(8,128)(2,1)S(1)} %get-tuple-element.28), channel_id=1, source_target_pairs={{0,1},{1,0},{2,3},{3,2},{4,5},{5,4},{6,7},{7,6},{8,9},{9,8},{10,11... | collective-permute-start | bytes 4718600 | tf_op jit(solution)/shard_map/ppermute | solution.py:442
  67.3 4.5 %copy-start.2 = (bf16[64,128,256]{2,1,0:T(8,128)(2,1)S(1)}, bf16[64,128,256]{2,1,0:T(8,128)(2,1)}, u32[]{:S(2)}) copy-start(bf16[64,128,256]{2,1,0:T(8,128)(2,1)} %part.1) | copy-start | bytes 12582916
  67.3 4.5 %collective-permute-start.7 = (bf16[8,128,256]{2,1,0:T(8,128)(2,1)S(1)}, bf16[8,128,256]{2,1,0:T(8,128)(2,1)S(1)}, u32[]{:S(2)}, u32[]{:S(2)}) collective-permute-start(bf16[8,128,256]{2,1,0:T(8,128)(2,1)S(1)} %get-tuple-element.29), channel_id=1, source_target_pairs={{0,1},{1,0},{2,3},{3,2},{4,5},{5,4},{6,7},{7,6},{8,9},{9,8},{10,11... | collective-permute-start | bytes 1572872 | tf_op jit(solution)/shard_map/ppermute | solution.py:442
  95.1 0.6 copy-start.9
  95.7 16.6 %collective-permute-start.8 = (bf16[8,128,256]{2,1,0:T(8,128)(2,1)}, bf16[8,128,256]{2,1,0:T(8,128)(2,1)S(1)}, u32[]{:S(2)}, u32[]{:S(2)}) collective-permute-start(bf16[8,128,256]{2,1,0:T(8,128)(2,1)} %get-tuple-element.32), channel_id=1, source_target_pairs={{0,2},{2,0},{4,6},{6,4},{8,10},{10,8},{12,14},{14,12},{16,18},{18,... | collective-permute-start | bytes 1572872 | tf_op jit(solution)/shard_map/ppermute | solution.py:442
  101.2 11.1 %copy-start.4 = (bf16[8,128,256]{2,1,0:T(8,128)(2,1)S(1)}, bf16[8,128,256]{2,1,0:T(8,128)(2,1)}, u32[]{:S(2)}) copy-start(bf16[8,128,256]{2,1,0:T(8,128)(2,1)} %picked.1.refs_2_) | copy-start | bytes 1572868
  101.2 11.1 %copy-start.11 = (s32[96]{0:T(128)S(1)}, s32[96]{0:T(128)}, u32[]{:S(2)}) copy-start(s32[96]{0:T(128)} %get-tuple-element.19.meta_ref) | copy-start | bytes 1156
  112.3 0.8 copy-start.7

commit v5 on v4

--- a/solution.py
+++ b/solution.py
@@ -359,6 +359,7 @@
         ),
         out_shape=jax.ShapeDtypeStruct((64, 128), F32),
         cost_estimate=SMALL,
+        compiler_params=params(20),
         name="energy",
     )(meta, swapped, before, *[image] * ENERGY_STEP)
 
@@ -463,7 +464,7 @@
     picked = make_picked(meta, FIRST + SECOND, third.shape[0], image)
     lines = make_energy(meta, FIRST, second, image, lines)
     partial = make_last_energy(meta, FIRST + SECOND, third, picked, lines)
-    energy = lax.psum(partial.reshape(64), "inner")
+    energy = (partial + exchanged(partial, "inner")).reshape(64)
     return (fock, new_density, energy)
 
 

time: 121 us -> 118 us (0.975)
  Pallas kernels: 72 us -> 65.6 us
  waiting for transfers between devices: 11.2 us -> 17.3 us
  blocking collectives: 4.76 us -> 0 us
  starting transfers between devices: 21.9 us -> 23.6 us
    pallas_call x2, Pallas kernels: 8.36 us -> 1.71 us  [make_energy(): pl.pallas_call(lambda meta_ref, *refs: energy_kernel(meta_ref, first, *re...]
    psum x1 -> x0, blocking collectives: 4.76 us -> none  [body(): energy = lax.psum(partial.reshape(64), 'inner')]
    ppermute x6 -> x7, waiting for transfers between devices: 9.51 us -> 13.5 us  [exchanged(): lax.ppermute(array, axis, [(i, i ^ 1) for i in range(lax.axis_size(axis))])]
    ppermute x4, waiting for transfers between devices: 1.74 us -> 3.7 us  [along(): lax.ppermute(array, axis, [(i, i + by) for i in range(length) if 0 <= i +...]
    ppermute x6 -> x7, starting transfers between devices: 3.45 us -> 5.27 us  [exchanged(): lax.ppermute(array, axis, [(i, i ^ 1) for i in range(lax.axis_size(axis))])]
    unnamed x24 -> x22, local copies, waits for them, and re-layouts: 7.28 us -> 8.65 us
  transfers between devices with their start and end apart: 10 -> 11, of which waited for: 4 -> 5; matrix products, arithmetic and copies ran while one was open for 1% -> 0% of each run, Pallas kernels for 60% -> 56%
where the time goes in v5:
time: 118 us; the launch traced here: 116 us
  Pallas kernels  65.6 us (56%)
  starting transfers between devices  23.6 us (20%)
  waiting for transfers between devices  17.3 us (15%)
  local copies, waits for them, and re-layouts  8.66 us (7%)
    pallas_call x1, Pallas kernels, make_pure(): pl.pallas_call(pure_kernel, grid_spec=pltpu.PrefetchScalarGridSpec(num_sc...  23.3 us
    ppermute x4, starting transfers between devices, along(): lax.ppermute(array, axis, [(i, i + by) for i in range(length) if 0 <= i +...  18.4 us
    pallas_call x1, Pallas kernels, make_local(): pl.pallas_call(local_kernel, grid_spec=pltpu.PrefetchScalarGridSpec(num_s...  18.2 us
    ppermute x7, waiting for transfers between devices, exchanged(): lax.ppermute(array, axis, [(i, i ^ 1) for i in range(lax.axis_size(axis))])  13.5 us
    unnamed x22, local copies, waits for them, and re-layouts  8.65 us
    pallas_call x2, Pallas kernels, make_fock(): pl.pallas_call(functools.partial(fock_kernel, shares), grid_spec=pltpu.Pr...  8.12 us
    pallas_call x1, Pallas kernels, make_outgoing(): pl.pallas_call(outgoing_kernel, grid_spec=pltpu.PrefetchScalarGridSpec(nu...  5.32 us
    ppermute x7, starting transfers between devices, exchanged(): lax.ppermute(array, axis, [(i, i ^ 1) for i in range(lax.axis_size(axis))])  5.27 us
  transfers between devices with their start and end apart: 11, of which 5 were waited for; matrix products, arithmetic and copies ran while one was open for 0% of the time, Pallas kernels for 56%

profile of v5, /device:TPU:97, one launch (start us, length us, event | category | flops | bytes accessed | tf_op | source)
XLA Modules:
  0.0 116.4 jit_solution(7371877800686737127)
XLA Ops:
  0.6 0.8 collective-permute-start.1
  1.4 2.5 %taken.1 = bf16[24,128,256]{2,1,0:T(8,128)(2,1)} custom-call(bf16[64,128,256]{2,1,0:T(8,128)(2,1)} %part.1), custom_call_target="tpu_custom_call" | custom-call | flops 65536 | bytes 4096 | tf_op jit(solution)/shard_map/taken/pallas_call | solution.py:425
  3.9 1.3 %collective-permute-start = (bf16[24,128,256]{2,1,0:T(8,128)(2,1)}, bf16[24,128,256]{2,1,0:T(8,128)(2,1)S(1)}, u32[]{:S(2)}, u32[]{:S(2)}) collective-permute-start(bf16[24,128,256]{2,1,0:T(8,128)(2,1)} %taken.1), channel_id=1, source_target_pairs={{0,2},{2,0},{4,6},{6,4},{8,10},{10,8},{12,14},{14,12},{16,18},{18,... | collective-permute-start | bytes 4718600 | tf_op jit(solution)/shard_map/ppermute | solution.py:443
  5.2 3.0 %slots.1 = (s32[96]{0:T(128)}, f32[16]{0:T(128)}, bf16[64,192]{1,0:T(8,128)(2,1)}) custom-call(s32[1]{0:T(128)} %bitcast.1.own_ref, s32[16,4096]{1,0:T(8,128)} %bitcast.9, s32[16,4096]{1,0:T(8,128)} %bitcast.10, s32[16,4096]{1,0:T(8,128)} %bitcast.11, f32[16,64]{1,0:T(8,128)} %bitcast.12, f32[16,64]{1,0:T(8,128)} %bitcast.13, s32[64]{0:T(128)} %partner_ref.1), custom_call_target="tpu_custom_call" | custom-call | tf_op jit(solution)/shard_map/slots/pallas_call | solution.py:93
  8.3 0.3 collective-permute-done.1.refs_8_.refs_9_.refs_10_.refs_11_.other
  8.5 5.3 %outgoing.1 = (bf16[4,128,256]{2,1,0:T(8,128)(2,1)}, bf16[4,128,256]{2,1,0:T(8,128)(2,1)}, bf16[4,128,256]{2,1,0:T(8,128)(2,1)}, bf16[4,128,256]{2,1,0:T(8,128)(2,1)}) custom-call(s32[96]{0:T(128)} %get-tuple-element.19.meta_ref, s32[1]{0:T(128)} %bitcast.inner_ref, f32[16]{0:T(128)} %get-tuple-element.21.sent_ref, bf16[64,128,256]{2,1,0:T(8,128)(2,1)} %esp.1, ...), custom_call_target="tpu_custom_call" | custom-call | flops 65536 | bytes 4096 | tf_op jit(solution)/shard_map/outgoing/pallas_call | solution.py:135
  13.8 6.9 %collective-permute-start.5 = (bf16[4,128,256]{2,1,0:T(8,128)(2,1)}, bf16[4,128,256]{2,1,0:T(8,128)(2,1)S(1)}, u32[]{:S(2)}, u32[]{:S(2)}) collective-permute-start(bf16[4,128,256]{2,1,0:T(8,128)(2,1)} %get-tuple-element.22.after), channel_id=1, source_target_pairs={{4,0},{6,2},{8,4},{10,6},{12,8},{14,10},{16,12},{18,14},{20,16},{2... | collective-permute-start | bytes 786440 | tf_op jit(solution)/shard_map/ppermute | solution.py:439
  20.8 2.3 %collective-permute-start.2 = (bf16[4,128,256]{2,1,0:T(8,128)(2,1)}, bf16[4,128,256]{2,1,0:T(8,128)(2,1)S(1)}, u32[]{:S(2)}, u32[]{:S(2)}) collective-permute-start(bf16[4,128,256]{2,1,0:T(8,128)(2,1)} %get-tuple-element.25), channel_id=1, source_target_pairs={{0,2},{2,4},{4,6},{6,8},{8,10},{10,12},{12,14},{14,16},{16,18},{18... | collective-permute-start | bytes 786440 | tf_op jit(solution)/shard_map/ppermute | solution.py:439
  23.1 7.2 %collective-permute-start.3 = (bf16[4,128,256]{2,1,0:T(8,128)(2,1)}, bf16[4,128,256]{2,1,0:T(8,128)(2,1)S(1)}, u32[]{:S(2)}, u32[]{:S(2)}) collective-permute-start(bf16[4,128,256]{2,1,0:T(8,128)(2,1)} %get-tuple-element.26), channel_id=1, source_target_pairs={{2,0},{4,2},{6,4},{8,6},{10,8},{12,10},{14,12},{16,14},{18,16},{20... | collective-permute-start | bytes 786440 | tf_op jit(solution)/shard_map/ppermute | solution.py:439
  30.3 1.9 %collective-permute-start.4 = (bf16[4,128,256]{2,1,0:T(8,128)(2,1)}, bf16[4,128,256]{2,1,0:T(8,128)(2,1)S(1)}, u32[]{:S(2)}, u32[]{:S(2)}) collective-permute-start(bf16[4,128,256]{2,1,0:T(8,128)(2,1)} %get-tuple-element.27), channel_id=1, source_target_pairs={{0,4},{2,6},{4,8},{6,10},{8,12},{10,14},{12,16},{14,18},{16,20},{1... | collective-permute-start | bytes 786440 | tf_op jit(solution)/shard_map/ppermute | solution.py:439
  32.3 0.0 copy-start.3
  32.3 2.2 %copy-done.3 = bf16[64,128,256]{2,1,0:T(8,128)(2,1)S(1)} copy-done((bf16[64,128,256]{2,1,0:T(8,128)(2,1)S(1)}, bf16[64,128,256]{2,1,0:T(8,128)(2,1)}, u32[]{:S(2)}) %copy-start.3) | copy-done | bytes 4194328
  34.5 0.9 copy-done.7
  35.4 18.2 %local.1 = (bf16[64,128,256]{2,1,0:T(8,128)(2,1)S(1)}, f32[2,8192,128]{2,1,0:T(8,128)}, bf16[32,128,256]{2,1,0:T(8,128)(2,1)}) custom-call(s32[1]{0:T(128)} %bitcast.inner_ref, bf16[64,128,256]{2,1,0:T(8,128)(2,1)S(1)} %copy-done.2, bf16[64,128,256]{2,1,0:T(8,128)(2,1)} %collective-permute-done.1.refs_8_.refs_9_.refs_10_.refs_11_.other, ...), custom_call_target="tpu_custom_call" | custom-call | flops 65536 | bytes 4096 | tf_op jit(solution)/shard_map/local/pallas_call | solution.py:192
  53.7 1.2 copy-done.5
  54.9 2.1 %copy-done.6 = bf16[24,128,256]{2,1,0:T(8,128)(2,1)S(1)} copy-done((bf16[24,128,256]{2,1,0:T(8,128)(2,1)S(1)}, bf16[24,128,256]{2,1,0:T(8,128)(2,1)}, u32[]{:S(2)}) %copy-start.6) | copy-done | bytes 1572888
  57.0 0.8 energy.2.lines
  57.9 3.7 %collective-permute-done.4.refs_2_ = bf16[4,128,256]{2,1,0:T(8,128)(2,1)S(1)} collective-permute-done((bf16[4,128,256]{2,1,0:T(8,128)(2,1)}, bf16[4,128,256]{2,1,0:T(8,128)(2,1)S(1)}, u32[]{:S(2)}, u32[]{:S(2)}) %collective-permute-start.4) | collective-permute-done | bytes 262176 | tf_op jit(solution)/shard_map/ppermute | solution.py:439
  61.6 4.1 %fock_rows.3 = (bf16[24,128,256]{2,1,0:T(8,128)(2,1)S(1)}, bf16[8,128,256]{2,1,0:T(8,128)(2,1)S(1)}) custom-call(s32[96]{0:T(128)S(1)} %copy-done.9, s32[1]{0:T(128)S(6)} %sub.3.first_ref, f32[64,128]{1,0:T(8,128)S(1)} %energy.2.lines, f32[2,16,512,128]{3,2,1,0:T(8,128)} %bitcast.7, bf16[4,128,256]{2,1,0:T(8,128)(2,1)S(1)} %collective-permute-done.2.refs_0_, ...), custom_call_target="tpu_custom_call" | custom-call | flops 65536 | bytes 4096 | tf_op jit(solution)/shard_map/fock_rows/pallas_call | solution.py:255
  65.6 0.9 collective-permute-start.6
  66.5 0.1 collective-permute-start.7
  66.6 4.1 %fock_rows.2.own = bf16[32,128,256]{2,1,0:T(8,128)(2,1)S(1)} custom-call(s32[96]{0:T(128)S(1)} %copy-done.9, s32[1]{0:T(128)S(6)} %mul.4.first_ref, f32[64,128]{1,0:T(8,128)S(1)} %energy.2.lines, f32[2,16,512,128]{3,2,1,0:T(8,128)} %bitcast.8, bf16[4,128,256]{2,1,0:T(8,128)(2,1)S(1)} %collective-permute-done.2.refs_0_, ...), custom_call_target="tpu_custom_call" | custom-call | flops 65536 | bytes 4096 | tf_op jit(solution)/shard_map/fock_rows/pallas_call | solution.py:255
  70.7 23.3 %purify.1 = (bf16[32,256,256]{2,1,0:T(8,128)(2,1)}, bf16[32,256,256]{2,1,0:T(8,128)(2,1)}, bf16[8,128,256]{2,1,0:T(8,128)(2,1)S(1)}, f32[64,128]{1,0:T(8,128)S(1)}) custom-call(s32[1]{0:T(128)} %bitcast.inner_ref, bf16[32,128,256]{2,1,0:T(8,128)(2,1)S(1)} %fock_rows.2.own, bf16[24,128,256]{2,1,0:T(8,128)(2,1)S(1)} %collective-permute-done.6.low, ...), custom_call_target="tpu_custom_call" | custom-call | flops 65536 | bytes 4096 | tf_op jit(solution)/shard_map/purify/pallas_call | solution.py:311
  94.0 2.6 %picked.1.refs_2_ = bf16[8,128,256]{2,1,0:T(8,128)(2,1)} custom-call(s32[96]{0:T(128)} %get-tuple-element.19.meta_ref, bf16[64,128,256]{2,1,0:T(8,128)(2,1)} %copy-done, bf16[64,128,256]{2,1,0:T(8,128)(2,1)} %copy-done, bf16[64,128,256]{2,1,0:T(8,128)(2,1)} %copy-done, bf16[64,128,256]{2,1,0:T(8,128)(2,1)} %copy-done, bf16[64,128,256]{2,1,0:T(8,128)(2,1)} %copy-done, ...), custom_call_target="tpu_custom_call" | custom-call | flops 65536 | bytes 4096 | tf_op jit(solution)/shard_map/picked/pallas_call | solution.py:376
  96.6 4.4 %collective-permute-done.9.refs_0_ = bf16[32,128,256]{2,1,0:T(8,128)(2,1)S(1)} collective-permute-done((bf16[32,128,256]{2,1,0:T(8,128)(2,1)}, bf16[32,128,256]{2,1,0:T(8,128)(2,1)S(1)}, u32[]{:S(2)}, u32[]{:S(2)}) %collective-permute-start.9) | collective-permute-done | bytes 2097184 | tf_op jit(solution)/shard_map/ppermute | solution.py:443
  101.0 2.2 %copy-done.1 = bf16[64,128,256]{2,1,0:T(8,128)(2,1)S(1)} copy-done((bf16[64,128,256]{2,1,0:T(8,128)(2,1)S(1)}, bf16[64,128,256]{2,1,0:T(8,128)(2,1)}, u32[]{:S(2)}) %copy-start.1) | copy-done | bytes 4194328
  103.2 0.9 energy.3.refs_1_
  104.1 8.1 %collective-permute-done.8.refs_0_ = bf16[8,128,256]{2,1,0:T(8,128)(2,1)S(1)} collective-permute-done((bf16[8,128,256]{2,1,0:T(8,128)(2,1)S(1)}, bf16[8,128,256]{2,1,0:T(8,128)(2,1)S(1)}, u32[]{:S(2)}, u32[]{:S(2)}) %collective-permute-start.8) | collective-permute-done | bytes 524320 | tf_op jit(solution)/shard_map/ppermute | solution.py:443
  112.2 0.7 energies.1
  112.9 2.2 %collective-permute-start.10 = (f32[1,64]{1,0:T(1,128)S(1)}, f32[1,64]{1,0:T(1,128)S(1)}, u32[]{:S(2)}, u32[]{:S(2)}) collective-permute-start(f32[1,64]{1,0:T(1,128)S(1)} %energies.1), channel_id=1, source_target_pairs={{0,1},{1,0},{2,3},{3,2},{4,5},{5,4},{6,7},{7,6},{8,9},{9,8},{10,11... | collective-permute-start | bytes 776 | tf_op jit(solution)/shard_map/ppermute | solution.py:443
  115.1 0.8 collective-permute-done.10
  115.9 0.5 add_bitcast_fusion
  (25 shorter events, 0.1 us)
Async XLA Ops:
  0.6 7.9 %collective-permute-start.1 = (bf16[64,128,256]{2,1,0:T(8,128)(2,1)}, bf16[64,128,256]{2,1,0:T(8,128)(2,1)}, u32[]{:S(2)}, u32[]{:S(2)}) collective-permute-start(bf16[64,128,256]{2,1,0:T(8,128)(2,1)} %part.1), channel_id=1, source_target_pairs={{0,1},{1,0},{2,3},{3,2},{4,5},{5,4},{6,7},{7,6},{8,9},{9,8},{10,11... | collective-permute-start | bytes 12582920 | tf_op jit(solution)/shard_map/ppermute | solution.py:443
  3.9 49.7 %collective-permute-start = (bf16[24,128,256]{2,1,0:T(8,128)(2,1)}, bf16[24,128,256]{2,1,0:T(8,128)(2,1)S(1)}, u32[]{:S(2)}, u32[]{:S(2)}) collective-permute-start(bf16[24,128,256]{2,1,0:T(8,128)(2,1)} %taken.1), channel_id=1, source_target_pairs={{0,2},{2,0},{4,6},{6,4},{8,10},{10,8},{12,14},{14,12},{16,18},{18,... | collective-permute-start | bytes 4718600 | tf_op jit(solution)/shard_map/ppermute | solution.py:443
  8.5 23.7 %copy-start.2 = (bf16[64,128,256]{2,1,0:T(8,128)(2,1)S(1)}, bf16[64,128,256]{2,1,0:T(8,128)(2,1)}, u32[]{:S(2)}) copy-start(bf16[64,128,256]{2,1,0:T(8,128)(2,1)} %part.1) | copy-start | bytes 12582916
  8.5 23.7 %copy-start.8 = (bf16[64,192]{1,0:T(8,128)(2,1)S(1)}, bf16[64,192]{1,0:T(8,128)(2,1)}, u32[]{:S(2)}) copy-start(bf16[64,192]{1,0:T(8,128)(2,1)} %get-tuple-element.20.weights) | copy-start | bytes 73732
  13.8 44.0 %collective-permute-start.5 = (bf16[4,128,256]{2,1,0:T(8,128)(2,1)}, bf16[4,128,256]{2,1,0:T(8,128)(2,1)S(1)}, u32[]{:S(2)}, u32[]{:S(2)}) collective-permute-start(bf16[4,128,256]{2,1,0:T(8,128)(2,1)} %get-tuple-element.22.after), channel_id=1, source_target_pairs={{4,0},{6,2},{8,4},{10,6},{12,8},{14,10},{16,12},{18,14},{20,16},{2... | collective-permute-start | bytes 786440 | tf_op jit(solution)/shard_map/ppermute | solution.py:439
  20.8 37.0 %collective-permute-start.2 = (bf16[4,128,256]{2,1,0:T(8,128)(2,1)}, bf16[4,128,256]{2,1,0:T(8,128)(2,1)S(1)}, u32[]{:S(2)}, u32[]{:S(2)}) collective-permute-start(bf16[4,128,256]{2,1,0:T(8,128)(2,1)} %get-tuple-element.25), channel_id=1, source_target_pairs={{0,2},{2,4},{4,6},{6,8},{8,10},{10,12},{12,14},{14,16},{16,18},{18... | collective-permute-start | bytes 786440 | tf_op jit(solution)/shard_map/ppermute | solution.py:439
  23.1 34.8 %collective-permute-start.3 = (bf16[4,128,256]{2,1,0:T(8,128)(2,1)}, bf16[4,128,256]{2,1,0:T(8,128)(2,1)S(1)}, u32[]{:S(2)}, u32[]{:S(2)}) collective-permute-start(bf16[4,128,256]{2,1,0:T(8,128)(2,1)} %get-tuple-element.26), channel_id=1, source_target_pairs={{2,0},{4,2},{6,4},{8,6},{10,8},{12,10},{14,12},{16,14},{18,16},{20... | collective-permute-start | bytes 786440 | tf_op jit(solution)/shard_map/ppermute | solution.py:439
  30.3 31.2 %collective-permute-start.4 = (bf16[4,128,256]{2,1,0:T(8,128)(2,1)}, bf16[4,128,256]{2,1,0:T(8,128)(2,1)S(1)}, u32[]{:S(2)}, u32[]{:S(2)}) collective-permute-start(bf16[4,128,256]{2,1,0:T(8,128)(2,1)} %get-tuple-element.27), channel_id=1, source_target_pairs={{0,4},{2,6},{4,8},{6,10},{8,12},{10,14},{12,16},{14,18},{16,20},{1... | collective-permute-start | bytes 786440 | tf_op jit(solution)/shard_map/ppermute | solution.py:439
  32.3 2.2 %copy-start.3 = (bf16[64,128,256]{2,1,0:T(8,128)(2,1)S(1)}, bf16[64,128,256]{2,1,0:T(8,128)(2,1)}, u32[]{:S(2)}) copy-start(bf16[64,128,256]{2,1,0:T(8,128)(2,1)} %esp.1) | copy-start | bytes 12582916
  34.5 0.9 copy-start.7
  35.4 19.4 %copy-start.9 = (s32[96]{0:T(128)S(1)}, s32[96]{0:T(128)}, u32[]{:S(2)}) copy-start(s32[96]{0:T(128)} %get-tuple-element.19.meta_ref) | copy-start | bytes 1156
  53.6 4.2 %copy-start = (bf16[64,128,256]{2,1,0:T(8,128)(2,1)}, bf16[64,128,256]{2,1,0:T(8,128)(2,1)S(1)}, u32[]{:S(2)}) copy-start(bf16[64,128,256]{2,1,0:T(8,128)(2,1)S(1)} %get-tuple-element.23.refs_2_.refs_3_.refs_4_.refs_5_.refs_6_.refs_7_.refs_8_.refs_9_.refs_0_.refs_1_) | copy-start | bytes 12582916
  53.7 1.2 %copy-start.5 = (bf16[24,128,256]{2,1,0:T(8,128)(2,1)}, bf16[24,128,256]{2,1,0:T(8,128)(2,1)S(1)}, u32[]{:S(2)}) copy-start(bf16[24,128,256]{2,1,0:T(8,128)(2,1)S(1)} %collective-permute-done.refs_0_) | copy-start | bytes 4718596
  54.8 46.2 %collective-permute-start.9 = (bf16[32,128,256]{2,1,0:T(8,128)(2,1)}, bf16[32,128,256]{2,1,0:T(8,128)(2,1)S(1)}, u32[]{:S(2)}, u32[]{:S(2)}) collective-permute-start(bf16[32,128,256]{2,1,0:T(8,128)(2,1)} %get-tuple-element.33), channel_id=1, source_target_pairs={{0,2},{2,0},{4,6},{6,4},{8,10},{10,8},{12,14},{14,12},{16,18},{18,... | collective-permute-start | bytes 6291464 | tf_op jit(solution)/shard_map/ppermute | solution.py:443
  54.8 2.2 %copy-start.6 = (bf16[24,128,256]{2,1,0:T(8,128)(2,1)S(1)}, bf16[24,128,256]{2,1,0:T(8,128)(2,1)}, u32[]{:S(2)}) copy-start(bf16[24,128,256]{2,1,0:T(8,128)(2,1)} %copy-done.5) | copy-start | bytes 4718596
  65.6 5.1 %collective-permute-start.6 = (bf16[24,128,256]{2,1,0:T(8,128)(2,1)S(1)}, bf16[24,128,256]{2,1,0:T(8,128)(2,1)S(1)}, u32[]{:S(2)}, u32[]{:S(2)}) collective-permute-start(bf16[24,128,256]{2,1,0:T(8,128)(2,1)S(1)} %get-tuple-element.28), channel_id=1, source_target_pairs={{0,1},{1,0},{2,3},{3,2},{4,5},{5,4},{6,7},{7,6},{8,9},{9,8},{10,11... | collective-permute-start | bytes 4718600 | tf_op jit(solution)/shard_map/ppermute | solution.py:443
  66.5 4.2 %collective-permute-start.7 = (bf16[8,128,256]{2,1,0:T(8,128)(2,1)S(1)}, bf16[8,128,256]{2,1,0:T(8,128)(2,1)S(1)}, u32[]{:S(2)}, u32[]{:S(2)}) collective-permute-start(bf16[8,128,256]{2,1,0:T(8,128)(2,1)S(1)} %get-tuple-element.29), channel_id=1, source_target_pairs={{0,1},{1,0},{2,3},{3,2},{4,5},{5,4},{6,7},{7,6},{8,9},{9,8},{10,11... | collective-permute-start | bytes 1572872 | tf_op jit(solution)/shard_map/ppermute | solution.py:443
  94.0 7.0 %copy-start.10 = (s32[96]{0:T(128)S(1)}, s32[96]{0:T(128)}, u32[]{:S(2)}) copy-start(s32[96]{0:T(128)} %get-tuple-element.19.meta_ref) | copy-start | bytes 1156
  94.0 18.2 %collective-permute-start.8 = (bf16[8,128,256]{2,1,0:T(8,128)(2,1)S(1)}, bf16[8,128,256]{2,1,0:T(8,128)(2,1)S(1)}, u32[]{:S(2)}, u32[]{:S(2)}) collective-permute-start(bf16[8,128,256]{2,1,0:T(8,128)(2,1)S(1)} %get-tuple-element.32), channel_id=1, source_target_pairs={{0,2},{2,0},{4,6},{6,4},{8,10},{10,8},{12,14},{14,12},{16,18},{18,... | collective-permute-start | bytes 1572872 | tf_op jit(solution)/shard_map/ppermute | solution.py:443
  101.0 2.2 %copy-start.1 = (bf16[64,128,256]{2,1,0:T(8,128)(2,1)S(1)}, bf16[64,128,256]{2,1,0:T(8,128)(2,1)}, u32[]{:S(2)}) copy-start(bf16[64,128,256]{2,1,0:T(8,128)(2,1)} %copy-done) | copy-start | bytes 12582916
  103.2 9.0 %copy-start.4 = (bf16[8,128,256]{2,1,0:T(8,128)(2,1)S(1)}, bf16[8,128,256]{2,1,0:T(8,128)(2,1)}, u32[]{:S(2)}) copy-start(bf16[8,128,256]{2,1,0:T(8,128)(2,1)} %picked.1.refs_2_) | copy-start | bytes 1572868
  112.9 3.0 %collective-permute-start.10 = (f32[1,64]{1,0:T(1,128)S(1)}, f32[1,64]{1,0:T(1,128)S(1)}, u32[]{:S(2)}, u32[]{:S(2)}) collective-permute-start(f32[1,64]{1,0:T(1,128)S(1)} %energies.1), channel_id=1, source_target_pairs={{0,1},{1,0},{2,3},{3,2},{4,5},{5,4},{6,7},{7,6},{8,9},{9,8},{10,11... | collective-permute-start | bytes 776 | tf_op jit(solution)/shard_map/ppermute | solution.py:443
